TPU v7x, 32 devices: a whole 2x2x4 slice. The times are simulated.
32 devices in a mesh: dp: 8 (over y, x, core), mp: 4 (over z).
Axes of the slice: x: 2, y: 2, z: 4, core: 2. Of those that a mesh axis runs over, the one named last changes fastest.
Arguments:
- tokens: bfloat16 [12608, 1024], P(('dp', 'mp')), may hold values from -6 to 6
- slide_tiles: int32 [16], P('dp'), may hold values from 1 to 4, as said below
- norm1_gain: float32 [1024], replicated, may hold values from 0.5 to 1.5
- norm1_bias: float32 [1024], replicated, may hold values from -1.75 to 1.75
- w_query: bfloat16 [1024, 1024], P(None, 'mp'), may hold values from -0.25 to 0.25
- b_query: float32 [1024], P('mp'), may hold values from -1.75 to 1.75
- w_key: bfloat16 [1024, 1024], P(None, 'mp'), may hold values from -0.1875 to 0.1875
- w_value: bfloat16 [1024, 1024], P(None, 'mp'), may hold values from -0.1875 to 0.1875
- b_value: float32 [1024], P('mp'), may hold values from -1.75 to 1.75
- w_out: bfloat16 [1024, 1024], P('mp'), may hold values from -1 to 1
- b_out: float32 [1024], replicated, may hold values from -1.75 to 1.75
- scale_attn: float32 [1024], replicated, may hold values from 0.3 to 1
- norm2_gain: float32 [1024], replicated, may hold values from 0.5 to 1.5
- norm2_bias: float32 [1024], replicated, may hold values from -1.75 to 1.75
- w_up: bfloat16 [1024, 4096], P(None, 'mp'), may hold values from -0.1875 to 0.1875
- b_up: float32 [4096], P('mp'), may hold values from -3 to 3
- w_down: bfloat16 [4096, 1024], P('mp'), may hold values from -0.09375 to 0.09375
- b_down: float32 [1024], replicated, may hold values from -1.75 to 1.75
- scale_mlp: float32 [1024], replicated, may hold values from 0.3 to 1
- cotangent: bfloat16 [12608, 1024], P(('dp', 'mp')), may hold values from -6 to 6
Outputs:
- layer_out: float32 [12608, 1024], P(('dp', 'mp'))
- grad_tokens: float32 [12608, 1024], P(('dp', 'mp'))
- grad_norm1_gain: float32 [1024], replicated
- grad_norm1_bias: float32 [1024], replicated
- grad_w_query: float32 [1024, 1024], P(None, 'mp')
- grad_b_query: float32 [1024], P('mp')
- grad_w_key: float32 [1024, 1024], P(None, 'mp')
- grad_w_value: float32 [1024, 1024], P(None, 'mp')
- grad_b_value: float32 [1024], P('mp')
- grad_w_out: float32 [1024, 1024], P('mp')
- grad_b_out: float32 [1024], replicated
- grad_scale_attn: float32 [1024], replicated
- grad_norm2_gain: float32 [1024], replicated
- grad_norm2_bias: float32 [1024], replicated
- grad_w_up: float32 [1024, 4096], P(None, 'mp')
- grad_b_up: float32 [4096], P('mp')
- grad_w_down: float32 [4096, 1024], P('mp')
- grad_b_down: float32 [1024], replicated
- grad_scale_mlp: float32 [1024], replicated
Inputs may be any that keep to these rules, and one draw needn't show every extreme that they name: `slide_tiles`: every draw has a slide with 4 crops.
All inputs are finite; a program needn't handle non-finite values.
Results may differ from a plain program's by a relative error of at most 0.023.
Values may be sent and summed in bfloat16 or wider, within the bound.
No kernel may reach another device: no remote copies, remote signals or barrier semaphores. Data moves between devices by JAX's collectives and lax.ppermute only.
A program may use at most 128 MiB of HBM per device.

v0:
```python
import math

import jax
import jax.numpy as jnp
from jax import lax
from jax.sharding import PartitionSpec as P

DH = 64
L = 197
SLIDES_DEV = 2
CROPS_DEV = 8


def layer_norm(values, gain, shift):
    average = jnp.mean(values, axis=-1, keepdims=True)
    centered = values - average
    spread = jnp.mean(centered * centered, axis=-1, keepdims=True)
    return centered * lax.rsqrt(spread + 1e-06) * gain + shift


def gelu_exact(values):
    return jax.nn.gelu(values, approximate=False)


def contract_rows(left, right):
    return lax.dot_general(
        left, right, (((0,), (0,)), ((), ())), preferred_element_type=jnp.float32
    )


def contract_cols(left, right):
    return lax.dot_general(
        left, right, (((1,), (1,)), ((), ())), preferred_element_type=jnp.float32
    )


def to_heads(matrix, heads_here):
    return matrix.reshape(matrix.shape[0] // L, L, heads_here, DH)


def attn_scores(query_heads, key_heads):
    product = jnp.einsum(
        "cqhd,ckhd->chqk", query_heads, key_heads, preferred_element_type=jnp.float32
    )
    return product * (1.0 / math.sqrt(DH))


def local(
    tokens,
    slide_tiles,
    norm1_gain,
    norm1_bias,
    w_query,
    b_query,
    w_key,
    w_value,
    b_value,
    w_out,
    b_out,
    scale_attn,
    norm2_gain,
    norm2_bias,
    w_up,
    b_up,
    w_down,
    b_down,
    scale_mlp,
    cotangent,
):
    row_count = tokens.shape[0]
    per_slide = CROPS_DEV // SLIDES_DEV
    crop_index = (lax.axis_index("mp") * row_count + jnp.arange(row_count, dtype=jnp.int32)) // L
    slide_index = crop_index // per_slide
    owner = slide_index[:, None] == jnp.arange(SLIDES_DEV, dtype=jnp.int32)[None, :]
    limit_rows = jnp.sum(jnp.where(owner, slide_tiles[None, :], 0), axis=1)
    valid_rows = (crop_index % per_slide < limit_rows).astype(jnp.float32)[:, None]
    inputs = tokens.astype(jnp.float32)
    normed_one = layer_norm(inputs, norm1_gain, norm1_bias).astype(jnp.bfloat16)
    rows_one = lax.all_gather(normed_one, "mp", axis=0, tiled=True)
    queries = (jnp.dot(rows_one, w_query, preferred_element_type=jnp.float32) + b_query).astype(
        jnp.bfloat16
    )
    keys_all = jnp.dot(rows_one, w_key, preferred_element_type=jnp.float32).astype(jnp.bfloat16)
    values_all = (jnp.dot(rows_one, w_value, preferred_element_type=jnp.float32) + b_value).astype(
        jnp.bfloat16
    )
    heads_here = w_query.shape[1] // DH
    query_heads = to_heads(queries, heads_here)
    key_heads = to_heads(keys_all, heads_here)
    value_heads = to_heads(values_all, heads_here)
    scores = attn_scores(query_heads, key_heads)
    top_score = jnp.max(scores, axis=-1, keepdims=True)
    log_total = top_score + jnp.log(jnp.sum(jnp.exp(scores - top_score), axis=-1, keepdims=True))
    weights_low = jnp.exp(scores - log_total).astype(jnp.bfloat16)
    mixed_heads = jnp.einsum(
        "chqk,ckhd->cqhd", weights_low, value_heads, preferred_element_type=jnp.float32
    )
    attended = mixed_heads.reshape(queries.shape).astype(jnp.bfloat16)
    attn_sum = lax.psum_scatter(
        jnp.dot(attended, w_out, preferred_element_type=jnp.float32).astype(jnp.bfloat16),
        "mp",
        scatter_dimension=0,
        tiled=True,
    ).astype(jnp.float32)
    branch_one = attn_sum + b_out
    hidden_state = inputs + scale_attn * branch_one
    normed_two = layer_norm(hidden_state, norm2_gain, norm2_bias).astype(jnp.bfloat16)
    rows_two = lax.all_gather(normed_two, "mp", axis=0, tiled=True)
    up_pre = jnp.dot(rows_two, w_up, preferred_element_type=jnp.float32) + b_up
    activated = gelu_exact(up_pre).astype(jnp.bfloat16)
    down_sum = lax.psum_scatter(
        jnp.dot(activated, w_down, preferred_element_type=jnp.float32).astype(jnp.bfloat16),
        "mp",
        scatter_dimension=0,
        tiled=True,
    ).astype(jnp.float32)
    branch_two = down_sum + b_down
    layer_out = valid_rows * (hidden_state + scale_mlp * branch_two)
    grad_out = valid_rows * cotangent.astype(jnp.float32)
    grad_scale_mlp = jnp.sum(grad_out * branch_two, axis=0)
    grad_branch_two = scale_mlp * grad_out
    grad_b_down = jnp.sum(grad_branch_two, axis=0)
    grad_down_low = grad_branch_two.astype(jnp.bfloat16)
    gelu_value, gelu_back = jax.vjp(gelu_exact, up_pre)
    grad_down_rows = lax.all_gather(grad_down_low, "mp", axis=0, tiled=True)
    grad_act = contract_cols(grad_down_rows, w_down)
    grad_up = gelu_back(grad_act)[0].astype(jnp.bfloat16)
    grad_w_up = contract_rows(rows_two, grad_up)
    grad_w_down = contract_rows(activated, grad_down_rows)
    grad_b_up = jnp.sum(grad_up.astype(jnp.float32), axis=0)
    grad_rows_two = lax.psum_scatter(
        contract_cols(grad_up, w_up).astype(jnp.bfloat16), "mp", scatter_dimension=0, tiled=True
    ).astype(jnp.float32)
    norm2_value, norm2_back = jax.vjp(layer_norm, hidden_state, norm2_gain, norm2_bias)
    grad_hidden_norm, grad_norm2_gain, grad_norm2_bias = norm2_back(grad_rows_two)
    grad_hidden = grad_out + grad_hidden_norm
    grad_scale_attn = jnp.sum(grad_hidden * branch_one, axis=0)
    grad_branch_one = scale_attn * grad_hidden
    grad_b_out = jnp.sum(grad_branch_one, axis=0)
    grad_attn_low = grad_branch_one.astype(jnp.bfloat16)
    grad_attn_rows = lax.all_gather(grad_attn_low, "mp", axis=0, tiled=True)
    grad_w_out = contract_rows(attended, grad_attn_rows)
    grad_mixed = contract_cols(grad_attn_rows, w_out).astype(jnp.bfloat16)
    grad_mixed_heads = to_heads(grad_mixed, heads_here)
    scores_again = attn_scores(query_heads, key_heads)
    probs = jnp.exp(scores_again - log_total)
    probs_low = probs.astype(jnp.bfloat16)
    grad_value_heads = jnp.einsum(
        "chqk,cqhd->ckhd", probs_low, grad_mixed_heads, preferred_element_type=jnp.float32
    )
    grad_values = grad_value_heads.reshape(queries.shape).astype(jnp.bfloat16)
    grad_probs = jnp.einsum(
        "cqhd,ckhd->chqk", grad_mixed_heads, value_heads, preferred_element_type=jnp.float32
    )
    row_inner = jnp.sum(probs * grad_probs, axis=-1, keepdims=True)
    grad_scores = (probs * (grad_probs - row_inner)).astype(jnp.bfloat16)
    inverse_root = 1.0 / math.sqrt(DH)
    grad_query_heads = jnp.einsum(
        "chqk,ckhd->cqhd", grad_scores, key_heads, preferred_element_type=jnp.float32
    )
    grad_queries = (inverse_root * grad_query_heads).reshape(queries.shape).astype(jnp.bfloat16)
    grad_key_heads = jnp.einsum(
        "chqk,cqhd->ckhd", grad_scores, query_heads, preferred_element_type=jnp.float32
    )
    grad_keys = (inverse_root * grad_key_heads).reshape(queries.shape).astype(jnp.bfloat16)
    grad_w_query = contract_rows(rows_one, grad_queries)
    grad_b_query = jnp.sum(grad_queries.astype(jnp.float32), axis=0)
    grad_w_key = contract_rows(rows_one, grad_keys)
    grad_w_value = contract_rows(rows_one, grad_values)
    grad_b_value = jnp.sum(grad_values.astype(jnp.float32), axis=0)
    grad_rows_one = lax.psum_scatter(
        (
            contract_cols(grad_queries, w_query)
            + contract_cols(grad_keys, w_key)
            + contract_cols(grad_values, w_value)
        ).astype(jnp.bfloat16),
        "mp",
        scatter_dimension=0,
        tiled=True,
    ).astype(jnp.float32)
    norm1_value, norm1_back = jax.vjp(layer_norm, inputs, norm1_gain, norm1_bias)
    grad_in_norm, grad_norm1_gain, grad_norm1_bias = norm1_back(grad_rows_one)
    grad_tokens = grad_hidden + grad_in_norm
    small_stack = jnp.stack(
        [
            grad_norm1_gain,
            grad_norm1_bias,
            grad_norm2_gain,
            grad_norm2_bias,
            grad_scale_attn,
            grad_scale_mlp,
            grad_b_out,
            grad_b_down,
        ],
        axis=1,
    )
    small_total = lax.psum(small_stack.astype(jnp.bfloat16), "mp")
    (
        share_wq,
        share_bq,
        share_wk,
        share_wv,
        share_bv,
        share_wo,
        share_up,
        share_bup,
        share_down,
        share_small,
    ) = (
        lax.psum_scatter(
            grad_w_query.astype(jnp.bfloat16), "dp", scatter_dimension=0, tiled=True
        ).astype(jnp.float32),
        lax.psum_scatter(
            grad_b_query.astype(jnp.bfloat16), "dp", scatter_dimension=0, tiled=True
        ).astype(jnp.float32),
        lax.psum_scatter(
            grad_w_key.astype(jnp.bfloat16), "dp", scatter_dimension=0, tiled=True
        ).astype(jnp.float32),
        lax.psum_scatter(
            grad_w_value.astype(jnp.bfloat16), "dp", scatter_dimension=0, tiled=True
        ).astype(jnp.float32),
        lax.psum_scatter(
            grad_b_value.astype(jnp.bfloat16), "dp", scatter_dimension=0, tiled=True
        ).astype(jnp.float32),
        lax.psum_scatter(
            grad_w_out.astype(jnp.bfloat16), "dp", scatter_dimension=0, tiled=True
        ).astype(jnp.float32),
        lax.psum_scatter(
            grad_w_up.astype(jnp.bfloat16), "dp", scatter_dimension=0, tiled=True
        ).astype(jnp.float32),
        lax.psum_scatter(
            grad_b_up.astype(jnp.bfloat16), "dp", scatter_dimension=0, tiled=True
        ).astype(jnp.float32),
        lax.psum_scatter(
            grad_w_down.astype(jnp.bfloat16), "dp", scatter_dimension=0, tiled=True
        ).astype(jnp.float32),
        lax.psum_scatter(small_total, "dp", scatter_dimension=0, tiled=True).astype(jnp.float32),
    )
    (
        full_wq,
        full_bq,
        full_wk,
        full_wv,
        full_bv,
        full_wo,
        full_up,
        full_bup,
        full_down,
        full_small,
    ) = (
        lax.all_gather(share_wq.astype(jnp.bfloat16), "dp", axis=0, tiled=True).astype(
            share_wq.dtype
        ),
        lax.all_gather(share_bq.astype(jnp.bfloat16), "dp", axis=0, tiled=True).astype(
            share_bq.dtype
        ),
        lax.all_gather(share_wk.astype(jnp.bfloat16), "dp", axis=0, tiled=True).astype(
            share_wk.dtype
        ),
        lax.all_gather(share_wv.astype(jnp.bfloat16), "dp", axis=0, tiled=True).astype(
            share_wv.dtype
        ),
        lax.all_gather(share_bv.astype(jnp.bfloat16), "dp", axis=0, tiled=True).astype(
            share_bv.dtype
        ),
        lax.all_gather(share_wo.astype(jnp.bfloat16), "dp", axis=0, tiled=True).astype(
            share_wo.dtype
        ),
        lax.all_gather(share_up.astype(jnp.bfloat16), "dp", axis=0, tiled=True).astype(
            share_up.dtype
        ),
        lax.all_gather(share_bup.astype(jnp.bfloat16), "dp", axis=0, tiled=True).astype(
            share_bup.dtype
        ),
        lax.all_gather(share_down.astype(jnp.bfloat16), "dp", axis=0, tiled=True).astype(
            share_down.dtype
        ),
        lax.all_gather(share_small.astype(jnp.bfloat16), "dp", axis=0, tiled=True).astype(
            share_small.dtype
        ),
    )
    return (
        layer_out,
        grad_tokens,
        full_small[:, 0],
        full_small[:, 1],
        full_wq,
        full_bq,
        full_wk,
        full_wv,
        full_bv,
        full_wo,
        full_small[:, 6],
        full_small[:, 4],
        full_small[:, 2],
        full_small[:, 3],
        full_up,
        full_bup,
        full_down,
        full_small[:, 7],
        full_small[:, 5],
    )


def solution(mesh):
    in_specs = (
        P(("dp", "mp"), None),
        P("dp"),
        P(),
        P(),
        P(None, "mp"),
        P("mp"),
        P(None, "mp"),
        P(None, "mp"),
        P("mp"),
        P("mp", None),
        P(),
        P(),
        P(),
        P(),
        P(None, "mp"),
        P("mp"),
        P("mp", None),
        P(),
        P(),
        P(("dp", "mp"), None),
    )
    out_specs = (
        P(("dp", "mp"), None),
        P(("dp", "mp"), None),
        P(),
        P(),
        P(None, "mp"),
        P("mp"),
        P(None, "mp"),
        P(None, "mp"),
        P("mp"),
        P("mp", None),
        P(),
        P(),
        P(),
        P(),
        P(None, "mp"),
        P("mp"),
        P("mp", None),
        P(),
        P(),
    )
    return jax.shard_map(local, mesh=mesh, in_specs=in_specs, out_specs=out_specs, check_vma=False)
```

profile of v0, /device:TPU:0, one launch (start us, length us, event | category | flops | bytes accessed | tf_op | source)
XLA Modules:
  0.0 931.7 jit_solution(16705572556709222904)
XLA Ops:
  15.4 67.1 %all-gather.16.cloned.1.call-done = bf16[4,394,1024]{2,1,0:T(8,128)(2,1)} async-done(((bf16[1,394,1024]{2,1,0:T(8,128)(2,1)}), bf16[4,394,1024]{2,1,0:T(8,128)(2,1)}) %all-gather.16.cloned.1.call-update) | async-done | bytes 3227664 | tf_op jit(solution)/shard_map/all_gather | solution.py:79
  82.4 4.5 reshape.201
  86.9 2.9 convolution_convert_fusion.4
  91.6 2.9 copy.95
  94.6 4.3 fusion.12
  98.9 3.6 reshape.225
  102.5 3.9 copy.94
  106.4 3.9 fusion.11
  110.3 3.6 reshape.224
  113.9 3.9 copy.96
  131.7 70.8 %fusion = bf16[400,1024]{1,0:T(8,128)(2,1)} fusion(bf16[1576,1024]{1,0:T(8,128)(2,1)} %convolution_convert_fusion.2), kind=kCustom, calls=%all-reduce-scatter | all-reduce-scatter fusion | flops 1638401 | bytes 4047360
  207.3 7.1 concatenate
  219.9 4.5 reshape.205
  224.3 61.9 %all-gather.18.cloned.1.call-done = bf16[4,394,1024]{2,1,0:T(8,128)(2,1)} async-done(((bf16[1,394,1024]{2,1,0:T(8,128)(2,1)}), bf16[4,394,1024]{2,1,0:T(8,128)(2,1)}) %all-gather.18.cloned.1.call-update) | async-done | bytes 3227664 | tf_op jit(solution)/shard_map/all_gather | solution.py:108
  286.2 4.5 reshape.203
  290.7 6.3 fusion.58
  297.1 19.8 %fusion.52 = (bf16[1024]{0:T(1024)(128)(2,1)S(1)}, bf16[1576,1024]{1,0:T(8,128)(2,1)S(1)}, f32[1576,1024]{1,0:T(8,128)}) fusion(f32[1576,1024]{1,0:T(8,128)S(1)} %fusion.58, f32[1024]{0:T(1024)S(1)} %copy-done.44, bf16[1576,1024]{1,0:T(8,128)(2,1)S(1)} %copy-done.23, bf16[1024,1024]{1,0:T(8,128)(2,1)S(1)} %copy-done), kind=kOutput, calls=%fused_computation.124 | convolution fusion | flops 3424533504 | bytes 21469184 | tf_op jit(solution)/shard_map/dot_general | solution.py:32
  318.5 5.1 convolution_convert_fusion
  323.6 61.5 %fusion.2 = bf16[400,1024]{1,0:T(8,128)(2,1)} fusion(bf16[1576,1024]{1,0:T(8,128)(2,1)} %convolution_convert_fusion), kind=kCustom, calls=%all-reduce-scatter.2 | all-reduce-scatter fusion | flops 1638401 | bytes 4047360
  389.6 6.9 concatenate.2
  399.1 2.7 fusion.24
  405.9 8.3 convolution_convert_fusion.6
  414.3 6.7 multiply_convert_fusion.1
  421.0 5.0 convolution_convert_fusion.1
  426.0 5.3 convolution_convert_fusion.5
  431.5 40.5 %all-gather.22.cloned.1.call-done = bf16[4,394,1024]{2,1,0:T(8,128)(2,1)} async-done(((bf16[1,394,1024]{2,1,0:T(8,128)(2,1)}), bf16[4,394,1024]{2,1,0:T(8,128)(2,1)}) %all-gather.22.cloned.1.call-update) | async-done | bytes 3227664 | tf_op jit(solution)/shard_map/all_gather | solution.py:141
  472.0 4.4 reshape.207
  476.4 3.9 convolution_convert_fusion.3
  480.2 4.0 reshape.227
  484.3 3.9 copy.100
  488.2 5.7 fusion.57
  493.9 7.8 multiply_reduce_fusion
  501.7 4.8 multiply_convert_fusion
  512.0 2.9 convert_element_type.221
  514.9 2.8 copy.104
  517.7 3.0 convert_element_type.215
  520.6 2.8 copy.107
  523.4 3.1 convert_element_type.218
  530.3 2.8 add_convert_fusion
  533.1 114.1 %fusion.51 = (bf16[400,1024]{1,0:T(8,128)(2,1)}, bf16[400,1024]{1,0:T(8,128)(2,1)}) fusion(bf16[1576,1024]{1,0:T(8,128)(2,1)} %convolution_convert_fusion.1, bf16[1576,1024]{1,0:T(8,128)(2,1)} %add_convert_fusion), kind=kCustom, calls=%all-reduce-scatter.4 | all-reduce-scatter fusion | flops 3276801 | bytes 8094208
  651.6 2.7 collective-permute-start.1
  654.3 6.0 concatenate.3
  664.7 6.0 concatenate.1
  670.6 5.0 fusion.29
  676.7 4.2 convolution_convert_fusion.9
  680.9 3.9 convolution_convert_fusion.10
  685.1 4.2 convolution_convert_fusion.12
  689.4 3.9 convolution_convert_fusion.11
  697.4 12.2 %all-reduce.14 = (bf16[256]{0:T(256)(128)(2,1)S(1)}, bf16[256]{0:T(256)(128)(2,1)S(1)}) all-reduce(bf16[256]{0:T(256)(128)(2,1)S(1)} %reduce_sum.279, bf16[256]{0:T(256)(128)(2,1)S(1)} %reduce_sum.281), channel_id=8, replica_groups=mesh['dp'=8,'mp'=4] {'dp'}, use_global_device_ids=true, to_apply=%region_28.29.clone | all-reduce | flops 512 | bytes 2048
  710.1 11.8 %all-reduce.13 = (bf16[256]{0:T(256)(128)(2,1)S(1)}, bf16[256]{0:T(256)(128)(2,1)S(1)}, bf16[1024]{0:T(1024)(128)(2,1)S(1)}) all-reduce(bf16[256]{0:T(256)(128)(2,1)S(1)} %dynamic-update-slice, bf16[256]{0:T(256)(128)(2,1)S(1)} %dynamic-update-slice.1, bf16[1024]{0:T(1024)(128)(2,1)S(1)} %get-tuple-element.36), channel_id=1, replica_groups=mesh['dp'=8,'mp'=4] {'dp'}, use_global_device_ids=true, to_apply=%add | all-reduce | flops 1536 | bytes 6144
  723.1 8.3 all-gather.4
  732.8 9.8 %psum.8 = bf16[128,8]{0,1:T(8,128)(2,1)S(1)} all-reduce(bf16[128,8]{0,1:T(8,128)(2,1)S(1)} %copy.116), channel_id=1, replica_groups=mesh['dp'=8,'mp'=4] {'mp'}, use_global_device_ids=true, to_apply=%region_24.25 | all-reduce | flops 1024 | bytes 4096 | tf_op jit(solution)/shard_map/psum | solution.py:197
  742.6 8.2 all_gather.46
  751.4 9.6 %all_gather.52 = bf16[256,1024]{1,0:T(8,128)(2,1)S(1)} all-gather(bf16[32,1024]{1,0:T(8,128)(2,1)} %reduce-scatter.24.cloned.1.call-done), channel_id=1, replica_groups=mesh['dp'=8,'mp'=4] {'dp'}, dimensions={0}, use_global_device_ids=true | all-gather | bytes 589824 | tf_op jit(solution)/shard_map/all_gather | solution.py:266
  762.1 23.2 %reduce-scatter.22.cloned.1.call-done = bf16[128,256]{1,0:T(8,128)(2,1)} async-done(((bf16[1024,256]{1,0:T(8,128)(2,1)}), bf16[128,256]{1,0:T(8,128)(2,1)}) %reduce-scatter.22.cloned.1.call-update) | async-done | bytes 65552 | tf_op jit(solution)/shard_map/reduce_scatter | solution.py:219
  785.3 9.8 %all_gather.50 = bf16[1024,256]{1,0:T(8,128)(2,1)S(1)} all-gather(bf16[128,256]{1,0:T(8,128)(2,1)} %reduce-scatter.22.cloned.1.call-done), channel_id=1, replica_groups=mesh['dp'=8,'mp'=4] {'dp'}, dimensions={0}, use_global_device_ids=true | all-gather | bytes 589824 | tf_op jit(solution)/shard_map/all_gather | solution.py:260
  796.1 27.2 %reduce-scatter.18.cloned.1.call-done = bf16[128,256]{1,0:T(8,128)(2,1)} async-done(((bf16[1024,256]{1,0:T(8,128)(2,1)}), bf16[128,256]{1,0:T(8,128)(2,1)}) %reduce-scatter.18.cloned.1.call-update) | async-done | bytes 65552 | tf_op jit(solution)/shard_map/reduce_scatter | solution.py:210
  823.3 9.8 %all_gather.47 = bf16[1024,256]{1,0:T(8,128)(2,1)S(1)} all-gather(bf16[128,256]{1,0:T(8,128)(2,1)} %reduce-scatter.18.cloned.1.call-done), channel_id=1, replica_groups=mesh['dp'=8,'mp'=4] {'dp'}, dimensions={0}, use_global_device_ids=true | all-gather | bytes 589824 | tf_op jit(solution)/shard_map/all_gather | solution.py:251
  834.1 27.0 %reduce-scatter.20.cloned.1.call-done = bf16[128,256]{1,0:T(8,128)(2,1)} async-done(((bf16[1024,256]{1,0:T(8,128)(2,1)}), bf16[128,256]{1,0:T(8,128)(2,1)}) %reduce-scatter.20.cloned.1.call-update) | async-done | bytes 65552 | tf_op jit(solution)/shard_map/reduce_scatter | solution.py:216
  861.1 9.8 %all_gather.49 = bf16[1024,256]{1,0:T(8,128)(2,1)S(1)} all-gather(bf16[128,256]{1,0:T(8,128)(2,1)} %reduce-scatter.20.cloned.1.call-done), channel_id=1, replica_groups=mesh['dp'=8,'mp'=4] {'dp'}, dimensions={0}, use_global_device_ids=true | all-gather | bytes 589824 | tf_op jit(solution)/shard_map/all_gather | solution.py:257
  871.9 19.0 %all-gather.12.cloned.1.call-done = bf16[1024,1024]{1,0:T(8,128)(2,1)} async-done(((bf16[128,1024]{1,0:T(8,128)(2,1)}), bf16[1024,1024]{1,0:T(8,128)(2,1)}) %all-gather.12.cloned.1.call-update) | async-done | bytes 2097168 | tf_op jit(solution)/shard_map/all_gather | solution.py:269
  890.9 4.1 convert_element_type.236
  895.0 25.9 %all-gather.14.cloned.1.call-done = bf16[1024,1024]{1,0:T(8,128)(2,1)} async-done(((bf16[128,1024]{1,0:T(8,128)(2,1)}), bf16[1024,1024]{1,0:T(8,128)(2,1)}) %all-gather.14.cloned.1.call-update) | async-done | bytes 2097168 | tf_op jit(solution)/shard_map/all_gather | solution.py:275
  920.9 4.1 convert_element_type.239
  (219 shorter events, 75.5 us)
Async XLA Ops:
  7.2 289.8 %copy-start = (bf16[1024,1024]{1,0:T(8,128)(2,1)S(1)}, bf16[1024,1024]{1,0:T(8,128)(2,1)}, u32[]{:S(2)}) copy-start(bf16[1024,1024]{1,0:T(8,128)(2,1)} %param.36) | copy-start | bytes 6291460
  7.2 6.8 copy-start.46
  7.2 6.9 copy-start.14
  7.2 6.9 copy-start.40
  7.2 75.2 %all-gather.16.cloned.1.call-start = ((), (), s32[]{:S(2)}) async-start(), calls=%async_computation.15 | async-start | bytes 4096000 | tf_op jit(solution)/shard_map/all_gather | solution.py:79
  8.8 2.1 copy-start.32
  13.9 205.9 %all-gather.20.cloned.1.call-start = ((), (), s32[]{:S(2)}) async-start(), calls=%async_computation.17 | async-start | bytes 4096000 | tf_op jit(solution)/shard_map/all_gather | solution.py:125
  15.3 71.6 %copy-start.26 = (bf16[1024,256]{1,0:T(8,128)(2,1)S(1)}, bf16[1024,256]{1,0:T(8,128)(2,1)}, u32[]{:S(2)}) copy-start(bf16[1024,256]{1,0:T(8,128)(2,1)} %param.26) | copy-start | bytes 1572868
  15.3 270.9 %all-gather.18.cloned.1.call-start = ((), (), s32[]{:S(2)}) async-start(), calls=%async_computation.16 | async-start | bytes 4096000 | tf_op jit(solution)/shard_map/all_gather | solution.py:108
  89.8 4.8 copy-start.49
  94.6 23.2 %copy-start.8 = (bf16[8,197,4,64]{1,3,2,0:T(8,128)(2,1)}, bf16[8,197,4,64]{1,3,2,0:T(8,128)(2,1)S(1)}, u32[]{:S(2)}) copy-start(bf16[8,197,4,64]{1,3,2,0:T(8,128)(2,1)S(1)} %copy.95) | copy-start | bytes 2420740
  98.9 7.5 copy-start.50
  120.2 2.7 copy-start.1
  120.2 2.7 copy-start.11
  124.3 4.7 copy-start.29
  131.7 74.1 %copy-start.47 = (u32[32]{0:T(128)S(1)}, u32[32]{0:T(128)}, u32[]{:S(2)}) copy-start(u32[32]{0:T(128)} %constant.146) | copy-start | bytes 388
  131.7 82.7 %copy-start.2 = (bf16[394,1024]{1,0:T(8,128)(2,1)S(1)}, bf16[394,1024]{1,0:T(8,128)(2,1)}, u32[]{:S(2)}) copy-start(bf16[394,1024]{1,0:T(8,128)(2,1)} %param.20) | copy-start | bytes 2420740
  131.7 82.7 %copy-start.30 = (f32[1024]{0:T(1024)S(1)}, f32[1024]{0:T(1024)}, u32[]{:S(2)}) copy-start(f32[1024]{0:T(1024)} %param.31) | copy-start | bytes 12292
  131.7 82.7 %copy-start.31 = (f32[1024]{0:T(1024)S(1)}, f32[1024]{0:T(1024)}, u32[]{:S(2)}) copy-start(f32[1024]{0:T(1024)} %param.30) | copy-start | bytes 12292
  202.5 15.6 %copy-start.35 = (f32[1024]{0:T(1024)S(1)}, f32[1024]{0:T(1024)}, u32[]{:S(2)}) copy-start(f32[1024]{0:T(1024)} %param.32) | copy-start | bytes 12292
  202.5 15.6 %copy-start.42 = (f32[1024]{0:T(1024)S(1)}, f32[1024]{0:T(1024)}, u32[]{:S(2)}) copy-start(f32[1024]{0:T(1024)} %param.33) | copy-start | bytes 12292
  203.9 3.3 collective-permute-start
  214.4 3.6 copy-start.3
  219.8 252.2 %all-gather.22.cloned.1.call-start = ((), (), s32[]{:S(2)}) async-start(), calls=%async_computation.18 | async-start | bytes 4096000 | tf_op jit(solution)/shard_map/all_gather | solution.py:141
  290.7 6.4 copy-start.23
  290.7 6.4 copy-start.44
  297.1 19.8 %copy-start.16 = (f32[1576,1024]{1,0:T(8,128)}, f32[1576,1024]{1,0:T(8,128)S(1)}, u32[]{:S(2)}) copy-start(f32[1576,1024]{1,0:T(8,128)S(1)} %fusion.58) | copy-start | bytes 19365892
  297.1 21.4 %copy-start.48 = (bf16[1024,1024]{1,0:T(8,128)(2,1)S(1)}, bf16[1024,1024]{1,0:T(8,128)(2,1)}, u32[]{:S(2)}) copy-start(bf16[1024,1024]{1,0:T(8,128)(2,1)} %param.34) | copy-start | bytes 6291460
  385.9 3.6 collective-permute-start.2
  396.5 5.3 copy-start.4
  396.5 5.4 copy-start.6
  396.5 5.4 copy-start.15
  405.9 287.5 %reduce-scatter.26.cloned.1.call-start = ((), (), s32[]{:S(2)}) async-start(), calls=%async_computation.11 | async-start | bytes 2359296 | tf_op jit(solution)/shard_map/reduce_scatter | solution.py:228
  414.3 279.7 %reduce-scatter.28.cloned.1.call-start = ((), (), s32[]{:S(2)}) async-start(), calls=%async_computation.13 | async-start | bytes 2359296 | tf_op jit(solution)/shard_map/reduce_scatter | solution.py:234
  421.0 5.0 copy-start.24
  431.4 300.6 %reduce-scatter.30.cloned.1.call-start = ((), (), s32[]{:S(2)}) async-start(), calls=%async_computation.19 | async-start | bytes 294912
  488.2 5.7 copy-start.12
  488.2 5.7 copy-start.13
  488.2 13.5 %slice-start = ((s8[6553600]{0:T(1024)(128)(4,1)}), s8[4194304]{0:T(1024)(128)(4,1)S(1)}, s32[]{:S(2)}) async-start(s8[6553600]{0:T(1024)(128)(4,1)} %bitcast.103), calls=%async_computation.20 | async-start | bytes 8388608
  493.9 7.8 slice-start.1
  501.7 4.8 copy-start.10
  506.5 2.1 copy-start.9
  508.7 1.7 copy-start.20
  517.7 8.8 copy-start.25
  526.5 2.4 copy-start.18
  526.5 2.4 copy-start.27
  533.1 127.2 %copy-start.33 = (f32[394]{0:T(512)S(1)}, f32[394]{0:T(512)}, u32[]{:S(2)}) copy-start(f32[394]{0:T(512)} %copy-done.32) | copy-start | bytes 4732
  533.1 127.2 %copy-start.34 = (f32[1024]{0:T(1024)S(1)}, f32[1024]{0:T(1024)}, u32[]{:S(2)}) copy-start(f32[1024]{0:T(1024)} %param.22) | copy-start | bytes 12292
  647.2 15.0 %copy-start.39 = (f32[394]{0:T(512)S(1)}, f32[394]{0:T(512)}, u32[]{:S(2)}) copy-start(f32[394]{0:T(512)} %copy-done.38) | copy-start | bytes 4732
  647.2 15.0 %copy-start.37 = (f32[394]{0:T(512)S(1)}, f32[394]{0:T(512)}, u32[]{:S(2)}) copy-start(f32[394]{0:T(512)} %copy-done.36) | copy-start | bytes 4732
  648.0 6.3 collective-permute-start.3
  651.6 13.0 %collective-permute-start.1 = (bf16[18,1024]{1,0:T(8,128)(2,1)S(1)}, bf16[18,1024]{1,0:T(8,128)(2,1)S(1)}, u32[]{:S(2)}, u32[]{:S(2)}) collective-permute-start(bf16[18,1024]{1,0:T(8,128)(2,1)S(1)} %slice.41), channel_id=1, source_target_pairs={{0,1},{1,2},{2,3},{4,5},{5,6},{6,7},{8,9},{9,10},{10,11},{12,13},{... | collective-permute-start | bytes 110600
  660.3 4.1 copy-start.5
  660.3 10.3 %copy-start.41 = (f32[1024]{0:T(1024)S(1)}, f32[1024]{0:T(1024)}, u32[]{:S(2)}) copy-start(f32[1024]{0:T(1024)} %param.38) | copy-start | bytes 12292
  660.3 10.3 %copy-start.43 = (f32[1024]{0:T(1024)S(1)}, f32[1024]{0:T(1024)}, u32[]{:S(2)}) copy-start(f32[1024]{0:T(1024)} %param.37) | copy-start | bytes 12292
  676.6 4.3 copy-start.22
  676.6 74.8 %reduce-scatter.24.cloned.1.call-start = ((), (), s32[]{:S(2)}) async-start(), calls=%async_computation.10 | async-start | bytes 589824 | tf_op jit(solution)/shard_map/reduce_scatter | solution.py:225
  680.9 104.4 %reduce-scatter.22.cloned.1.call-start = ((), (), s32[]{:S(2)}) async-start(), calls=%async_computation.9 | async-start | bytes 589824 | tf_op jit(solution)/shard_map/reduce_scatter | solution.py:219
  684.9 4.5 copy-start.19
  684.9 138.4 %reduce-scatter.18.cloned.1.call-start = ((), (), s32[]{:S(2)}) async-start(), calls=%async_computation.7 | async-start | bytes 589824 | tf_op jit(solution)/shard_map/reduce_scatter | solution.py:210
  689.3 5.3 copy-start.45
  689.3 171.7 %reduce-scatter.20.cloned.1.call-start = ((), (), s32[]{:S(2)}) async-start(), calls=%async_computation.8 | async-start | bytes 589824 | tf_op jit(solution)/shard_map/reduce_scatter | solution.py:216
  693.3 197.6 %all-gather.12.cloned.1.call-start = ((), (), s32[]{:S(2)}) async-start(), calls=%async_computation.12 | async-start | bytes 2359296 | tf_op jit(solution)/shard_map/all_gather | solution.py:269
  693.9 227.0 %all-gather.14.cloned.1.call-start = ((), (), s32[]{:S(2)}) async-start(), calls=%async_computation.14 | async-start | bytes 2359296 | tf_op jit(solution)/shard_map/all_gather | solution.py:275
  (7 other events, 7.5 us)
Sparse Core Ops, SparseCore 0:
  14.0 68.3 all-gather.15
  84.6 75.5 all-gather.19
  219.9 66.2 all-gather.17
  406.0 65.9 all-gather.21
  475.1 39.8 reduce-scatter.25
  518.5 41.2 reduce-scatter.27
  676.7 32.5 reduce-scatter.29
  713.3 34.1 reduce-scatter.23
  751.2 34.0 reduce-scatter.21
  789.1 34.1 reduce-scatter.17
  826.9 34.0 reduce-scatter.19
  863.0 27.8 all-gather.11
  892.9 27.8 all-gather.13
where the time goes:
time: 938 us; the launch traced here: 932 us
  blocking collectives  336 us (36%)
  waiting for transfers between devices  294 us (31%)
  matrix products  111 us (12%)
  local copies, waits for them, and re-layouts  106 us (11%)
  other arithmetic  57.8 us (6%)
  between operations  17.4 us (2%)
    unnamed x5, blocking collectives  270 us
    all_gather x1, waiting for transfers between devices, local(): rows_one = lax.all_gather(normed_one, 'mp', axis=0, tiled=True)  67.1 us
    all_gather x1, waiting for transfers between devices, local(): rows_two = lax.all_gather(normed_two, 'mp', axis=0, tiled=True)  61.9 us
    unnamed x131, local copies, waits for them, and re-layouts  57.9 us
    all_gather x1, waiting for transfers between devices, local(): grad_attn_rows = lax.all_gather(grad_attn_low, 'mp', axis=0, tiled=True)  40.5 us
    dot_general x6, matrix products, contract_cols(): lax.dot_general(left, right, (((1,), (1,)), ((), ())), preferred_element_...  35 us
    dot_general x6, matrix products, contract_rows(): lax.dot_general(left, right, (((0,), (0,)), ((), ())), preferred_element_...  29.8 us
    reshape x8, local copies, waits for them, and re-layouts, to_heads(): return matrix.reshape(matrix.shape[0] // L, L, heads_here, DH)  27.6 us
  transfers between devices with their start and end apart: 17, of which 10 were waited for; matrix products, arithmetic and copies ran while one was open for 42% of the time, Pallas kernels for 0%

commit v1 on v0

--- a/solution.py
+++ b/solution.py
@@ -3,6 +3,8 @@
 import jax
 import jax.numpy as jnp
 from jax import lax
+from jax.experimental import pallas as pl
+from jax.experimental.pallas import tpu as pltpu
 from jax.sharding import PartitionSpec as P
 
 DH = 64
@@ -45,7 +47,521 @@
     return product * (1.0 / math.sqrt(DH))
 
 
-def local(
+BLOCK = 128
+X_SIDE, Y_SIDE, CORE_SIDE = 2, 4, 1
+PLANE = 8
+DEPTH = 4
+
+
+def swap_plane(values, mask):
+    return lax.ppermute(values, "dp", [(i, i ^ mask) for i in range(PLANE)])
+
+
+def swap_depth(values, mask):
+    return lax.ppermute(values, "mp", [(i, i ^ mask) for i in range(DEPTH)])
+
+
+def place_offset(place):
+    return (place & 3) * 2 + (place >> 2)
+
+
+def offset_place(offset):
+    return (offset & 1) * 4 + (offset >> 1)
+
+
+def to_places(values, here):
+    return jnp.concatenate(
+        [
+            lax.dynamic_slice_in_dim(values, (here ^ place_offset(j)) * BLOCK, BLOCK, axis=-1)
+            for j in range(PLANE)
+        ],
+        axis=-1,
+    )
+
+
+def from_places(values, here):
+    return jnp.concatenate(
+        [
+            lax.dynamic_slice_in_dim(values, offset_place(here ^ j) * BLOCK, BLOCK, axis=-1)
+            for j in range(PLANE)
+        ],
+        axis=-1,
+    )
+
+
+def row_blocks(matrix):
+    return matrix.reshape(BLOCK, matrix.shape[1] // BLOCK, BLOCK).transpose(1, 0, 2)
+
+
+def plane_gather(far):
+    half = far.shape[0] // 2
+    from_x = swap_plane(far, X_SIDE)
+    from_y = swap_plane(far, Y_SIDE)
+    corner_low = swap_plane(from_y[:half], X_SIDE)
+    corner_high = swap_plane(from_x[half:], Y_SIDE)
+    corner = jnp.concatenate([corner_low, corner_high], axis=0)
+    mine = jnp.stack([far, from_x, from_y, corner])
+    return mine, swap_plane(mine, CORE_SIDE)
+
+
+def crop_ranges(rows):
+    ranges = []
+    for crop in range(rows // L):
+        low = crop * L // 16 * 16
+        high = min((crop + 1) * L + 15, rows + 15) // 16 * 16
+        ranges.append((low, min(high, rows), crop * L - low))
+    return ranges
+
+
+def assemble_attn(table, own, mine, other):
+    width = own.shape[1]
+    count = mine.shape[1]
+
+    def body(table_ref, own_ref, mine_ref, other_ref, out_ref):
+        out_ref[:, 0:width] = own_ref[...]
+
+        @pl.when(pl.program_id(0) < 4)
+        def _():
+            for b in range(count):
+                out_ref[:, width + b * BLOCK : width + (b + 1) * BLOCK] = mine_ref[0, b]
+
+        @pl.when(pl.program_id(0) >= 4)
+        def _():
+            for b in range(count):
+                out_ref[:, width + b * BLOCK : width + (b + 1) * BLOCK] = other_ref[0, b]
+
+    total = width + count * BLOCK
+    return pl.pallas_call(
+        body,
+        grid_spec=pltpu.PrefetchScalarGridSpec(
+            num_scalar_prefetch=1,
+            grid=(PLANE,),
+            in_specs=[
+                pl.BlockSpec((BLOCK, width), lambda j, t: (t[j], 0)),
+                pl.BlockSpec((1, count, BLOCK, BLOCK), lambda j, t: (jnp.minimum(j, 3), 0, 0, 0)),
+                pl.BlockSpec((1, count, BLOCK, BLOCK), lambda j, t: (jnp.maximum(j - 4, 0), 0, 0, 0)),
+            ],
+            out_specs=pl.BlockSpec((BLOCK, total), lambda j, t: (j, 0)),
+        ),
+        out_shape=jax.ShapeDtypeStruct((PLANE * BLOCK, total), jnp.bfloat16),
+        cost_estimate=pl.CostEstimate(flops=0, bytes_accessed=4 * PLANE * BLOCK * total, transcendentals=0),
+        name="assemble_attn",
+    )(table, own, mine, other)
+
+
+def assemble_rest(table, own_o, own_up, own_down, mine, other):
+    heads_w = own_o.shape[0]
+    unit_w = own_up.shape[1]
+    n_o = heads_w // BLOCK
+    n_u = unit_w // BLOCK
+    count = mine.shape[1]
+
+    def fill(src, o_ref, up_ref, down_ref):
+        def put_o(slot, first):
+            for b in range(n_o):
+                o_ref[slot * heads_w + b * BLOCK : slot * heads_w + (b + 1) * BLOCK, :] = src[0, first + b]
+
+        put_o(1, 0)
+        put_o(2, n_o)
+        for b in range(n_u):
+            up_ref[:, unit_w + b * BLOCK : unit_w + (b + 1) * BLOCK] = src[0, 2 * n_o + b]
+            down_ref[unit_w + b * BLOCK : unit_w + (b + 1) * BLOCK, :] = src[0, 2 * n_o + n_u + b]
+        put_o(3, 2 * n_o + 2 * n_u)
+
+    def body(table_ref, own_o_ref, own_up_ref, own_down_ref, mine_ref, other_ref, o_ref, up_ref, down_ref):
+        o_ref[0:heads_w, :] = own_o_ref[...]
+        up_ref[:, 0:unit_w] = own_up_ref[...]
+        down_ref[0:unit_w, :] = own_down_ref[...]
+
+        @pl.when(pl.program_id(0) < 4)
+        def _():
+            fill(mine_ref, o_ref, up_ref, down_ref)
+
+        @pl.when(pl.program_id(0) >= 4)
+        def _():
+            fill(other_ref, o_ref, up_ref, down_ref)
+
+    width = PLANE * BLOCK
+    return pl.pallas_call(
+        body,
+        grid_spec=pltpu.PrefetchScalarGridSpec(
+            num_scalar_prefetch=1,
+            grid=(PLANE,),
+            in_specs=[
+                pl.BlockSpec((heads_w, BLOCK), lambda j, t: (0, t[j])),
+                pl.BlockSpec((BLOCK, unit_w), lambda j, t: (t[j], 0)),
+                pl.BlockSpec((unit_w, BLOCK), lambda j, t: (0, t[j])),
+                pl.BlockSpec((1, count, BLOCK, BLOCK), lambda j, t: (jnp.minimum(j, 3), 0, 0, 0)),
+                pl.BlockSpec((1, count, BLOCK, BLOCK), lambda j, t: (jnp.maximum(j - 4, 0), 0, 0, 0)),
+            ],
+            out_specs=[
+                pl.BlockSpec((4 * heads_w, BLOCK), lambda j, t: (0, j)),
+                pl.BlockSpec((BLOCK, 2 * unit_w), lambda j, t: (j, 0)),
+                pl.BlockSpec((2 * unit_w, BLOCK), lambda j, t: (0, j)),
+            ],
+        ),
+        out_shape=[
+            jax.ShapeDtypeStruct((4 * heads_w, width), jnp.bfloat16),
+            jax.ShapeDtypeStruct((width, 2 * unit_w), jnp.bfloat16),
+            jax.ShapeDtypeStruct((2 * unit_w, width), jnp.bfloat16),
+        ],
+        cost_estimate=pl.CostEstimate(flops=0, bytes_accessed=20 * 2**20, transcendentals=0),
+        name="assemble_rest",
+    )(table, own_o, own_up, own_down, mine, other)
+
+
+def dot_nt(left, right):
+    return lax.dot_general(left, right, (((1,), (1,)), ((), ())), preferred_element_type=jnp.float32)
+
+
+def dot_tn(left, right):
+    return lax.dot_general(left, right, (((0,), (0,)), ((), ())), preferred_element_type=jnp.float32)
+
+
+def dot_nn(left, right):
+    return lax.dot_general(left, right, (((1,), (0,)), ((), ())), preferred_element_type=jnp.float32)
+
+
+def attention_forward(qkv, group):
+    rows = qkv.shape[0]
+    heads_w = group // 3
+    ranges = crop_ranges(rows)
+    span = max(high - low for low, high, _ in ranges)
+    pairs = heads_w // BLOCK
+    groups = qkv.shape[1] // group
+    scale = 1.0 / math.sqrt(DH)
+
+    def body(qkv_ref, out_ref, prob_ref):
+        for pair in range(pairs):
+            col = pair * BLOCK
+            for index, (low, high, skip) in enumerate(ranges):
+                size = high - low
+                query = qkv_ref[low:high, col : col + BLOCK]
+                key = qkv_ref[low:high, heads_w + col : heads_w + col + BLOCK]
+                value = qkv_ref[low:high, 2 * heads_w + col : 2 * heads_w + col + BLOCK]
+                lane = lax.broadcasted_iota(jnp.int32, (size, BLOCK), 1)
+                row = lax.broadcasted_iota(jnp.int32, (size, size), 0)
+                column = lax.broadcasted_iota(jnp.int32, (size, size), 1)
+                seen = (column >= skip) & (column < skip + L)
+                inside = seen & (row >= skip) & (row < skip + L)
+                parts = []
+                for head in range(2):
+                    mine = (lane < DH) if head == 0 else (lane >= DH)
+                    scores = dot_nt(jnp.where(mine, query, jnp.zeros_like(query)), key) * scale
+                    scores = jnp.where(seen, scores, -1e30)
+                    top = jnp.max(scores, axis=1, keepdims=True)
+                    raised = jnp.exp(scores - top)
+                    total = jnp.sum(raised, axis=1, keepdims=True)
+                    probs = jnp.where(inside, raised * (1.0 / total), 0.0).astype(jnp.bfloat16)
+                    prob_ref[0, pair, index, head, 0:size, 0:size] = probs
+                    parts.append(dot_nn(probs, value))
+                mixed = jnp.where(lane < DH, parts[0], parts[1]).astype(jnp.bfloat16)
+                if skip:
+                    mixed = jnp.where(
+                        lax.broadcasted_iota(jnp.int32, (size, BLOCK), 0) >= skip,
+                        mixed,
+                        out_ref[low:high, col : col + BLOCK],
+                    )
+                out_ref[low:high, col : col + BLOCK] = mixed
+
+    prob_shape = (groups, pairs, len(ranges), 2, span, span)
+    return pl.pallas_call(
+        body,
+        grid=(groups,),
+        in_specs=[pl.BlockSpec((rows, group), lambda g: (0, g))],
+        out_specs=[
+            pl.BlockSpec((rows, heads_w), lambda g: (0, g)),
+            pl.BlockSpec((1,) + prob_shape[1:], lambda g: (g, 0, 0, 0, 0, 0)),
+        ],
+        out_shape=[
+            jax.ShapeDtypeStruct((rows, groups * heads_w), jnp.bfloat16),
+            jax.ShapeDtypeStruct(prob_shape, jnp.bfloat16),
+        ],
+        compiler_params=pltpu.CompilerParams(vmem_limit_bytes=48 * 2**20),
+        cost_estimate=pl.CostEstimate(flops=10**9, bytes_accessed=8 * 2**20, transcendentals=2 * 10**6),
+        name="attention_forward",
+    )(qkv)
+
+
+def attention_backward(qkv, probs, grad_mixed, group):
+    rows = qkv.shape[0]
+    heads_w = group // 3
+    ranges = crop_ranges(rows)
+    pairs = heads_w // BLOCK
+    groups = qkv.shape[1] // group
+    scale = 1.0 / math.sqrt(DH)
+
+    def body(qkv_ref, prob_ref, grad_ref, out_ref):
+        for pair in range(pairs):
+            col = pair * BLOCK
+            for index, (low, high, skip) in enumerate(ranges):
+                size = high - low
+                query = qkv_ref[low:high, col : col + BLOCK]
+                key = qkv_ref[low:high, heads_w + col : heads_w + col + BLOCK]
+                value = qkv_ref[low:high, 2 * heads_w + col : 2 * heads_w + col + BLOCK]
+                grad = grad_ref[low:high, col : col + BLOCK]
+                lane = lax.broadcasted_iota(jnp.int32, (size, BLOCK), 1)
+                row = lax.broadcasted_iota(jnp.int32, (size, BLOCK), 0)
+                parts = []
+                for head in range(2):
+                    mine = (lane < DH) if head == 0 else (lane >= DH)
+                    low_probs = prob_ref[0, pair, index, head, 0:size, 0:size]
+                    grad_value = dot_tn(low_probs, grad)
+                    grad_probs = dot_nt(jnp.where(mine, grad, jnp.zeros_like(grad)), value)
+                    wide = low_probs.astype(jnp.float32)
+                    weighted = wide * grad_probs
+                    inner = jnp.sum(weighted, axis=1, keepdims=True)
+                    grad_scores = (weighted - wide * inner).astype(jnp.bfloat16)
+                    grad_query = dot_nn(grad_scores, key) * scale
+                    grad_key = dot_tn(grad_scores, query) * scale
+                    parts.append((grad_query, grad_key, grad_value))
+                for which in range(3):
+                    first = which * heads_w + col
+                    joined = jnp.where(lane < DH, parts[0][which], parts[1][which]).astype(jnp.bfloat16)
+                    if skip:
+                        joined = jnp.where(row >= skip, joined, out_ref[low:high, first : first + BLOCK])
+                    out_ref[low:high, first : first + BLOCK] = joined
+
+    return pl.pallas_call(
+        body,
+        grid=(groups,),
+        in_specs=[
+            pl.BlockSpec((rows, group), lambda g: (0, g)),
+            pl.BlockSpec((1,) + probs.shape[1:], lambda g: (g, 0, 0, 0, 0, 0)),
+            pl.BlockSpec((rows, heads_w), lambda g: (0, g)),
+        ],
+        out_specs=pl.BlockSpec((rows, group), lambda g: (0, g)),
+        out_shape=jax.ShapeDtypeStruct(qkv.shape, jnp.bfloat16),
+        compiler_params=pltpu.CompilerParams(vmem_limit_bytes=48 * 2**20),
+        cost_estimate=pl.CostEstimate(flops=2 * 10**9, bytes_accessed=12 * 2**20, transcendentals=0),
+        name="attention_backward",
+    )(qkv, probs, grad_mixed)
+
+
+def reduce_plane(near, across, axis):
+    arrived = swap_plane(across, CORE_SIDE)
+    long = 1 - axis
+    half = near.shape[long] // 2
+
+    def part(side, chip):
+        def cut(values):
+            values = lax.slice_in_dim(values, side * half, (side + 1) * half, axis=long)
+            return lax.slice_in_dim(values, chip * BLOCK, (chip + 1) * BLOCK, axis=axis)
+
+        return cut(near).astype(jnp.float32) + cut(arrived).astype(jnp.float32)
+
+    def piece(values, index):
+        return lax.slice_in_dim(values, index * BLOCK, (index + 1) * BLOCK, axis=axis).astype(jnp.float32)
+
+    halves = []
+    for side, (first, second, one, two) in enumerate(((X_SIDE, Y_SIDE, 1, 2), (Y_SIDE, X_SIDE, 2, 1))):
+        sent = jnp.concatenate([part(side, one), part(side, 3)], axis=axis).astype(jnp.bfloat16)
+        halves.append((swap_plane(sent, first), second, two))
+    done = []
+    for side, (received, second, two) in enumerate(halves):
+        onward = (part(side, two) + piece(received, 1)).astype(jnp.bfloat16)
+        done.append((part(side, 0) + piece(received, 0), swap_plane(onward, second)))
+    return [kept + last.astype(jnp.float32) for kept, last in done]
+
+
+def local_paired(
+    tokens,
+    slide_tiles,
+    norm1_gain,
+    norm1_bias,
+    w_query,
+    b_query,
+    w_key,
+    w_value,
+    b_value,
+    w_out,
+    b_out,
+    scale_attn,
+    norm2_gain,
+    norm2_bias,
+    w_up,
+    b_up,
+    w_down,
+    b_down,
+    scale_mlp,
+    cotangent,
+):
+    row_count = tokens.shape[0]
+    heads_w = w_query.shape[1]
+    unit_w = w_up.shape[1]
+    here = lax.axis_index("dp")
+    level = lax.axis_index("mp")
+    table = jnp.stack([here ^ place_offset(j) for j in range(PLANE)]).astype(jnp.int32)
+
+    own_attn = jnp.concatenate([w_query, w_key, w_value], axis=1)
+    slice_attn = row_blocks(lax.dynamic_slice_in_dim(own_attn, here * BLOCK, BLOCK, axis=0))
+    slice_out = lax.dynamic_slice_in_dim(w_out, here * BLOCK, BLOCK, axis=1).reshape(-1, BLOCK, BLOCK)
+    slice_up = row_blocks(lax.dynamic_slice_in_dim(w_up, here * BLOCK, BLOCK, axis=0))
+    slice_down = lax.dynamic_slice_in_dim(w_down, here * BLOCK, BLOCK, axis=1).reshape(-1, BLOCK, BLOCK)
+    far_attn = jnp.concatenate([swap_depth(slice_attn, mask) for mask in (1, 2, 3)], axis=0)
+    far_rest = jnp.concatenate(
+        [
+            swap_depth(slice_out, 1),
+            swap_depth(jnp.concatenate([slice_out, slice_up, slice_down], axis=0), 2),
+            swap_depth(slice_out, 3),
+        ],
+        axis=0,
+    )
+    biases = lax.all_gather(jnp.concatenate([b_query, b_value, b_up]), "mp", axis=0)
+    near_first = [lax.dynamic_index_in_dim(biases, level ^ mask, 0, keepdims=False) for mask in range(DEPTH)]
+    bias_attn = jnp.concatenate(
+        [
+            jnp.concatenate([row[0:heads_w], jnp.zeros((heads_w,), jnp.float32), row[heads_w : 2 * heads_w]])
+            for row in near_first
+        ]
+    )
+    bias_up = jnp.concatenate([near_first[0][2 * heads_w :], near_first[2][2 * heads_w :]])
+    full_qkv = assemble_attn(table, own_attn, *plane_gather(far_attn))
+    full_out, full_up, full_down = assemble_rest(table, w_out, w_up, w_down, *plane_gather(far_rest))
+
+    per_slide = CROPS_DEV // SLIDES_DEV
+    crop_index = (level * row_count + jnp.arange(row_count, dtype=jnp.int32)) // L
+    slide_index = crop_index // per_slide
+    owner = slide_index[:, None] == jnp.arange(SLIDES_DEV, dtype=jnp.int32)[None, :]
+    limit_rows = jnp.sum(jnp.where(owner, slide_tiles[None, :], 0), axis=1)
+    valid_rows = (crop_index % per_slide < limit_rows).astype(jnp.float32)[:, None]
+    vectors = to_places(
+        jnp.stack(
+            [norm1_gain, norm1_bias, norm2_gain, norm2_bias, scale_attn, scale_mlp, b_out, b_down]
+        ),
+        here,
+    )
+    gain_one, shift_one, gain_two, shift_two, scale_one, scale_two, bias_out, bias_down = vectors
+    inputs = to_places(tokens, here).astype(jnp.float32)
+    grad_out = valid_rows * to_places(cotangent, here).astype(jnp.float32)
+    grad_branch_two = scale_two * grad_out
+    grad_b_down = jnp.sum(grad_branch_two, axis=0)
+    grad_down_low = grad_branch_two.astype(jnp.bfloat16)
+    down_rows = jnp.concatenate([grad_down_low, swap_depth(grad_down_low, 1)], axis=0)
+
+    normed_one = layer_norm(inputs, gain_one, shift_one).astype(jnp.bfloat16)
+    qkv = (dot_nn(normed_one, full_qkv) + bias_attn).astype(jnp.bfloat16)
+    attended, probs = attention_forward(qkv, 3 * heads_w)
+    branch_one = dot_nn(attended, full_out) + bias_out
+    hidden_state = inputs + scale_one * branch_one
+    normed_two = layer_norm(hidden_state, gain_two, shift_two).astype(jnp.bfloat16)
+
+    rows_two = jnp.concatenate([normed_two, swap_depth(normed_two, 1)], axis=0)
+    up_pre = dot_nn(rows_two, full_up) + bias_up
+    spread = 0.5 * (1.0 + lax.erf(up_pre * (1.0 / math.sqrt(2.0))))
+    activated = (up_pre * spread).astype(jnp.bfloat16)
+    slope = spread + up_pre * jnp.exp(-0.5 * up_pre * up_pre) * (1.0 / math.sqrt(2.0 * math.pi))
+    grad_up = (dot_nt(down_rows, full_down) * slope).astype(jnp.bfloat16)
+    norm_rows = dot_nt(grad_up, full_up).astype(jnp.bfloat16)
+    grad_rows_two = norm_rows[:row_count].astype(jnp.float32) + swap_depth(norm_rows[row_count:], 1).astype(
+        jnp.float32
+    )
+    down_part = dot_nn(activated, full_down).astype(jnp.bfloat16)
+    down_sum = down_part[:row_count].astype(jnp.float32) + swap_depth(down_part[row_count:], 1).astype(jnp.float32)
+    branch_two = down_sum + bias_down
+    layer_out = valid_rows * (hidden_state + scale_two * branch_two)
+    grad_scale_mlp = jnp.sum(grad_out * branch_two, axis=0)
+
+    side = PLANE * BLOCK // 2
+    down_near = dot_tn(activated, down_rows[:, :side]).astype(jnp.bfloat16)
+    down_across = dot_tn(activated, down_rows[:, side:]).astype(jnp.bfloat16)
+    down_own, down_other = reduce_plane(down_near, down_across, 1)
+    grad_down = down_own + swap_depth(down_other.astype(jnp.bfloat16), 2).astype(jnp.float32)
+    full_grad_down = lax.all_gather(grad_down.astype(jnp.bfloat16), "dp", axis=1, tiled=True).astype(jnp.float32)
+
+    up_across = dot_tn(rows_two[:, side:], grad_up).astype(jnp.bfloat16)
+    up_near = dot_tn(rows_two[:, :side], grad_up).astype(jnp.bfloat16)
+    up_own, up_other = reduce_plane(up_near, up_across, 0)
+    grad_w_up = up_own + swap_depth(up_other.astype(jnp.bfloat16), 2).astype(jnp.float32)
+    full_grad_up = lax.all_gather(grad_w_up.astype(jnp.bfloat16), "dp", axis=0, tiled=True).astype(jnp.float32)
+    grad_b_up = jnp.sum(grad_up.astype(jnp.float32), axis=0)
+
+    norm2_value, norm2_back = jax.vjp(layer_norm, hidden_state, gain_two, shift_two)
+    grad_hidden_norm, grad_norm2_gain, grad_norm2_bias = norm2_back(grad_rows_two)
+    grad_hidden = grad_out + grad_hidden_norm
+    grad_scale_attn = jnp.sum(grad_hidden * branch_one, axis=0)
+    grad_branch_one = scale_one * grad_hidden
+    grad_b_out = jnp.sum(grad_branch_one, axis=0)
+    grad_attn_low = grad_branch_one.astype(jnp.bfloat16)
+    grad_mixed = dot_nt(grad_attn_low, full_out).astype(jnp.bfloat16)
+
+    out_near = dot_tn(attended, grad_attn_low[:, :side]).astype(jnp.bfloat16)
+    out_across = dot_tn(attended, grad_attn_low[:, side:]).astype(jnp.bfloat16)
+    out_low, out_high = reduce_plane(out_near, out_across, 1)
+    grad_w_out = out_low[:heads_w]
+    for mask, values in ((1, out_low[heads_w:]), (2, out_high[:heads_w]), (3, out_high[heads_w:])):
+        grad_w_out = grad_w_out + swap_depth(values.astype(jnp.bfloat16), mask).astype(jnp.float32)
+    full_grad_out = lax.all_gather(grad_w_out.astype(jnp.bfloat16), "dp", axis=1, tiled=True).astype(jnp.float32)
+
+    grad_qkv = attention_backward(qkv, probs, grad_mixed, 3 * heads_w)
+    qkv_across = dot_tn(normed_one[:, side:], grad_qkv).astype(jnp.bfloat16)
+    qkv_near = dot_tn(normed_one[:, :side], grad_qkv).astype(jnp.bfloat16)
+    qkv_low, qkv_high = reduce_plane(qkv_near, qkv_across, 0)
+    group = 3 * heads_w
+    grad_attn = qkv_low[:, :group]
+    for mask, values in ((1, qkv_low[:, group:]), (2, qkv_high[:, :group]), (3, qkv_high[:, group:])):
+        grad_attn = grad_attn + swap_depth(values.astype(jnp.bfloat16), mask).astype(jnp.float32)
+    full_grad_attn = lax.all_gather(grad_attn.astype(jnp.bfloat16), "dp", axis=0, tiled=True).astype(jnp.float32)
+
+    grad_rows_one = dot_nt(grad_qkv, full_qkv)
+    norm1_value, norm1_back = jax.vjp(layer_norm, inputs, gain_one, shift_one)
+    grad_in_norm, grad_norm1_gain, grad_norm1_bias = norm1_back(grad_rows_one)
+    grad_tokens = grad_hidden + grad_in_norm
+
+    column_sums = jnp.sum(grad_qkv.astype(jnp.float32), axis=0).reshape(DEPTH, group)
+    column_sums = jnp.concatenate([column_sums[:, :heads_w], column_sums[:, 2 * heads_w :]], axis=1)
+    up_sums = jnp.stack(
+        [grad_b_up[:unit_w], jnp.zeros((unit_w,), jnp.float32), grad_b_up[unit_w:], jnp.zeros((unit_w,), jnp.float32)]
+    )
+    shared = jnp.concatenate([column_sums, up_sums], axis=1)
+    shared = jnp.concatenate(
+        [lax.dynamic_index_in_dim(shared, level ^ index, 0, keepdims=False) for index in range(DEPTH)]
+    )
+    small = from_places(
+        jnp.stack(
+            [
+                grad_norm1_gain,
+                grad_norm1_bias,
+                grad_norm2_gain,
+                grad_norm2_bias,
+                grad_scale_attn,
+                grad_scale_mlp,
+                grad_b_out,
+                grad_b_down,
+            ]
+        ),
+        here,
+    )
+    totals = lax.psum(jnp.concatenate([small.reshape(-1), shared]), ("dp", "mp"))
+    width = PLANE * BLOCK
+    small_total = totals[: 8 * width].reshape(8, width)
+    shared_total = lax.dynamic_index_in_dim(
+        totals[8 * width :].reshape(DEPTH, 2 * heads_w + unit_w), level, 0, keepdims=False
+    )
+    return (
+        from_places(layer_out, here),
+        from_places(grad_tokens, here),
+        small_total[0],
+        small_total[1],
+        full_grad_attn[:, :heads_w],
+        shared_total[:heads_w],
+        full_grad_attn[:, heads_w : 2 * heads_w],
+        full_grad_attn[:, 2 * heads_w :],
+        shared_total[heads_w : 2 * heads_w],
+        full_grad_out,
+        small_total[6],
+        small_total[4],
+        small_total[2],
+        small_total[3],
+        full_grad_up,
+        shared_total[2 * heads_w :],
+        full_grad_down,
+        small_total[7],
+        small_total[5],
+    )
+
+
+def local_general(
     tokens,
     slide_tiles,
     norm1_gain,
@@ -346,4 +862,6 @@
         P(),
         P(),
     )
+    paired = mesh.shape["dp"] == 8 and mesh.shape["mp"] == 4
+    local = local_paired if paired else local_general
     return jax.shard_map(local, mesh=mesh, in_specs=in_specs, out_specs=out_specs, check_vma=False)

time: 938 us -> 532 us (0.57)
  blocking collectives: 336 us -> 88.4 us
  waiting for transfers between devices: 294 us -> 160 us
  local copies, waits for them, and re-layouts: 106 us -> 51.3 us
  starting transfers between devices: 9.17 us -> 57.4 us
  matrix products: 111 us -> 64.7 us
  Pallas kernels: 0 us -> 39.9 us
    unnamed x5 -> x0, blocking collectives: 270 us -> none
    all_gather x6 -> x3, waiting for transfers between devices: 214 us -> 0.01 us  [the longest x1 0.01 us: local_paired(): lax.all_gather(grad_w_up.astype(jnp.bfloat16), 'dp', axis=0, tiled=True)]
    ppermute x0 -> x48, waiting for transfers between devices: none -> 159 us  [the longest x30 89.4 us: swap_plane(): return lax.ppermute(values, 'dp', [(i, i ^ mask) for i in range(PLANE)])]
    reduce_scatter x6 -> x0, waiting for transfers between devices: 77.4 us -> none  [the longest x1 27.2 us: local(): lax.psum_scatter(grad_w_query.astype(jnp.bfloat16), 'dp', scatter_dimensi...]
    ppermute x0 -> x48, starting transfers between devices: none -> 57.1 us  [the longest x18 28.8 us: swap_depth(): return lax.ppermute(values, 'mp', [(i, i ^ mask) for i in range(DEPTH)])]
    dot_general x24 -> x16, matrix products: 111 us -> 64.7 us  [the longest x8 28.7 us: dot_tn(): lax.dot_general(left, right, (((0,), (0,)), ((), ())), preferred_element_...]
    pallas_call x0 -> x4, Pallas kernels: none -> 39.9 us  [the longest x1 13.7 us: attention_backward(): pl.pallas_call(body, grid=(groups,), in_specs=[pl.BlockSpec((rows, group)...]
    psum x1, blocking collectives: 9.76 us -> 43.1 us  [local_paired(): lax.psum(jnp.concatenate([small.reshape(-1), shared]), ('dp', 'mp'))]
  transfers between devices with their start and end apart: 17 -> 51, of which waited for: 10 -> 23; matrix products, arithmetic and copies ran while one was open for 42% -> 26% of each run, Pallas kernels for 0% -> 6%
where the time goes in v1:
time: 532 us; the launch traced here: 526 us
  waiting for transfers between devices  160 us (30%)
  blocking collectives  88.4 us (17%)
  matrix products  64.7 us (12%)
  starting transfers between devices  57.4 us (11%)
  local copies, waits for them, and re-layouts  51.3 us (10%)
  other arithmetic  49.7 us (9%)
  Pallas kernels  39.9 us (8%)
  between operations  15.4 us (3%)
    ppermute x30, waiting for transfers between devices, swap_plane(): return lax.ppermute(values, 'dp', [(i, i ^ mask) for i in range(PLANE)])  89.4 us
    ppermute x18, waiting for transfers between devices, swap_depth(): return lax.ppermute(values, 'mp', [(i, i ^ mask) for i in range(DEPTH)])  70.1 us
    psum x1, blocking collectives, local_paired(): lax.psum(jnp.concatenate([small.reshape(-1), shared]), ('dp', 'mp'))  43.1 us
    all_gather x1, blocking collectives, local_paired(): lax.all_gather(jnp.concatenate([b_query, b_value, b_up]), 'mp', axis=0)  35.8 us
    unnamed x190, local copies, waits for them, and re-layouts  34.2 us
    ppermute x18, starting transfers between devices, swap_depth(): return lax.ppermute(values, 'mp', [(i, i ^ mask) for i in range(DEPTH)])  28.8 us
    dot_general x8, matrix products, dot_tn(): lax.dot_general(left, right, (((0,), (0,)), ((), ())), preferred_element_...  28.7 us
    ppermute x30, starting transfers between devices, swap_plane(): return lax.ppermute(values, 'dp', [(i, i ^ mask) for i in range(PLANE)])  28.3 us
  transfers between devices with their start and end apart: 51, of which 23 were waited for; matrix products, arithmetic and copies ran while one was open for 26% of the time, Pallas kernels for 6%

profile of v1, /device:TPU:0, one launch (start us, length us, event | category | flops | bytes accessed | tf_op | source)
XLA Modules:
  0.0 526.3 jit_solution(11289120712506035560)
XLA Ops:
  8.1 3.0 collective-permute-start.8
  11.2 2.5 collective-permute-start.10
  20.8 1.8 collective-permute-start.9
  22.7 35.8 %all-gather.1 = f32[4,1,1536]{2,1,0:T(1,128)S(1)} all-gather(f32[1,1,1536]{2,1,0:T(1,128)S(1)} %reshape.216), channel_id=2, replica_groups=mesh['dp'=8,'mp'=4] {'mp'}, dimensions={0}, use_global_device_ids=true | all-gather | bytes 30720 | tf_op jit(solution)/shard_map/all_gather | solution.py:410
  62.8 2.8 collective-permute-start.2
  68.3 2.1 collective-permute-done.2
  78.5 8.3 %collective-permute-done.3 = bf16[18,128,128]{2,1,0:T(8,128)(2,1)S(1)} collective-permute-done((bf16[18,128,128]{2,1,0:T(8,128)(2,1)S(1)}, bf16[18,128,128]{2,1,0:T(8,128)(2,1)S(1)}, u32[]{:S(2)}, u32[]{:S(2)}) %collective-permute-start.3) | collective-permute-done | bytes 589856 | tf_op jit(solution)/shard_map/ppermute | solution.py:57
  92.4 9.9 %collective-permute-done.11 = bf16[22,128,128]{2,1,0:T(8,128)(2,1)S(1)} collective-permute-done((bf16[22,128,128]{2,1,0:T(8,128)(2,1)S(1)}, bf16[22,128,128]{2,1,0:T(8,128)(2,1)S(1)}, u32[]{:S(2)}, u32[]{:S(2)}) %collective-permute-start.11) | collective-permute-done | bytes 720928 | tf_op jit(solution)/shard_map/ppermute | solution.py:57
  110.0 1.7 pad_maximum_fusion.1.mine_ref
  114.0 2.0 pad_maximum_fusion.mine_ref
  117.4 8.8 %assemble_attn.1 = bf16[1024,3072]{1,0:T(8,128)(2,1)} custom-call(s32[8]{0:T(128)} %stack.129.table_ref, bf16[1024,768]{1,0:T(8,128)(2,1)} %copy-done.14, bf16[4,18,128,128]{3,2,1,0:T(8,128)(2,1)} %copy-done.7, bf16[4,18,128,128]{3,2,1,0:T(8,128)(2,1)} %collective-permute-done.7.other_ref), custom_call_target="tpu_custom_call" | custom-call | bytes 12582912 | tf_op jit(solution)/shard_map/assemble_attn/pallas_call | solution.py:134
  126.2 5.7 %add_convert_fusion.qkv_ref = bf16[394,3072]{1,0:T(8,128)(2,1)S(1)} fusion(bf16[394,1024]{1,0:T(8,128)(2,1)S(1)} %fusion.13, bf16[1024,3072]{1,0:T(8,128)(2,1)} %assemble_attn.1, f32[3072]{0:T(1024)S(1)} %constant_dynamic-update-slice_fusion.46), kind=kOutput, calls=%fused_computation.11 | convolution fusion | flops 2481254400 | bytes 9531392 | tf_op jit(solution)/shard_map/dot_general | solution.py:222
  131.9 7.0 %attention_forward.1 = (bf16[394,1024]{1,0:T(8,128)(2,1)S(1)}, bf16[4,2,2,2,208,208]{5,4,3,2,1,0:T(8,128)(2,1)}) custom-call(bf16[394,3072]{1,0:T(8,128)(2,1)S(1)} %add_convert_fusion.qkv_ref), custom_call_target="tpu_custom_call" | custom-call | flops 1000000000 | bytes 8388608 | tf_op jit(solution)/shard_map/attention_forward/pallas_call | solution.py:268
  139.0 10.5 %assemble_rest.1 = (bf16[1024,1024]{1,0:T(8,128)(2,1)}, bf16[1024,2048]{1,0:T(8,128)(2,1)}, bf16[2048,1024]{1,0:T(8,128)(2,1)}) custom-call(s32[8]{0:T(128)} %stack.129.table_ref, bf16[256,1024]{1,0:T(8,128)(2,1)} %own_o_ref.1, bf16[1024,1024]{1,0:T(8,128)(2,1)} %own_up_ref.1, bf16[1024,1024]{1,0:T(8,128)(2,1)} %own_down_ref.1, ...), custom_call_target="tpu_custom_call" | custom-call | bytes 20971520 | tf_op jit(solution)/shard_map/assemble_rest/pallas_call | solution.py:185
  149.4 3.8 fusion.64
  157.2 1.9 collective-permute-start.18
  159.1 17.1 %collective-permute-done.16 = bf16[394,1024]{1,0:T(8,128)(2,1)} collective-permute-done((bf16[394,1024]{1,0:T(8,128)(2,1)}, bf16[394,1024]{1,0:T(8,128)(2,1)}, u32[]{:S(2)}, u32[]{:S(2)}) %collective-permute-start.16) | collective-permute-done | bytes 806944 | tf_op jit(solution)/shard_map/ppermute | solution.py:61
  176.2 6.9 %multiply_convert_fusion = (bf16[788,2048]{1,0:T(8,128)(2,1)S(1)}, f32[788,2048]{1,0:T(8,128)S(1)}) fusion(f32[2048]{0:T(1024)S(1)} %pad_maximum_fusion.16, bf16[1024,2048]{1,0:T(8,128)(2,1)} %get-tuple-element.26, bf16[394,1024]{1,0:T(8,128)(2,1)} %collective-permute-done.16, bf16[394,1024]{1,0:T(8,128)(2,1)} %add_convert_fusion.1), kind=kOutput, calls=%fused_computation.8 | convolution fusion | flops 3318022144 | bytes 15499264 | tf_op jit(solution)/shard_map/dot_general | solution.py:222
  183.1 10.3 %collective-permute-done.18 = bf16[394,1024]{1,0:T(8,128)(2,1)} collective-permute-done((bf16[394,1024]{1,0:T(8,128)(2,1)}, bf16[394,1024]{1,0:T(8,128)(2,1)}, u32[]{:S(2)}, u32[]{:S(2)}) %collective-permute-start.18) | collective-permute-done | bytes 806944 | tf_op jit(solution)/shard_map/ppermute | solution.py:61
  193.4 8.5 %convert_reduce_fusion = (f32[2048]{0:T(1024)S(1)}, bf16[788,2048]{1,0:T(8,128)(2,1)S(1)}) fusion(f32[788,2048]{1,0:T(8,128)S(1)} %get-tuple-element.195, f32[2048]{0:T(1024)S(1)} %pad_maximum_fusion.16, bf16[2048,1024]{1,0:T(8,128)(2,1)S(1)} %copy-done.55, bf16[394,1024]{1,0:T(8,128)(2,1)} %collective-permute-done.18, bf16[394,1024]{1,0:T(8,128)(2,1)} %fusion.19), kind=kOutput, calls=%fused_computation.7 | convolution fusion | flops 3329316864 | bytes 15507456 | tf_op jit(solution)/shard_map/dot_general | solution.py:214
  201.9 3.6 convolution_convert_fusion.6
  206.1 3.5 convolution_convert_fusion.7
  209.8 1.8 collective-permute-start.17
  211.6 4.9 convolution_convert_fusion.4
  216.5 4.9 convolution_convert_fusion.2
  222.0 5.1 convolution_convert_fusion.5
  227.1 4.9 convolution_convert_fusion.3
  233.6 9.6 %collective-permute-done.17 = bf16[394,1024]{1,0:T(8,128)(2,1)S(1)} collective-permute-done((bf16[394,1024]{1,0:T(8,128)(2,1)S(1)}, bf16[394,1024]{1,0:T(8,128)(2,1)S(1)}, u32[]{:S(2)}, u32[]{:S(2)}) %collective-permute-start.17) | collective-permute-done | bytes 806944 | tf_op jit(solution)/shard_map/ppermute | solution.py:61
  243.2 2.8 multiply_reduce_fusion.5
  248.0 13.7 %attention_backward.1 = bf16[394,3072]{1,0:T(8,128)(2,1)S(1)} custom-call(bf16[394,3072]{1,0:T(8,128)(2,1)S(1)} %copy-done.1, bf16[4,2,2,2,208,208]{5,4,3,2,1,0:T(8,128)(2,1)} %get-tuple-element.28.prob_ref, bf16[394,1024]{1,0:T(8,128)(2,1)S(1)} %convolution_convert_fusion.10.grad_ref), custom_call_target="tpu_custom_call" | custom-call | flops 2000000000 | bytes 12582912 | tf_op jit(solution)/shard_map/attention_backward/pallas_call | solution.py:325
  261.7 2.9 fusion.62
  278.8 3.5 convolution_convert_fusion
  282.3 7.0 %collective-permute-done.37 = bf16[256,1024]{1,0:T(8,128)(2,1)S(1)} collective-permute-done((bf16[256,1024]{1,0:T(8,128)(2,1)S(1)}, bf16[256,1024]{1,0:T(8,128)(2,1)S(1)}, u32[]{:S(2)}, u32[]{:S(2)}) %collective-permute-start.37) | collective-permute-done | bytes 524320 | tf_op jit(solution)/shard_map/ppermute | solution.py:57
  294.1 3.8 collective-permute-done.40
  299.0 1.9 collective-permute-start.41
  301.0 1.7 convolution_convert_fusion.8
  302.7 7.6 %collective-permute-done.41 = bf16[128,1024]{1,0:T(8,128)(2,1)S(1)} collective-permute-done((bf16[128,1024]{1,0:T(8,128)(2,1)S(1)}, bf16[128,1024]{1,0:T(8,128)(2,1)S(1)}, u32[]{:S(2)}, u32[]{:S(2)}) %collective-permute-start.41) | collective-permute-done | bytes 262176 | tf_op jit(solution)/shard_map/ppermute | solution.py:61
  310.3 1.9 add_convert_fusion.17
  314.1 3.7 add_add_fusion.2
  322.2 1.9 convolution_convert_fusion.1
  324.1 10.5 %collective-permute-done.43 = bf16[1024,256]{0,1:T(8,128)(2,1)S(1)} collective-permute-done((bf16[1024,256]{0,1:T(8,128)(2,1)S(1)}, bf16[1024,256]{0,1:T(8,128)(2,1)S(1)}, u32[]{:S(2)}, u32[]{:S(2)}) %collective-permute-start.43) | collective-permute-done | bytes 524320 | tf_op jit(solution)/shard_map/ppermute | solution.py:57
  336.1 2.0 add_convert_fusion.14
  338.4 1.9 collective-permute-start.44
  341.9 4.2 collective-permute-done.46
  346.2 1.8 add_convert_fusion.10
  348.0 1.7 collective-permute-start.47
  349.8 12.3 %collective-permute-done.47 = bf16[1024,128]{0,1:T(8,128)(2,1)} collective-permute-done((bf16[1024,128]{0,1:T(8,128)(2,1)}, bf16[1024,128]{0,1:T(8,128)(2,1)}, u32[]{:S(2)}, u32[]{:S(2)}) %collective-permute-start.47) | collective-permute-done | bytes 262176 | tf_op jit(solution)/shard_map/ppermute | solution.py:61
  362.1 2.2 add_convert_fusion.9
  365.3 1.9 add_convert_fusion.3
  369.7 1.7 convolution_convert_fusion.9
  371.4 31.3 %collective-permute-done.25 = bf16[128,1536]{1,0:T(8,128)(2,1)S(1)} collective-permute-done((bf16[128,1536]{1,0:T(8,128)(2,1)S(1)}, bf16[128,1536]{1,0:T(8,128)(2,1)S(1)}, u32[]{:S(2)}, u32[]{:S(2)}) %collective-permute-start.25) | collective-permute-done | bytes 393248 | tf_op jit(solution)/shard_map/ppermute | solution.py:57
  405.4 4.7 collective-permute-start.27
  410.1 3.6 collective-permute-done.22
  415.0 2.0 collective-permute-start.23
  417.1 8.0 %collective-permute-done.26 = bf16[128,768]{1,0:T(8,128)(2,1)S(1)} collective-permute-done((bf16[128,768]{1,0:T(8,128)(2,1)S(1)}, bf16[128,768]{1,0:T(8,128)(2,1)S(1)}, u32[]{:S(2)}, u32[]{:S(2)}) %collective-permute-start.26) | collective-permute-done | bytes 196640 | tf_op jit(solution)/shard_map/ppermute | solution.py:61
  430.3 43.1 %psum.7 = f32[14336]{0:T(1024)S(1)} all-reduce(f32[14336]{0:T(1024)S(1)} %constant_dynamic-update-slice_fusion.54), channel_id=1, replica_groups=mesh['dp'=8,'mp'=4] {'dp','mp'}, use_global_device_ids=true, to_apply=%region_19.20 | all-reduce | flops 14336 | bytes 114688 | tf_op jit(solution)/shard_map/psum | solution.py:535
  474.0 1.8 add_convert_fusion.26
  475.9 2.3 collective-permute-start.29
  481.8 4.3 collective-permute-done.33
  490.0 2.2 collective-permute-done.30
  497.6 9.5 %all_gather.21 = bf16[256,1024]{0,1:T(8,128)(2,1)S(1)} all-gather(bf16[256,128]{0,1:T(8,128)(2,1)S(1)} %fusion.39), channel_id=1, replica_groups=mesh['dp'=8,'mp'=4] {'dp'}, dimensions={1}, use_global_device_ids=true | all-gather | bytes 589824 | tf_op jit(solution)/shard_map/all_gather | solution.py:494
  508.3 4.1 convert_element_type.551
  512.3 4.1 copy.66
  516.4 3.1 fusion.65
  (362 shorter events, 105.3 us)
Async XLA Ops:
  7.2 501.1 %all-gather.8.cloned.1.call-start = ((), (), s32[]{:S(2)}) async-start(), calls=%async_computation.1 | async-start | bytes 2359296 | tf_op jit(solution)/shard_map/all_gather | solution.py:476
  8.1 54.6 %collective-permute-start.8 = (bf16[2,128,128]{2,1,0:T(8,128)(2,1)S(1)}, bf16[2,128,128]{2,1,0:T(8,128)(2,1)}, u32[]{:S(2)}, u32[]{:S(2)}) collective-permute-start(bf16[2,128,128]{2,1,0:T(8,128)(2,1)S(1)} %bitcast.108), channel_id=1, source_target_pairs={{0,1},{1,0},{2,3},{3,2},{4,5},{5,4},{6,7},{7,6},{8,9},{9,8},{10,11... | collective-permute-start | bytes 196616 | tf_op jit(solution)/shard_map/ppermute | solution.py:61
  11.2 62.5 %collective-permute-start.10 = (bf16[2,128,128]{2,1,0:T(8,128)(2,1)S(1)}, bf16[2,128,128]{2,1,0:T(8,128)(2,1)S(1)}, u32[]{:S(2)}, u32[]{:S(2)}) collective-permute-start(bf16[2,128,128]{2,1,0:T(8,128)(2,1)S(1)} %bitcast.109), channel_id=1, source_target_pairs={{0,3},{1,2},{2,1},{3,0},{4,7},{5,6},{6,5},{7,4},{8,11},{9,10},{10,... | collective-permute-start | bytes 196616 | tf_op jit(solution)/shard_map/ppermute | solution.py:61
  16.4 50.1 %collective-permute-start = (bf16[6,128,128]{2,1,0:T(8,128)(2,1)S(1)}, bf16[6,128,128]{2,1,0:T(8,128)(2,1)}, u32[]{:S(2)}, u32[]{:S(2)}) collective-permute-start(bf16[6,128,128]{2,1,0:T(8,128)(2,1)S(1)} %bitcast.111), channel_id=1, source_target_pairs={{0,1},{1,0},{2,3},{3,2},{4,5},{5,4},{6,7},{7,6},{8,9},{9,8},{10,11... | collective-permute-start | bytes 589832 | tf_op jit(solution)/shard_map/ppermute | solution.py:61
  17.1 50.3 %collective-permute-start.1 = (bf16[6,128,128]{2,1,0:T(8,128)(2,1)S(1)}, bf16[6,128,128]{2,1,0:T(8,128)(2,1)}, u32[]{:S(2)}, u32[]{:S(2)}) collective-permute-start(bf16[6,128,128]{2,1,0:T(8,128)(2,1)S(1)} %bitcast.112), channel_id=1, source_target_pairs={{0,2},{1,3},{2,0},{3,1},{4,6},{5,7},{6,4},{7,5},{8,10},{9,11},{10,... | collective-permute-start | bytes 589832 | tf_op jit(solution)/shard_map/ppermute | solution.py:61
  20.8 52.8 %collective-permute-start.9 = (bf16[18,128,128]{2,1,0:T(8,128)(2,1)S(1)}, bf16[18,128,128]{2,1,0:T(8,128)(2,1)S(1)}, u32[]{:S(2)}, u32[]{:S(2)}) collective-permute-start(bf16[18,128,128]{2,1,0:T(8,128)(2,1)S(1)} %pad_maximum_fusion.8), channel_id=1, source_target_pairs={{0,2},{1,3},{2,0},{3,1},{4,6},{5,7},{6,4},{7,5},{8,10},{9,11},{10,... | collective-permute-start | bytes 1769480 | tf_op jit(solution)/shard_map/ppermute | solution.py:61
  62.8 7.6 %collective-permute-start.2 = (bf16[6,128,128]{2,1,0:T(8,128)(2,1)S(1)}, bf16[6,128,128]{2,1,0:T(8,128)(2,1)S(1)}, u32[]{:S(2)}, u32[]{:S(2)}) collective-permute-start(bf16[6,128,128]{2,1,0:T(8,128)(2,1)S(1)} %bitcast.113), channel_id=1, source_target_pairs={{0,3},{1,2},{2,1},{3,0},{4,7},{5,6},{6,5},{7,4},{8,11},{9,10},{10,... | collective-permute-start | bytes 589832 | tf_op jit(solution)/shard_map/ppermute | solution.py:61
  70.5 19.4 %copy-start.20 = (bf16[18,128,128]{2,1,0:T(8,128)(2,1)}, bf16[18,128,128]{2,1,0:T(8,128)(2,1)S(1)}, u32[]{:S(2)}) copy-start(bf16[18,128,128]{2,1,0:T(8,128)(2,1)S(1)} %constant_dynamic-update-slice_fusion.19) | copy-start | bytes 1769476
  70.5 16.3 %collective-permute-start.3 = (bf16[18,128,128]{2,1,0:T(8,128)(2,1)S(1)}, bf16[18,128,128]{2,1,0:T(8,128)(2,1)S(1)}, u32[]{:S(2)}, u32[]{:S(2)}) collective-permute-start(bf16[18,128,128]{2,1,0:T(8,128)(2,1)S(1)} %constant_dynamic-update-slice_fusion.19), channel_id=1, source_target_pairs={{0,8},{4,12},{8,0},{12,4},{16,24},{20,28},{24,16},{28,20},{1,9},{5... | collective-permute-start | bytes 1769480 | tf_op jit(solution)/shard_map/ppermute | solution.py:57
  72.0 17.1 %collective-permute-start.4 = (bf16[18,128,128]{2,1,0:T(8,128)(2,1)S(1)}, bf16[18,128,128]{2,1,0:T(8,128)(2,1)S(1)}, u32[]{:S(2)}, u32[]{:S(2)}) collective-permute-start(bf16[18,128,128]{2,1,0:T(8,128)(2,1)S(1)} %constant_dynamic-update-slice_fusion.19), channel_id=1, source_target_pairs={{0,16},{4,20},{8,24},{12,28},{16,0},{20,4},{24,8},{28,12},{1,17},{... | collective-permute-start | bytes 1769480 | tf_op jit(solution)/shard_map/ppermute | solution.py:57
  73.7 31.0 %copy-start.21 = (bf16[22,128,128]{2,1,0:T(8,128)(2,1)}, bf16[22,128,128]{2,1,0:T(8,128)(2,1)S(1)}, u32[]{:S(2)}) copy-start(bf16[22,128,128]{2,1,0:T(8,128)(2,1)S(1)} %constant_dynamic-update-slice_fusion.23) | copy-start | bytes 2162692
  73.7 28.6 %collective-permute-start.11 = (bf16[22,128,128]{2,1,0:T(8,128)(2,1)S(1)}, bf16[22,128,128]{2,1,0:T(8,128)(2,1)S(1)}, u32[]{:S(2)}, u32[]{:S(2)}) collective-permute-start(bf16[22,128,128]{2,1,0:T(8,128)(2,1)S(1)} %constant_dynamic-update-slice_fusion.23), channel_id=1, source_target_pairs={{0,8},{4,12},{8,0},{12,4},{16,24},{20,28},{24,16},{28,20},{1,9},{5... | collective-permute-start | bytes 2162696 | tf_op jit(solution)/shard_map/ppermute | solution.py:57
  74.3 29.6 %collective-permute-start.12 = (bf16[22,128,128]{2,1,0:T(8,128)(2,1)S(1)}, bf16[22,128,128]{2,1,0:T(8,128)(2,1)S(1)}, u32[]{:S(2)}, u32[]{:S(2)}) collective-permute-start(bf16[22,128,128]{2,1,0:T(8,128)(2,1)S(1)} %constant_dynamic-update-slice_fusion.23), channel_id=1, source_target_pairs={{0,16},{4,20},{8,24},{12,28},{16,0},{20,4},{24,8},{28,12},{1,17},{... | collective-permute-start | bytes 2162696 | tf_op jit(solution)/shard_map/ppermute | solution.py:57
  86.8 17.1 %copy-start.18 = (bf16[18,128,128]{2,1,0:T(8,128)(2,1)}, bf16[18,128,128]{2,1,0:T(8,128)(2,1)S(1)}, u32[]{:S(2)}) copy-start(bf16[18,128,128]{2,1,0:T(8,128)(2,1)S(1)} %collective-permute-done.3) | copy-start | bytes 1769476
  87.6 21.3 %collective-permute-start.6 = (bf16[9,128,128]{2,1,0:T(8,128)(2,1)}, bf16[9,128,128]{2,1,0:T(8,128)(2,1)}, u32[]{:S(2)}, u32[]{:S(2)}) collective-permute-start(bf16[9,128,128]{2,1,0:T(8,128)(2,1)} %slice.736), channel_id=1, source_target_pairs={{0,16},{4,20},{8,24},{12,28},{16,0},{20,4},{24,8},{28,12},{1,17},{... | collective-permute-start | bytes 884744 | tf_op jit(solution)/shard_map/ppermute | solution.py:57
  89.1 15.5 %copy-start.19 = (bf16[18,128,128]{2,1,0:T(8,128)(2,1)}, bf16[18,128,128]{2,1,0:T(8,128)(2,1)S(1)}, u32[]{:S(2)}) copy-start(bf16[18,128,128]{2,1,0:T(8,128)(2,1)S(1)} %collective-permute-done.4) | copy-start | bytes 1769476
  89.9 19.0 %collective-permute-start.5 = (bf16[9,128,128]{2,1,0:T(8,128)(2,1)}, bf16[9,128,128]{2,1,0:T(8,128)(2,1)}, u32[]{:S(2)}, u32[]{:S(2)}) collective-permute-start(bf16[9,128,128]{2,1,0:T(8,128)(2,1)} %slice.735), channel_id=1, source_target_pairs={{0,8},{4,12},{8,0},{12,4},{16,24},{20,28},{24,16},{28,20},{1,9},{5... | collective-permute-start | bytes 884744 | tf_op jit(solution)/shard_map/ppermute | solution.py:57
  92.3 57.1 %copy-start.2 = (bf16[394,1024]{1,0:T(8,128)(2,1)}, bf16[394,1024]{1,0:T(8,128)(2,1)S(1)}, u32[]{:S(2)}) copy-start(bf16[394,1024]{1,0:T(8,128)(2,1)S(1)} %constant_dynamic-update-slice_fusion) | copy-start | bytes 2420740
  102.3 10.5 %collective-permute-start.14 = (bf16[11,128,128]{2,1,0:T(8,128)(2,1)S(1)}, bf16[11,128,128]{2,1,0:T(8,128)(2,1)}, u32[]{:S(2)}, u32[]{:S(2)}) collective-permute-start(bf16[11,128,128]{2,1,0:T(8,128)(2,1)S(1)} %slice.746), channel_id=1, source_target_pairs={{0,16},{4,20},{8,24},{12,28},{16,0},{20,4},{24,8},{28,12},{1,17},{... | collective-permute-start | bytes 1081352 | tf_op jit(solution)/shard_map/ppermute | solution.py:57
  104.6 8.1 %collective-permute-start.13 = (bf16[11,128,128]{2,1,0:T(8,128)(2,1)}, bf16[11,128,128]{2,1,0:T(8,128)(2,1)}, u32[]{:S(2)}, u32[]{:S(2)}) collective-permute-start(bf16[11,128,128]{2,1,0:T(8,128)(2,1)} %slice.745), channel_id=1, source_target_pairs={{0,8},{4,12},{8,0},{12,4},{16,24},{20,28},{24,16},{28,20},{1,9},{5... | collective-permute-start | bytes 1081352 | tf_op jit(solution)/shard_map/ppermute | solution.py:57
  111.8 5.7 %collective-permute-start.7 = (bf16[4,18,128,128]{3,2,1,0:T(8,128)(2,1)S(1)}, bf16[4,18,128,128]{3,2,1,0:T(8,128)(2,1)}, u32[]{:S(2)}, u32[]{:S(2)}) collective-permute-start(bf16[4,18,128,128]{3,2,1,0:T(8,128)(2,1)S(1)} %pad_maximum_fusion.1.mine_ref), channel_id=1, source_target_pairs={{0,4},{4,0},{8,12},{12,8},{16,20},{20,16},{24,28},{28,24},{1,5},{5... | collective-permute-start | bytes 7077896 | tf_op jit(solution)/shard_map/ppermute | solution.py:57
  116.0 22.9 %collective-permute-start.15 = (bf16[4,22,128,128]{3,2,1,0:T(8,128)(2,1)}, bf16[4,22,128,128]{3,2,1,0:T(8,128)(2,1)}, u32[]{:S(2)}, u32[]{:S(2)}) collective-permute-start(bf16[4,22,128,128]{3,2,1,0:T(8,128)(2,1)} %pad_maximum_fusion.mine_ref), channel_id=1, source_target_pairs={{0,4},{4,0},{8,12},{12,8},{16,20},{20,16},{24,28},{28,24},{1,5},{5... | collective-permute-start | bytes 8650760 | tf_op jit(solution)/shard_map/ppermute | solution.py:57
  154.9 21.4 %collective-permute-start.16 = (bf16[394,1024]{1,0:T(8,128)(2,1)}, bf16[394,1024]{1,0:T(8,128)(2,1)}, u32[]{:S(2)}, u32[]{:S(2)}) collective-permute-start(bf16[394,1024]{1,0:T(8,128)(2,1)} %add_convert_fusion.1), channel_id=1, source_target_pairs={{0,1},{1,0},{2,3},{3,2},{4,5},{5,4},{6,7},{7,6},{8,9},{9,8},{10,11... | collective-permute-start | bytes 2420744 | tf_op jit(solution)/shard_map/ppermute | solution.py:61
  156.0 87.2 %copy-start.11 = (bf16[394,1024]{1,0:T(8,128)(2,1)}, bf16[394,1024]{1,0:T(8,128)(2,1)S(1)}, u32[]{:S(2)}) copy-start(bf16[394,1024]{1,0:T(8,128)(2,1)S(1)} %constant_dynamic-update-slice_fusion.26) | copy-start | bytes 2420740
  157.2 36.2 %collective-permute-start.18 = (bf16[394,1024]{1,0:T(8,128)(2,1)}, bf16[394,1024]{1,0:T(8,128)(2,1)}, u32[]{:S(2)}, u32[]{:S(2)}) collective-permute-start(bf16[394,1024]{1,0:T(8,128)(2,1)} %fusion.19), channel_id=1, source_target_pairs={{0,1},{1,0},{2,3},{3,2},{4,5},{5,4},{6,7},{7,6},{8,9},{9,8},{10,11... | collective-permute-start | bytes 2420744 | tf_op jit(solution)/shard_map/ppermute | solution.py:61
  176.2 17.2 %copy-start.55 = (bf16[2048,1024]{1,0:T(8,128)(2,1)S(1)}, bf16[2048,1024]{1,0:T(8,128)(2,1)}, u32[]{:S(2)}) copy-start(bf16[2048,1024]{1,0:T(8,128)(2,1)} %get-tuple-element.27) | copy-start | bytes 12582916
  205.7 26.3 %collective-permute-start.19 = (bf16[394,1024]{1,0:T(8,128)(2,1)S(1)}, bf16[394,1024]{1,0:T(8,128)(2,1)S(1)}, u32[]{:S(2)}, u32[]{:S(2)}) collective-permute-start(bf16[394,1024]{1,0:T(8,128)(2,1)S(1)} %slice.752), channel_id=1, source_target_pairs={{0,1},{1,0},{2,3},{3,2},{4,5},{5,4},{6,7},{7,6},{8,9},{9,8},{10,11... | collective-permute-start | bytes 2420744 | tf_op jit(solution)/shard_map/ppermute | solution.py:61
  209.8 33.4 %collective-permute-start.17 = (bf16[394,1024]{1,0:T(8,128)(2,1)S(1)}, bf16[394,1024]{1,0:T(8,128)(2,1)S(1)}, u32[]{:S(2)}, u32[]{:S(2)}) collective-permute-start(bf16[394,1024]{1,0:T(8,128)(2,1)S(1)} %slice.750), channel_id=1, source_target_pairs={{0,1},{1,0},{2,3},{3,2},{4,5},{5,4},{6,7},{7,6},{8,9},{9,8},{10,11... | collective-permute-start | bytes 2420744 | tf_op jit(solution)/shard_map/ppermute | solution.py:61
  216.5 58.4 %collective-permute-start.36 = (bf16[512,2048]{1,0:T(8,128)(2,1)}, bf16[512,2048]{1,0:T(8,128)(2,1)}, u32[]{:S(2)}, u32[]{:S(2)}) collective-permute-start(bf16[512,2048]{1,0:T(8,128)(2,1)} %convolution_convert_fusion.4), channel_id=1, source_target_pairs={{0,4},{4,0},{8,12},{12,8},{16,20},{20,16},{24,28},{28,24},{1,5},{5... | collective-permute-start | bytes 6291464 | tf_op jit(solution)/shard_map/ppermute | solution.py:57
  221.5 96.4 %collective-permute-start.42 = (bf16[2048,512]{0,1:T(8,128)(2,1)}, bf16[2048,512]{0,1:T(8,128)(2,1)}, u32[]{:S(2)}, u32[]{:S(2)}) collective-permute-start(bf16[2048,512]{0,1:T(8,128)(2,1)} %convolution_convert_fusion.2), channel_id=1, source_target_pairs={{0,4},{4,0},{8,12},{12,8},{16,20},{20,16},{24,28},{28,24},{1,5},{5... | collective-permute-start | bytes 6291464 | tf_op jit(solution)/shard_map/ppermute | solution.py:57
  243.2 18.5 %slice-start = ((s8[6291456]{0:T(1024)(128)(4,1)}), s8[4194304]{0:T(1024)(128)(4,1)S(1)}, s32[]{:S(2)}) async-start(s8[6291456]{0:T(1024)(128)(4,1)} %bitcast.96), calls=%async_computation.3 | async-start | bytes 8388608
  246.0 15.7 %slice-start.1 = ((s8[6291456]{0:T(1024)(128)(4,1)}), s8[2097152]{0:T(1024)(128)(4,1)S(1)}, s32[]{:S(2)}) async-start(s8[6291456]{0:T(1024)(128)(4,1)} %bitcast.96), calls=%async_computation.4 | async-start | bytes 4194304
  248.0 13.7 %copy-start.3 = (bf16[394,1024]{1,0:T(8,128)(2,1)S(1)}, bf16[394,1024]{1,0:T(8,128)(2,1)}, u32[]{:S(2)}) copy-start(bf16[394,1024]{1,0:T(8,128)(2,1)} %copy-done.2) | copy-start | bytes 2420740
  276.6 12.7 %collective-permute-start.37 = (bf16[256,1024]{1,0:T(8,128)(2,1)S(1)}, bf16[256,1024]{1,0:T(8,128)(2,1)S(1)}, u32[]{:S(2)}, u32[]{:S(2)}) collective-permute-start(bf16[256,1024]{1,0:T(8,128)(2,1)S(1)} %pad_maximum_fusion.9), channel_id=1, source_target_pairs={{0,8},{4,12},{8,0},{12,4},{16,24},{20,28},{24,16},{28,20},{1,9},{5... | collective-permute-start | bytes 1572872 | tf_op jit(solution)/shard_map/ppermute | solution.py:57
  277.7 12.4 %collective-permute-start.39 = (bf16[256,1024]{1,0:T(8,128)(2,1)S(1)}, bf16[256,1024]{1,0:T(8,128)(2,1)S(1)}, u32[]{:S(2)}, u32[]{:S(2)}) collective-permute-start(bf16[256,1024]{1,0:T(8,128)(2,1)S(1)} %pad_maximum_fusion.10), channel_id=1, source_target_pairs={{0,16},{4,20},{8,24},{12,28},{16,0},{20,4},{24,8},{28,12},{1,17},{... | collective-permute-start | bytes 1572872 | tf_op jit(solution)/shard_map/ppermute | solution.py:57
  282.3 18.7 %copy-start.24 = (bf16[394,1024]{1,0:T(8,128)(2,1)S(1)}, bf16[394,1024]{1,0:T(8,128)(2,1)}, u32[]{:S(2)}) copy-start(bf16[394,1024]{1,0:T(8,128)(2,1)} %copy-done.23) | copy-start | bytes 2420740
  291.5 6.4 %collective-permute-start.40 = (bf16[128,1024]{1,0:T(8,128)(2,1)S(1)}, bf16[128,1024]{1,0:T(8,128)(2,1)S(1)}, u32[]{:S(2)}, u32[]{:S(2)}) collective-permute-start(bf16[128,1024]{1,0:T(8,128)(2,1)S(1)} %get-tuple-element.138), channel_id=1, source_target_pairs={{0,8},{4,12},{8,0},{12,4},{16,24},{20,28},{24,16},{28,20},{1,9},{5... | collective-permute-start | bytes 786440 | tf_op jit(solution)/shard_map/ppermute | solution.py:57
  292.5 47.8 %collective-permute-start.20 = (bf16[512,3072]{1,0:T(8,128)(2,1)}, bf16[512,3072]{1,0:T(8,128)(2,1)}, u32[]{:S(2)}, u32[]{:S(2)}) collective-permute-start(bf16[512,3072]{1,0:T(8,128)(2,1)} %convolution_convert_fusion), channel_id=1, source_target_pairs={{0,4},{4,0},{8,12},{12,8},{16,20},{20,16},{24,28},{28,24},{1,5},{5... | collective-permute-start | bytes 9437192 | tf_op jit(solution)/shard_map/ppermute | solution.py:57
  292.5 10.2 %collective-permute-start.38 = (bf16[128,1024]{1,0:T(8,128)(2,1)S(1)}, bf16[128,1024]{1,0:T(8,128)(2,1)S(1)}, u32[]{:S(2)}, u32[]{:S(2)}) collective-permute-start(bf16[128,1024]{1,0:T(8,128)(2,1)S(1)} %get-tuple-element.137), channel_id=1, source_target_pairs={{0,16},{4,20},{8,24},{12,28},{16,0},{20,4},{24,8},{28,12},{1,17},{... | collective-permute-start | bytes 786440 | tf_op jit(solution)/shard_map/ppermute | solution.py:57
  299.0 11.3 %collective-permute-start.41 = (bf16[128,1024]{1,0:T(8,128)(2,1)S(1)}, bf16[128,1024]{1,0:T(8,128)(2,1)S(1)}, u32[]{:S(2)}, u32[]{:S(2)}) collective-permute-start(bf16[128,1024]{1,0:T(8,128)(2,1)S(1)} %add_convert_fusion.18), channel_id=1, source_target_pairs={{0,2},{1,3},{2,0},{3,1},{4,6},{5,7},{6,4},{7,5},{8,10},{9,11},{10,... | collective-permute-start | bytes 786440 | tf_op jit(solution)/shard_map/ppermute | solution.py:61
  312.2 200.2 %all-gather.10.cloned.1.call-start = ((), (), s32[]{:S(2)}) async-start(), calls=%async_computation.2 | async-start | bytes 2359296 | tf_op jit(solution)/shard_map/all_gather | solution.py:470
  319.6 15.0 %collective-permute-start.43 = (bf16[1024,256]{0,1:T(8,128)(2,1)S(1)}, bf16[1024,256]{0,1:T(8,128)(2,1)S(1)}, u32[]{:S(2)}, u32[]{:S(2)}) collective-permute-start(bf16[1024,256]{0,1:T(8,128)(2,1)S(1)} %pad_maximum_fusion.11), channel_id=1, source_target_pairs={{0,8},{4,12},{8,0},{12,4},{16,24},{20,28},{24,16},{28,20},{1,9},{5... | collective-permute-start | bytes 1572872 | tf_op jit(solution)/shard_map/ppermute | solution.py:57
  320.6 15.5 %collective-permute-start.45 = (bf16[1024,256]{0,1:T(8,128)(2,1)S(1)}, bf16[1024,256]{0,1:T(8,128)(2,1)S(1)}, u32[]{:S(2)}, u32[]{:S(2)}) collective-permute-start(bf16[1024,256]{0,1:T(8,128)(2,1)S(1)} %pad_maximum_fusion.12), channel_id=1, source_target_pairs={{0,16},{4,20},{8,24},{12,28},{16,0},{20,4},{24,8},{28,12},{1,17},{... | collective-permute-start | bytes 1572872 | tf_op jit(solution)/shard_map/ppermute | solution.py:57
  324.1 17.6 %copy-start.15 = (bf16[512,3072]{1,0:T(8,128)(2,1)}, bf16[512,3072]{1,0:T(8,128)(2,1)S(1)}, u32[]{:S(2)}) copy-start(bf16[512,3072]{1,0:T(8,128)(2,1)S(1)} %convolution_convert_fusion.1) | copy-start | bytes 9437188
  338.1 8.1 %collective-permute-start.46 = (bf16[1024,128]{0,1:T(8,128)(2,1)S(1)}, bf16[1024,128]{0,1:T(8,128)(2,1)S(1)}, u32[]{:S(2)}, u32[]{:S(2)}) collective-permute-start(bf16[1024,128]{0,1:T(8,128)(2,1)S(1)} %get-tuple-element.132), channel_id=1, source_target_pairs={{0,8},{4,12},{8,0},{12,4},{16,24},{20,28},{24,16},{28,20},{1,9},{5... | collective-permute-start | bytes 786440 | tf_op jit(solution)/shard_map/ppermute | solution.py:57
  338.4 11.4 %collective-permute-start.44 = (bf16[1024,128]{0,1:T(8,128)(2,1)}, bf16[1024,128]{0,1:T(8,128)(2,1)}, u32[]{:S(2)}, u32[]{:S(2)}) collective-permute-start(bf16[1024,128]{0,1:T(8,128)(2,1)} %get-tuple-element.131), channel_id=1, source_target_pairs={{0,16},{4,20},{8,24},{12,28},{16,0},{20,4},{24,8},{28,12},{1,17},{... | collective-permute-start | bytes 786440 | tf_op jit(solution)/shard_map/ppermute | solution.py:57
  341.7 22.7 %collective-permute-start.24 = (bf16[256,1536]{1,0:T(8,128)(2,1)S(1)}, bf16[256,1536]{1,0:T(8,128)(2,1)S(1)}, u32[]{:S(2)}, u32[]{:S(2)}) collective-permute-start(bf16[256,1536]{1,0:T(8,128)(2,1)S(1)} %pad_maximum_fusion.7), channel_id=1, source_target_pairs={{0,16},{4,20},{8,24},{12,28},{16,0},{20,4},{24,8},{28,12},{1,17},{... | collective-permute-start | bytes 2359304 | tf_op jit(solution)/shard_map/ppermute | solution.py:57
  348.0 14.1 %collective-permute-start.47 = (bf16[1024,128]{0,1:T(8,128)(2,1)}, bf16[1024,128]{0,1:T(8,128)(2,1)}, u32[]{:S(2)}, u32[]{:S(2)}) collective-permute-start(bf16[1024,128]{0,1:T(8,128)(2,1)} %add_convert_fusion.10), channel_id=1, source_target_pairs={{0,2},{1,3},{2,0},{3,1},{4,6},{5,7},{6,4},{7,5},{8,10},{9,11},{10,... | collective-permute-start | bytes 786440 | tf_op jit(solution)/shard_map/ppermute | solution.py:61
  349.7 78.2 %collective-permute-start.28 = (bf16[1024,512]{0,1:T(8,128)(2,1)}, bf16[1024,512]{0,1:T(8,128)(2,1)S(1)}, u32[]{:S(2)}, u32[]{:S(2)}) collective-permute-start(bf16[1024,512]{0,1:T(8,128)(2,1)} %convolution_convert_fusion.8), channel_id=1, source_target_pairs={{0,4},{4,0},{8,12},{12,8},{16,20},{20,16},{24,28},{28,24},{1,5},{5... | collective-permute-start | bytes 3145736 | tf_op jit(solution)/shard_map/ppermute | solution.py:57
  364.3 152.1 %all-gather.6.cloned.1.call-start = ((), (), s32[]{:S(2)}) async-start(), calls=%async_computation | async-start | bytes 1769472 | tf_op jit(solution)/shard_map/all_gather | solution.py:504
  367.3 35.5 %collective-permute-start.21 = (bf16[256,1536]{1,0:T(8,128)(2,1)S(1)}, bf16[256,1536]{1,0:T(8,128)(2,1)S(1)}, u32[]{:S(2)}, u32[]{:S(2)}) collective-permute-start(bf16[256,1536]{1,0:T(8,128)(2,1)S(1)} %pad_maximum_fusion.6), channel_id=1, source_target_pairs={{0,8},{4,12},{8,0},{12,4},{16,24},{20,28},{24,16},{28,20},{1,9},{5... | collective-permute-start | bytes 2359304 | tf_op jit(solution)/shard_map/ppermute | solution.py:57
  368.7 34.1 %copy-start.31 = (bf16[256,1536]{1,0:T(8,128)(2,1)S(1)}, bf16[256,1536]{1,0:T(8,128)(2,1)}, u32[]{:S(2)}) copy-start(bf16[256,1536]{1,0:T(8,128)(2,1)} %copy-done.30) | copy-start | bytes 2359300
  368.7 34.0 %collective-permute-start.25 = (bf16[128,1536]{1,0:T(8,128)(2,1)S(1)}, bf16[128,1536]{1,0:T(8,128)(2,1)S(1)}, u32[]{:S(2)}, u32[]{:S(2)}) collective-permute-start(bf16[128,1536]{1,0:T(8,128)(2,1)S(1)} %get-tuple-element.126), channel_id=1, source_target_pairs={{0,8},{4,12},{8,0},{12,4},{16,24},{20,28},{24,16},{28,20},{1,9},{5... | collective-permute-start | bytes 1179656 | tf_op jit(solution)/shard_map/ppermute | solution.py:57
  404.4 9.3 %collective-permute-start.22 = (bf16[128,1536]{1,0:T(8,128)(2,1)S(1)}, bf16[128,1536]{1,0:T(8,128)(2,1)S(1)}, u32[]{:S(2)}, u32[]{:S(2)}) collective-permute-start(bf16[128,1536]{1,0:T(8,128)(2,1)S(1)} %get-tuple-element.125), channel_id=1, source_target_pairs={{0,16},{4,20},{8,24},{12,28},{16,0},{20,4},{24,8},{28,12},{1,17},{... | collective-permute-start | bytes 1179656 | tf_op jit(solution)/shard_map/ppermute | solution.py:57
  405.4 11.7 %collective-permute-start.27 = (bf16[128,768]{1,0:T(8,128)(2,1)S(1)}, bf16[128,768]{1,0:T(8,128)(2,1)S(1)}, u32[]{:S(2)}, u32[]{:S(2)}) collective-permute-start(bf16[128,768]{1,0:T(8,128)(2,1)S(1)} %get-tuple-element.156), channel_id=1, source_target_pairs={{0,3},{1,2},{2,1},{3,0},{4,7},{5,6},{6,5},{7,4},{8,11},{9,10},{10,... | collective-permute-start | bytes 589832 | tf_op jit(solution)/shard_map/ppermute | solution.py:61
  410.1 15.0 %collective-permute-start.26 = (bf16[128,768]{1,0:T(8,128)(2,1)S(1)}, bf16[128,768]{1,0:T(8,128)(2,1)S(1)}, u32[]{:S(2)}, u32[]{:S(2)}) collective-permute-start(bf16[128,768]{1,0:T(8,128)(2,1)S(1)} %get-tuple-element.155), channel_id=1, source_target_pairs={{0,2},{1,3},{2,0},{3,1},{4,6},{5,7},{6,4},{7,5},{8,10},{9,11},{10,... | collective-permute-start | bytes 589832 | tf_op jit(solution)/shard_map/ppermute | solution.py:61
  415.0 10.1 %collective-permute-start.23 = (bf16[128,768]{1,0:T(8,128)(2,1)S(1)}, bf16[128,768]{1,0:T(8,128)(2,1)S(1)}, u32[]{:S(2)}, u32[]{:S(2)}) collective-permute-start(bf16[128,768]{1,0:T(8,128)(2,1)S(1)} %slice.1011), channel_id=1, source_target_pairs={{0,1},{1,0},{2,3},{3,2},{4,5},{5,4},{6,7},{7,6},{8,9},{9,8},{10,11... | collective-permute-start | bytes 589832 | tf_op jit(solution)/shard_map/ppermute | solution.py:61
  429.0 45.0 %collective-permute-start.32 = (bf16[512,256]{0,1:T(8,128)(2,1)S(1)}, bf16[512,256]{0,1:T(8,128)(2,1)S(1)}, u32[]{:S(2)}, u32[]{:S(2)}) collective-permute-start(bf16[512,256]{0,1:T(8,128)(2,1)S(1)} %pad_maximum_fusion.14), channel_id=1, source_target_pairs={{0,16},{4,20},{8,24},{12,28},{16,0},{20,4},{24,8},{28,12},{1,17},{... | collective-permute-start | bytes 786440 | tf_op jit(solution)/shard_map/ppermute | solution.py:57
  475.9 10.2 %collective-permute-start.29 = (bf16[512,256]{0,1:T(8,128)(2,1)S(1)}, bf16[512,256]{0,1:T(8,128)(2,1)S(1)}, u32[]{:S(2)}, u32[]{:S(2)}) collective-permute-start(bf16[512,256]{0,1:T(8,128)(2,1)S(1)} %pad_maximum_fusion.13), channel_id=1, source_target_pairs={{0,8},{4,12},{8,0},{12,4},{16,24},{20,28},{24,16},{28,20},{1,9},{5... | collective-permute-start | bytes 786440 | tf_op jit(solution)/shard_map/ppermute | solution.py:57
  478.9 7.2 %collective-permute-start.33 = (bf16[512,128]{0,1:T(8,128)(2,1)}, bf16[512,128]{0,1:T(8,128)(2,1)}, u32[]{:S(2)}, u32[]{:S(2)}) collective-permute-start(bf16[512,128]{0,1:T(8,128)(2,1)} %get-tuple-element.147), channel_id=1, source_target_pairs={{0,8},{4,12},{8,0},{12,4},{16,24},{20,28},{24,16},{28,20},{1,9},{5... | collective-permute-start | bytes 393224 | tf_op jit(solution)/shard_map/ppermute | solution.py:57
  487.2 5.0 collective-permute-start.30
  488.4 6.2 %collective-permute-start.35 = (bf16[256,128]{0,1:T(8,128)(2,1)S(1)}, bf16[256,128]{0,1:T(8,128)(2,1)S(1)}, u32[]{:S(2)}, u32[]{:S(2)}) collective-permute-start(bf16[256,128]{0,1:T(8,128)(2,1)S(1)} %get-tuple-element.158), channel_id=1, source_target_pairs={{0,3},{1,2},{2,1},{3,0},{4,7},{5,6},{6,5},{7,4},{8,11},{9,10},{10,... | collective-permute-start | bytes 196616 | tf_op jit(solution)/shard_map/ppermute | solution.py:61
  490.0 5.9 %collective-permute-start.34 = (bf16[256,128]{0,1:T(8,128)(2,1)S(1)}, bf16[256,128]{0,1:T(8,128)(2,1)S(1)}, u32[]{:S(2)}, u32[]{:S(2)}) collective-permute-start(bf16[256,128]{0,1:T(8,128)(2,1)S(1)} %get-tuple-element.157), channel_id=1, source_target_pairs={{0,2},{1,3},{2,0},{3,1},{4,6},{5,7},{6,4},{7,5},{8,10},{9,11},{10,... | collective-permute-start | bytes 196616 | tf_op jit(solution)/shard_map/ppermute | solution.py:61
  493.2 4.3 collective-permute-start.31
  (49 other events, 212.4 us)
Sparse Core Ops, SparseCore 0:
  312.3 30.9 all-gather.7
  364.5 36.1 all-gather.9
  426.0 26.3 all-gather.5

commit v2 on v0

--- a/solution.py
+++ b/solution.py
@@ -3,6 +3,8 @@
 import jax
 import jax.numpy as jnp
 from jax import lax
+from jax.experimental import pallas as pl
+from jax.experimental.pallas import tpu as pltpu
 from jax.sharding import PartitionSpec as P
 
 DH = 64
@@ -45,7 +47,987 @@
     return product * (1.0 / math.sqrt(DH))
 
 
-def local(
+BLOCK = 128
+QUARTER = 256
+X_SIDE, Y_SIDE, CORE_SIDE = 2, 4, 1
+PLANE = 8
+CHIPS = 4
+DEPTH = 4
+OWN_CORE = CHIPS
+FLAGS = CHIPS + 1
+GAIN_ONE, SHIFT_ONE, GAIN_TWO, SHIFT_TWO, SCALE_ATTN, SCALE_MLP, BIAS_OUT, BIAS_DOWN = range(8)
+VMEM_BYTES = 24 * 2**20
+
+
+def swap_plane(values, mask):
+    return lax.ppermute(values, "dp", [(i, i ^ mask) for i in range(PLANE)])
+
+
+def swap_depth(values, mask):
+    return lax.ppermute(values, "mp", [(i, i ^ mask) for i in range(DEPTH)])
+
+
+def plane_swaps(values):
+    return [swap_plane(values, side) for side in (X_SIDE, Y_SIDE, X_SIDE | Y_SIDE)]
+
+
+class Order:
+    def __init__(self):
+        self.last = None
+
+    def hold(self, values):
+        leaves, tree = jax.tree.flatten(values)
+        return jax.tree.unflatten(tree, lax.optimization_barrier(tuple(leaves) + (self.last,))[:-1])
+
+    def land(self, *arrays):
+        *arrays, self.last = lax.optimization_barrier(arrays + (self.last,))
+        return arrays
+
+    def __call__(self, step, *args):
+        leaves, tree = jax.tree.flatten(args)
+        arrays = [i for i, leaf in enumerate(leaves) if isinstance(leaf, jax.Array)]
+        if self.last is not None:
+            held = lax.optimization_barrier(tuple(leaves[i] for i in arrays) + (self.last,))
+            for i, value in zip(arrays, held):
+                leaves[i] = value
+        out = step(*jax.tree.unflatten(tree, leaves))
+        self.last = jax.tree.leaves(out)[0]
+        return out
+
+
+def dot_nt(left, right):
+    return lax.dot_general(left, right, (((1,), (1,)), ((), ())), preferred_element_type=jnp.float32)
+
+
+def dot_tn(left, right):
+    return lax.dot_general(left, right, (((0,), (0,)), ((), ())), preferred_element_type=jnp.float32)
+
+
+def dot_nn(left, right):
+    return lax.dot_general(left, right, (((1,), (0,)), ((), ())), preferred_element_type=jnp.float32)
+
+
+def add_low(*values):
+    return sum(value.astype(jnp.float32) for value in values).astype(jnp.bfloat16)
+
+
+def crop_ranges(rows):
+    ranges = []
+    for crop in range(rows // L):
+        low = crop * L // 16 * 16
+        high = min((crop + 1) * L + 15, rows + 15) // 16 * 16
+        ranges.append((low, min(high, rows), crop * L - low))
+    return ranges
+
+
+def whole(array):
+    zeros = (0,) * array.ndim
+    return pl.BlockSpec(array.shape, lambda *_: zeros)
+
+
+def kernel_call(body, name, meta, args, in_specs, out_shape, out_specs, grid=(1,), scratch=(), flops=1000):
+    return pl.pallas_call(
+        body,
+        grid_spec=pltpu.PrefetchScalarGridSpec(
+            num_scalar_prefetch=1,
+            grid=grid,
+            in_specs=in_specs,
+            out_specs=out_specs,
+            scratch_shapes=list(scratch),
+        ),
+        out_shape=out_shape,
+        compiler_params=pltpu.CompilerParams(vmem_limit_bytes=VMEM_BYTES),
+        cost_estimate=pl.CostEstimate(flops=flops, bytes_accessed=1000, transcendentals=0),
+        name=name,
+    )(meta, *args)
+
+
+def shape_of(*dims, dtype=jnp.bfloat16):
+    return jax.ShapeDtypeStruct(dims, dtype)
+
+
+def normalized(values):
+    centered = values - jnp.mean(values, axis=-1, keepdims=True)
+    inverse = lax.rsqrt(jnp.mean(centered * centered, axis=-1, keepdims=True) + 1e-06)
+    return centered * inverse, inverse
+
+
+def norm_gradient(unit, inverse, gain, grad):
+    wide = grad * gain
+    return inverse * (
+        wide - jnp.mean(wide, axis=-1, keepdims=True) - unit * jnp.mean(wide * unit, axis=-1, keepdims=True)
+    )
+
+
+def valid_column(meta_ref, rows):
+    row = lax.broadcasted_iota(jnp.int32, (rows, 1), 0)
+    valid = jnp.zeros((rows, 1), jnp.float32)
+    for crop in range(rows // L):
+        inside = (row >= crop * L) & (row < (crop + 1) * L)
+        valid = jnp.where(inside, meta_ref[FLAGS + crop].astype(jnp.float32), valid)
+    return valid
+
+
+def quarter_of(meta_ref, side):
+    return pl.ds(pl.multiple_of(meta_ref[side] * QUARTER, QUARTER), QUARTER)
+
+
+def slice_weights(meta, w_query, w_key, w_value, w_out, w_up, w_down, biases):
+    half_h, half_u = w_query.shape[1] // 2, w_up.shape[1] // 2
+    n_h, n_u = half_h // BLOCK, half_u // BLOCK
+
+    def body(meta_ref, q_ref, k_ref, v_ref, o_ref, up_ref, down_ref, bias_ref, attn_ref, rest_ref):
+        core = meta_ref[OWN_CORE]
+        for which, ref in enumerate((q_ref, k_ref, v_ref)):
+            attn_ref[which * QUARTER : (which + 1) * QUARTER, :] = ref[...]
+        for b in range(2):
+            row = 3 * QUARTER + b * half_h
+            attn_ref[row : row + half_h, :] = o_ref[:, b * BLOCK : (b + 1) * BLOCK]
+        picked = jnp.concatenate(
+            [
+                bias_ref[pl.ds(core, n_h), :],
+                bias_ref[pl.ds(2 * n_h + core, n_h), :],
+                bias_ref[pl.ds(4 * n_h + n_u * core, n_u), :],
+            ],
+            axis=0,
+        )
+        high = picked.astype(jnp.bfloat16)
+        low = (picked - high.astype(jnp.float32)).astype(jnp.bfloat16)
+        spare = jnp.zeros((16 - 2 * picked.shape[0], BLOCK), jnp.bfloat16)
+        attn_ref[4 * QUARTER :, :] = jnp.concatenate([high, low, spare], axis=0)
+        for b in range(n_u):
+            rest_ref[b * QUARTER : (b + 1) * QUARTER, :] = up_ref[:, b * BLOCK : (b + 1) * BLOCK]
+        for b in range(2):
+            row = n_u * QUARTER + b * half_u
+            rest_ref[row : row + half_u, :] = down_ref[:, b * BLOCK : (b + 1) * BLOCK]
+
+    args = (w_query, w_key, w_value, w_out, w_up, w_down, biases)
+    out = [shape_of(4 * QUARTER + 16, BLOCK), shape_of(2 * n_u * QUARTER, BLOCK)]
+    return kernel_call(
+        body,
+        "slice_weights",
+        meta,
+        args,
+        [pl.BlockSpec((QUARTER, half_h), lambda i, m: (m[0], m[OWN_CORE]))] * 3
+        + [
+            pl.BlockSpec((half_h, QUARTER), lambda i, m: (m[OWN_CORE], m[0])),
+            pl.BlockSpec((QUARTER, half_u), lambda i, m: (m[0], m[OWN_CORE])),
+            pl.BlockSpec((half_u, QUARTER), lambda i, m: (m[OWN_CORE], m[0])),
+            whole(biases),
+        ],
+        out,
+        [whole(o) for o in out],
+    )
+
+
+def turn_into(meta_ref, values, turned_ref, index=None):
+    for side in range(CHIPS):
+        rows = slice(side * QUARTER, (side + 1) * QUARTER)
+        if index is None:
+            turned_ref[rows, :] = values[:, quarter_of(meta_ref, side)].T
+        else:
+            turned_ref[rows, :] = values[index, :, quarter_of(meta_ref, side)].T
+
+
+def turn(meta, *arrays):
+    def body(meta_ref, *refs):
+        for source, target in zip(refs[: len(arrays)], refs[len(arrays) :]):
+            turn_into(meta_ref, source, target)
+
+    out = [shape_of(*a.shape[::-1]) for a in arrays]
+    return kernel_call(body, "turn", meta, arrays, [whole(a) for a in arrays], out, [whole(o) for o in out])
+
+
+def prepare(meta, tokens, tokens_other, cotangent, vectors):
+    rows, width = tokens.shape
+
+    def body(meta_ref, tokens_ref, other_ref, cot_ref, vec_ref, one_ref, two_ref, grad_ref, sum_ref, *turned):
+        for source, target in ((tokens_ref, one_ref), (other_ref, two_ref)):
+            unit, _ = normalized(source[...].astype(jnp.float32))
+            target[...] = (unit * vec_ref[GAIN_ONE : GAIN_ONE + 1] + vec_ref[SHIFT_ONE : SHIFT_ONE + 1]).astype(
+                jnp.bfloat16
+            )
+        grad = vec_ref[SCALE_MLP : SCALE_MLP + 1] * (valid_column(meta_ref, rows) * cot_ref[...].astype(jnp.float32))
+        sum_ref[...] = jnp.sum(grad, axis=0, keepdims=True)
+        grad_ref[...] = grad.astype(jnp.bfloat16)
+        for source, target in zip((one_ref, two_ref, grad_ref), turned):
+            turn_into(meta_ref, source, target)
+
+    args = (tokens, tokens_other, cotangent, vectors)
+    out = [shape_of(rows, width)] * 3 + [shape_of(1, width, dtype=jnp.float32)] + [shape_of(width, rows)] * 3
+    return kernel_call(body, "prepare", meta, args, [whole(a) for a in args], out, [whole(o) for o in out])
+
+
+def fill_heads(meta_ref, chip_refs, weight_ref):
+    for side, ref in enumerate(chip_refs):
+        at = quarter_of(meta_ref, side)
+        for which in range(3):
+            weight_ref[at, which * BLOCK : (which + 1) * BLOCK] = ref[which * QUARTER : (which + 1) * QUARTER, :]
+
+
+def head_specs(width, chips):
+    own = [pl.BlockSpec((width, BLOCK), lambda g, m: (0, m[OWN_CORE]))] * 3
+    far = [pl.BlockSpec((3 * QUARTER, BLOCK), lambda g, m: (jnp.maximum(g - 1, 0), 0))] * len(chips)
+    return own, far
+
+
+def attention_forward(meta, normed, other, w_query, w_key, w_value, biases, level_attn, chips):
+    rows, width = normed.shape
+    group = 3 * BLOCK
+    ranges = crop_ranges(rows)
+    span = max(high - low for low, high, _ in ranges)
+    scale = 1.0 / math.sqrt(DH)
+    count = (level_attn[0].shape[0] - 4 * QUARTER - 4) // 2
+
+    def body(meta_ref, normed_ref, other_ref, q_ref, k_ref, v_ref, bias_ref, one_ref, two_ref, three_ref, *refs):
+        chip_refs, (qkv_ref, out_ref, prob_ref, weight_ref, sum_ref) = refs[:CHIPS], refs[CHIPS:]
+        step = pl.program_id(0)
+        core = meta_ref[OWN_CORE]
+
+        @pl.when(step == 0)
+        def _():
+            for which, ref in enumerate((q_ref, k_ref, v_ref)):
+                weight_ref[:, which * BLOCK : (which + 1) * BLOCK] = ref[...]
+            sum_ref[0:1, :] = bias_ref[pl.ds(core, 1), :]
+            sum_ref[1:2, :] = bias_ref[pl.ds(2 + core, 1), :]
+
+        for index, ref in enumerate((one_ref, two_ref, three_ref)):
+            @pl.when(step == index + 1)
+            def _():
+                both = ref[...].astype(jnp.float32)
+                sum_ref[0:2, :] = both[0:2] + both[count : count + 2]
+
+        @pl.when(step > 0)
+        def _():
+            fill_heads(meta_ref, chip_refs, weight_ref)
+
+        bias = jnp.concatenate([sum_ref[0:1, :], jnp.zeros((1, BLOCK), jnp.float32), sum_ref[1:2, :]], axis=1)
+        for part, rows_ref in enumerate((normed_ref, other_ref)):
+            qkv_ref[part] = (dot_nn(rows_ref[...], weight_ref[...]) + bias).astype(jnp.bfloat16)
+        for part in range(2):
+            for index, (low, high, skip) in enumerate(ranges):
+                size = high - low
+                query = qkv_ref[part, low:high, 0:BLOCK]
+                key = qkv_ref[part, low:high, BLOCK : 2 * BLOCK]
+                value = qkv_ref[part, low:high, 2 * BLOCK : 3 * BLOCK]
+                lane = lax.broadcasted_iota(jnp.int32, (size, BLOCK), 1)
+                row = lax.broadcasted_iota(jnp.int32, (size, size), 0)
+                column = lax.broadcasted_iota(jnp.int32, (size, size), 1)
+                seen = (column >= skip) & (column < skip + L)
+                inside = seen & (row >= skip) & (row < skip + L)
+                parts = []
+                for head in range(2):
+                    own = (lane < DH) if head == 0 else (lane >= DH)
+                    scores = dot_nt(jnp.where(own, query, jnp.zeros_like(query)), key) * scale
+                    scores = jnp.where(seen, scores, -1e30)
+                    top = jnp.max(scores, axis=1, keepdims=True)
+                    raised = jnp.exp(scores - top)
+                    total = jnp.sum(raised, axis=1, keepdims=True)
+                    probs = jnp.where(inside, raised * (1.0 / total), 0.0).astype(jnp.bfloat16)
+                    prob_ref[0, part, index, head, 0:size, 0:size] = probs
+                    parts.append(dot_nn(probs, value))
+                mixed = jnp.where(lane < DH, parts[0], parts[1]).astype(jnp.bfloat16)
+                if skip:
+                    edge = lax.broadcasted_iota(jnp.int32, (size, BLOCK), 0) >= skip
+                    mixed = jnp.where(edge, mixed, out_ref[part, low:high, :])
+                out_ref[part, low:high, :] = mixed
+
+    prob_shape = (DEPTH, 2, len(ranges), 2, span, span)
+    own_specs, far_specs = head_specs(width, chips)
+    tail = 4 * QUARTER // 16
+    args = (normed, other, w_query, w_key, w_value, biases) + tuple(level_attn) + tuple(chips)
+    return kernel_call(
+        body,
+        "attention_forward",
+        meta,
+        args,
+        [whole(normed), whole(other)] + own_specs + [whole(biases)] + [pl.BlockSpec((16, BLOCK), lambda g, m: (tail, 0))] * 3 + far_specs,
+        [shape_of(2, rows, DEPTH * group), shape_of(2, rows, DEPTH * BLOCK), shape_of(*prob_shape)],
+        [
+            pl.BlockSpec((2, rows, group), lambda g, m: (0, 0, g)),
+            pl.BlockSpec((2, rows, BLOCK), lambda g, m: (0, 0, g)),
+            pl.BlockSpec((1,) + prob_shape[1:], lambda g, m: (g, 0, 0, 0, 0, 0)),
+        ],
+        grid=(DEPTH,),
+        scratch=[pltpu.VMEM((width, group), jnp.bfloat16), pltpu.VMEM((8, BLOCK), jnp.float32)],
+    )
+
+
+def attention_out(meta, attended, w_out, chips):
+    rows, width = attended.shape[1], w_out.shape[1]
+
+    def body(meta_ref, attended_ref, own_ref, *refs):
+        chip_refs, (near_ref, low_ref, high_ref, weight_ref) = refs[:CHIPS], refs[CHIPS:]
+        weight_ref[0:BLOCK, :] = own_ref[...]
+        for side, ref in enumerate(chip_refs):
+            start = pl.multiple_of(meta_ref[side] * QUARTER, QUARTER)
+            for index in range(DEPTH - 1):
+                for b in range(2):
+                    weight_ref[(index + 1) * BLOCK : (index + 2) * BLOCK, pl.ds(start + b * BLOCK, BLOCK)] = ref[
+                        index, b * BLOCK : (b + 1) * BLOCK, :
+                    ]
+        near_ref[...] = dot_nn(attended_ref[0], weight_ref[...])
+        across = dot_nn(attended_ref[1], weight_ref[...]).astype(jnp.bfloat16)
+        low_ref[...] = across[:, : width // 2]
+        high_ref[...] = across[:, width // 2 :]
+
+    views = tuple(chip.reshape(DEPTH - 1, QUARTER, BLOCK) for chip in chips)
+    view_spec = whole(views[0])
+    out = [shape_of(rows, width, dtype=jnp.float32)] + [shape_of(rows, width // 2)] * 2
+    return kernel_call(
+        body, "attention_out", meta, (attended, w_out) + views,
+        [whole(attended), pl.BlockSpec((BLOCK, width), lambda i, m: (m[OWN_CORE], 0))] + [view_spec] * CHIPS,
+        out, [whole(o) for o in out], scratch=[pltpu.VMEM((DEPTH * BLOCK, width), jnp.bfloat16)],
+    )
+
+
+def attention_norm(meta, near, low, high, tokens, vectors):
+    rows, width = tokens.shape
+
+    def body(meta_ref, near_ref, low_ref, high_ref, tokens_ref, vec_ref, hidden_ref, branch_ref, normed_ref):
+        got = jnp.concatenate([low_ref[...], high_ref[...]], axis=1).astype(jnp.float32)
+        branch = near_ref[...] + got + vec_ref[BIAS_OUT : BIAS_OUT + 1]
+        branch_ref[...] = branch
+        hidden = tokens_ref[...].astype(jnp.float32) + vec_ref[SCALE_ATTN : SCALE_ATTN + 1] * branch
+        hidden_ref[...] = hidden
+        unit, _ = normalized(hidden)
+        normed_ref[...] = (unit * vec_ref[GAIN_TWO : GAIN_TWO + 1] + vec_ref[SHIFT_TWO : SHIFT_TWO + 1]).astype(
+            jnp.bfloat16
+        )
+
+    args = (near, low, high, tokens, vectors)
+    out = [shape_of(rows, width, dtype=jnp.float32)] * 2 + [shape_of(rows, width)]
+    return kernel_call(body, "attention_norm", meta, args, [whole(a) for a in args], out, [whole(o) for o in out])
+
+
+def fill_units(meta_ref, chip_refs, up_weight, down_weight):
+    half_u = down_weight.shape[0]
+    n_u = half_u // BLOCK
+    for side, ref in enumerate(chip_refs):
+        at = quarter_of(meta_ref, side)
+        start = pl.multiple_of(meta_ref[side] * QUARTER, QUARTER)
+        for b in range(n_u):
+            up_weight[at, b * BLOCK : (b + 1) * BLOCK] = ref[b * QUARTER : (b + 1) * QUARTER, :]
+        base = n_u * QUARTER
+        for b in range(2):
+            down_weight[:, pl.ds(start + b * BLOCK, BLOCK)] = ref[base + b * half_u : base + (b + 1) * half_u, :]
+
+
+def feed_forward(meta, normed, grads, w_up, w_down, bias_up, chips, flops=1000):
+    rows, width = normed[0].shape
+    half_u = w_up.shape[1] // 2
+    count = len(normed)
+
+    def body(meta_ref, *refs):
+        normed_refs, grad_refs, refs = refs[:count], refs[count : 2 * count], refs[2 * count :]
+        up_ref, down_ref, bias_ref = refs[:3]
+        chip_refs, refs = refs[3 : 3 + CHIPS], refs[3 + CHIPS :]
+        act_refs, gup_refs, back_refs, refs = refs[:count], refs[count : 2 * count], refs[2 * count : 3 * count], refs[3 * count :]
+        sum_ref, up_weight, down_weight, total_ref = refs
+        step = pl.program_id(0)
+
+        @pl.when(step == 0)
+        def _():
+            up_weight[...] = up_ref[...]
+            down_weight[...] = down_ref[...]
+
+        @pl.when(step == 1)
+        def _():
+            fill_units(meta_ref, chip_refs, up_weight, down_weight)
+
+        sums = jnp.zeros(sum_ref.shape, jnp.float32)
+        for part in range(count):
+            pre = dot_nn(normed_refs[part][...], up_weight[...]) + bias_ref[...]
+            spread = 0.5 * (1.0 + lax.erf(pre * (1.0 / math.sqrt(2.0))))
+            act_refs[part][...] = (pre * spread).astype(jnp.bfloat16)
+            slope = spread + pre * jnp.exp(-0.5 * pre * pre) * (1.0 / math.sqrt(2.0 * math.pi))
+            grad_up = (dot_nt(grad_refs[part][...], down_weight[...]) * slope).astype(jnp.bfloat16)
+            gup_refs[part][...] = grad_up
+            sums = sums + jnp.sum(grad_up.astype(jnp.float32), axis=0, keepdims=True)
+            back = dot_nt(grad_up, up_weight[...])
+
+            @pl.when(step == 0)
+            def _():
+                total_ref[part] = back
+
+            @pl.when(step == 1)
+            def _():
+                back_refs[part][...] = (total_ref[part] + back).astype(jnp.bfloat16)
+
+        sum_ref[...] = sums
+
+    args = tuple(normed) + tuple(grads)
+    chip_spec = whole(chips[0])
+    by_unit = pl.BlockSpec((rows, half_u), lambda g, m: (0, g))
+    outs = kernel_call(
+        body,
+        "feed_forward",
+        meta,
+        args + (w_up, w_down, bias_up) + tuple(chips),
+        [whole(a) for a in args]
+        + [
+            pl.BlockSpec((width, half_u), lambda g, m: (0, m[OWN_CORE])),
+            pl.BlockSpec((half_u, width), lambda g, m: (m[OWN_CORE], 0)),
+            pl.BlockSpec((1, half_u), lambda g, m: (0, g)),
+        ]
+        + [chip_spec] * CHIPS,
+        [shape_of(rows, 2 * half_u)] * (2 * count)
+        + [shape_of(rows, width)] * count
+        + [shape_of(1, 2 * half_u, dtype=jnp.float32)],
+        [by_unit] * (2 * count)
+        + [pl.BlockSpec((rows, width), lambda g, m: (0, 0))] * count
+        + [pl.BlockSpec((1, half_u), lambda g, m: (0, g))],
+        grid=(2,),
+        scratch=[
+            pltpu.VMEM((width, half_u), jnp.bfloat16),
+            pltpu.VMEM((half_u, width), jnp.bfloat16),
+            pltpu.VMEM((count, rows, width), jnp.float32),
+        ],
+        flops=flops,
+    )
+    return outs[:count], outs[count : 2 * count], outs[2 * count : 3 * count], outs[3 * count]
+
+
+def feed_down(meta, acts, w_down, chips):
+    rows = acts[0].shape[0]
+    half_u, width = w_down.shape[0] // 2, w_down.shape[1]
+    count = len(acts)
+
+    def body(meta_ref, *refs):
+        act_refs, down_ref, refs = refs[:count], refs[count], refs[count + 1 :]
+        chip_refs, out_refs, weight_ref = refs[:CHIPS], refs[CHIPS:-1], refs[-1]
+        weight_ref[0:half_u, :] = down_ref[...]
+        for side, ref in enumerate(chip_refs):
+            start = pl.multiple_of(meta_ref[side] * QUARTER, QUARTER)
+            for b in range(2):
+                weight_ref[half_u:, pl.ds(start + b * BLOCK, BLOCK)] = ref[b * half_u : (b + 1) * half_u, :]
+        for act_ref, out_ref in zip(act_refs, out_refs):
+            out_ref[...] = dot_nn(act_ref[...], weight_ref[...]).astype(jnp.bfloat16)
+
+    out = [shape_of(rows, width)] * count
+    return kernel_call(
+        body, "feed_down", meta, tuple(acts) + (w_down,) + tuple(chips),
+        [whole(a) for a in acts]
+        + [pl.BlockSpec((half_u, width), lambda i, m: (m[OWN_CORE], 0))]
+        + [pl.BlockSpec((2 * half_u, BLOCK), lambda i, m: (1, 0))] * CHIPS,
+        out, [whole(o) for o in out], scratch=[pltpu.VMEM((2 * half_u, width), jnp.bfloat16)],
+    )
+
+
+def put_sides(lane, values, keep_ref, send_ref, at):
+    keep, send = ((0, 2), (1, 3)) if lane == 0 else ((0, 1), (2, 3))
+    for ref, sides in ((keep_ref, keep), (send_ref, send)):
+        for index, side in enumerate(sides):
+            ref[index * QUARTER : (index + 1) * QUARTER, at] = values[side * QUARTER : (side + 1) * QUARTER].astype(
+                jnp.bfloat16
+            )
+
+
+def feed_gradients(meta, normed, turned_grads, gups, acts):
+    rows, width = normed[0].shape
+    half_u = gups[0].shape[1] // 2
+
+    def body(meta_ref, *refs):
+        normed_refs, turned_refs, refs = refs[:4], refs[4:8], refs[8:]
+        n = len(gups)
+        gup_refs, act_refs, refs = refs[:n], refs[n : 2 * n], refs[2 * n :]
+        outs, own_turned = refs[:4], refs[4:]
+        step = pl.program_id(0)
+
+        @pl.when(step == 0)
+        def _():
+            for source, target in zip(normed_refs, own_turned):
+                turn_into(meta_ref, source, target)
+
+        def product(lefts, rights):
+            return sum(dot_nn(left[...], right[...]) for left, right in zip(lefts, rights))
+
+        for lane in range(2):
+            @pl.when(step == 2 * lane)
+            def _():
+                put_sides(lane, product(own_turned, gup_refs), outs[2 * lane], outs[2 * lane + 1], slice(None))
+
+            @pl.when(step == 2 * lane + 1)
+            def _():
+                put_sides(lane, product(turned_refs, act_refs), outs[2 * lane], outs[2 * lane + 1], slice(None))
+
+    args = tuple(normed) + tuple(turned_grads)
+    out = [shape_of(width // 2, 2 * half_u)] * 4
+    by_lane = [pl.BlockSpec((rows, half_u), lambda g, m: (0, g >> 1))] * len(gups)
+    out_specs = [pl.BlockSpec((width // 2, half_u), lambda g, m: (0, jnp.minimum(g, 1)))] * 2
+    out_specs += [pl.BlockSpec((width // 2, half_u), lambda g, m: (0, jnp.maximum(g - 2, 0)))] * 2
+    return kernel_call(
+        body, "feed_gradients", meta, args + tuple(gups) + tuple(acts),
+        [whole(a) for a in args] + by_lane * 2, out, out_specs, grid=(4,),
+        scratch=[pltpu.VMEM((width, rows), jnp.bfloat16)] * 4,
+    )
+
+
+def hidden_gradient(meta, backs, hidden, branch, cotangent, vectors):
+    rows, width = hidden.shape
+
+    def body(meta_ref, *refs):
+        back_refs, (hidden_ref, branch_ref, cot_ref, vec_ref, dh_ref, e1_ref, sum_ref) = refs[: len(backs)], refs[len(backs) :]
+        grad = sum(ref[...].astype(jnp.float32) for ref in back_refs)
+        unit, inverse = normalized(hidden_ref[...])
+        sum_ref[0:1, :] = jnp.sum(grad * unit, axis=0, keepdims=True)
+        sum_ref[1:2, :] = jnp.sum(grad, axis=0, keepdims=True)
+        total = valid_column(meta_ref, rows) * cot_ref[...].astype(jnp.float32) + norm_gradient(
+            unit, inverse, vec_ref[GAIN_TWO : GAIN_TWO + 1], grad
+        )
+        dh_ref[...] = total
+        sum_ref[2:3, :] = jnp.sum(total * branch_ref[...], axis=0, keepdims=True)
+        scaled = vec_ref[SCALE_ATTN : SCALE_ATTN + 1] * total
+        sum_ref[3:4, :] = jnp.sum(scaled, axis=0, keepdims=True)
+        e1_ref[...] = scaled.astype(jnp.bfloat16)
+
+    args = tuple(backs) + (hidden, branch, cotangent, vectors)
+    out = [shape_of(rows, width, dtype=jnp.float32), shape_of(rows, width), shape_of(4, width, dtype=jnp.float32)]
+    return kernel_call(body, "hidden_gradient", meta, args, [whole(a) for a in args], out, [whole(o) for o in out])
+
+
+def attention_backward(meta, qkv, probs, attended, grads, turned_normed, w_out, chips, lane):
+    rows, width = grads[0].shape
+    group = 3 * BLOCK
+    ranges = crop_ranges(rows)
+    groups = DEPTH // 2
+    scale = 1.0 / math.sqrt(DH)
+    base = lane * groups
+
+    def body(meta_ref, qkv_ref, prob_ref, mixed_ref, e1_ref, e1_other_ref, n_ref, n_other_ref, own_ref, *refs):
+        chip_refs, (out_ref, keep_ref, send_ref, weight_ref, grad_ref, turned_e, turned_other) = refs[:CHIPS], refs[CHIPS:]
+        step = pl.program_id(0)
+
+        @pl.when(step == 0)
+        def _():
+            turn_into(meta_ref, e1_ref, turned_e)
+            turn_into(meta_ref, e1_other_ref, turned_other)
+
+        def far_weights():
+            for side, ref in enumerate(chip_refs):
+                start = pl.multiple_of(meta_ref[side] * QUARTER, QUARTER)
+                for b in range(2):
+                    weight_ref[:, pl.ds(start + b * BLOCK, BLOCK)] = ref[0, b * BLOCK : (b + 1) * BLOCK, :]
+
+        if lane == 0:
+            @pl.when(step == 0)
+            def _():
+                weight_ref[...] = own_ref[...]
+
+            pl.when(step > 0)(far_weights)
+        else:
+            far_weights()
+        for part, ref in enumerate((e1_ref, e1_other_ref)):
+            grad_ref[part] = dot_nt(ref[...], weight_ref[...]).astype(jnp.bfloat16)
+        for part in range(2):
+            for index, (low, high, skip) in enumerate(ranges):
+                size = high - low
+                query = qkv_ref[part, low:high, 0:BLOCK]
+                key = qkv_ref[part, low:high, BLOCK : 2 * BLOCK]
+                value = qkv_ref[part, low:high, 2 * BLOCK : 3 * BLOCK]
+                grad = grad_ref[part, low:high, :]
+                lane_of = lax.broadcasted_iota(jnp.int32, (size, BLOCK), 1)
+                row = lax.broadcasted_iota(jnp.int32, (size, BLOCK), 0)
+                parts = []
+                for head in range(2):
+                    own = (lane_of < DH) if head == 0 else (lane_of >= DH)
+                    low_probs = prob_ref[0, part, index, head, 0:size, 0:size]
+                    grad_value = dot_tn(low_probs, grad)
+                    grad_probs = dot_nt(jnp.where(own, grad, jnp.zeros_like(grad)), value)
+                    wide = low_probs.astype(jnp.float32)
+                    weighted = wide * grad_probs
+                    inner = jnp.sum(weighted, axis=1, keepdims=True)
+                    grad_scores = (weighted - wide * inner).astype(jnp.bfloat16)
+                    parts.append(
+                        (dot_nn(grad_scores, key) * scale, dot_tn(grad_scores, query) * scale, grad_value)
+                    )
+                for which in range(3):
+                    at = slice(which * BLOCK, (which + 1) * BLOCK)
+                    joined = jnp.where(lane_of < DH, parts[0][which], parts[1][which]).astype(jnp.bfloat16)
+                    if skip:
+                        joined = jnp.where(row >= skip, joined, out_ref[part, low:high, at])
+                    out_ref[part, low:high, at] = joined
+        both = dot_nn(n_ref[...], out_ref[0]) + dot_nn(n_other_ref[...], out_ref[1])
+        put_sides(lane, both, keep_ref, send_ref, slice(0, group))
+        both = dot_nn(turned_e[...], mixed_ref[0]) + dot_nn(turned_other[...], mixed_ref[1])
+        put_sides(lane, both, keep_ref, send_ref, slice(group, group + BLOCK))
+
+    views = tuple(chip.reshape(DEPTH - 1, QUARTER, BLOCK) for chip in chips)
+    args = (qkv, probs, attended) + tuple(grads) + tuple(turned_normed) + (w_out,) + views
+    return kernel_call(
+        body,
+        "attention_backward",
+        meta,
+        args,
+        [
+            pl.BlockSpec((2, rows, group), lambda g, m: (0, 0, base + g)),
+            pl.BlockSpec((1,) + probs.shape[1:], lambda g, m: (base + g, 0, 0, 0, 0, 0)),
+            pl.BlockSpec((2, rows, BLOCK), lambda g, m: (0, 0, base + g)),
+            whole(grads[0]),
+            whole(grads[1]),
+            whole(turned_normed[0]),
+            whole(turned_normed[1]),
+            pl.BlockSpec((BLOCK, width), lambda g, m: (m[OWN_CORE], 0)),
+        ]
+        + [pl.BlockSpec((1, QUARTER, BLOCK), lambda g, m: (jnp.maximum(base + g - 1, 0), 0, 0))] * CHIPS,
+        [shape_of(2, rows, groups * group)] + [shape_of(width // 2, groups * 4 * BLOCK)] * 2,
+        [pl.BlockSpec((2, rows, group), lambda g, m: (0, 0, g))]
+        + [pl.BlockSpec((width // 2, 4 * BLOCK), lambda g, m: (0, g))] * 2,
+        grid=(groups,),
+        scratch=[
+            pltpu.VMEM((BLOCK, width), jnp.bfloat16),
+            pltpu.VMEM((2, rows, BLOCK), jnp.bfloat16),
+            pltpu.VMEM((width, rows), jnp.bfloat16),
+            pltpu.VMEM((width, rows), jnp.bfloat16),
+        ],
+    )
+
+
+def token_shares(meta, grads, w_query, w_key, w_value, chips):
+    rows = grads[0].shape[1]
+    width = w_query.shape[0]
+    group = 3 * BLOCK
+
+    def body(meta_ref, low_ref, high_ref, q_ref, k_ref, v_ref, *refs):
+        chip_refs, (near_ref, across_ref, bias_ref, weight_ref, total_ref) = refs[:CHIPS], refs[CHIPS:]
+        step = pl.program_id(0)
+
+        @pl.when(step == 0)
+        def _():
+            for which, ref in enumerate((q_ref, k_ref, v_ref)):
+                weight_ref[:, which * BLOCK : (which + 1) * BLOCK] = ref[...]
+
+        @pl.when(step > 0)
+        def _():
+            fill_heads(meta_ref, chip_refs, weight_ref)
+
+        def add(ref):
+            sums = jnp.sum(ref[0].astype(jnp.float32), axis=0, keepdims=True)
+            bias_ref[0] = sums + jnp.sum(ref[1].astype(jnp.float32), axis=0, keepdims=True)
+            for part in range(2):
+                share = dot_nt(ref[part], weight_ref[...])
+
+                @pl.when(step == 0)
+                def _():
+                    total_ref[part] = share
+
+                @pl.when(step > 0)
+                def _():
+                    total_ref[part] += share
+
+        pl.when(step < 2)(lambda: add(low_ref))
+        pl.when(step >= 2)(lambda: add(high_ref))
+
+        @pl.when(step == DEPTH - 1)
+        def _():
+            near_ref[...] = total_ref[0]
+            across_ref[...] = total_ref[1].astype(jnp.bfloat16)
+
+    own_specs, far_specs = head_specs(width, chips)
+    out = [shape_of(rows, width, dtype=jnp.float32), shape_of(rows, width)]
+    return kernel_call(
+        body,
+        "token_shares",
+        meta,
+        tuple(grads) + (w_query, w_key, w_value) + tuple(chips),
+        [
+            pl.BlockSpec((2, rows, group), lambda g, m: (0, 0, jnp.minimum(g, 1))),
+            pl.BlockSpec((2, rows, group), lambda g, m: (0, 0, jnp.maximum(g - 2, 0))),
+        ]
+        + own_specs
+        + far_specs,
+        out + [shape_of(DEPTH, 1, group, dtype=jnp.float32)],
+        [whole(o) for o in out] + [pl.BlockSpec((1, 1, group), lambda g, m: (g, 0, 0))],
+        grid=(DEPTH,),
+        scratch=[pltpu.VMEM((width, group), jnp.bfloat16), pltpu.VMEM((2, rows, width), jnp.float32)],
+    )
+
+
+def token_gradient(meta, near, got, tokens, dh, vectors):
+    rows, width = tokens.shape
+
+    def body(meta_ref, near_ref, got_ref, tokens_ref, dh_ref, vec_ref, out_ref, sum_ref):
+        grad = near_ref[...] + got_ref[...].astype(jnp.float32)
+        unit, inverse = normalized(tokens_ref[...].astype(jnp.float32))
+        sum_ref[0:1, :] = jnp.sum(grad * unit, axis=0, keepdims=True)
+        sum_ref[1:2, :] = jnp.sum(grad, axis=0, keepdims=True)
+        out_ref[...] = dh_ref[...] + norm_gradient(unit, inverse, vec_ref[GAIN_ONE : GAIN_ONE + 1], grad)
+
+    args = (near, got, tokens, dh, vectors)
+    out = [shape_of(rows, width, dtype=jnp.float32), shape_of(2, width, dtype=jnp.float32)]
+    return kernel_call(body, "token_gradient", meta, args, [whole(a) for a in args], out, [whole(o) for o in out])
+
+
+def layer_result(meta, downs, hidden, cotangent, vectors):
+    rows, width = hidden.shape
+
+    def body(meta_ref, *refs):
+        down_refs, (hidden_ref, cot_ref, vec_ref, out_ref, sum_ref) = refs[: len(downs)], refs[len(downs) :]
+        branch = sum(ref[...].astype(jnp.float32) for ref in down_refs) + vec_ref[BIAS_DOWN : BIAS_DOWN + 1]
+        valid = valid_column(meta_ref, rows)
+        out_ref[...] = valid * (hidden_ref[...] + vec_ref[SCALE_MLP : SCALE_MLP + 1] * branch)
+        sum_ref[...] = jnp.sum(valid * cot_ref[...].astype(jnp.float32) * branch, axis=0, keepdims=True)
+
+    args = tuple(downs) + (hidden, cotangent, vectors)
+    out = [shape_of(rows, width, dtype=jnp.float32), shape_of(1, width, dtype=jnp.float32)]
+    return kernel_call(body, "layer_result", meta, args, [whole(a) for a in args], out, [whole(o) for o in out])
+
+
+def finish(meta, mine, other, kinds, name):
+    width = CHIPS * QUARTER
+
+    def body(meta_ref, mine_ref, other_ref, *outs):
+        core = meta_ref[OWN_CORE]
+        for ref, half in ((mine_ref, core), (other_ref, 1 - core)):
+            at = 0
+            for out_ref, (units, turned) in zip(outs, kinds):
+                values = ref[0, :, at : at + units].astype(jnp.float32)
+                place = pl.ds(pl.multiple_of(half * units, units), units)
+                if turned:
+                    out_ref[place, :] = values.T
+                else:
+                    out_ref[:, place] = values
+                at += units
+
+    side = pl.BlockSpec((1,) + mine.shape[1:], lambda j, m: (j, 0, 0))
+    out, specs = [], []
+    for units, turned in kinds:
+        shape = (2 * units, width) if turned else (width, 2 * units)
+        block = (2 * units, QUARTER) if turned else (QUARTER, 2 * units)
+        out.append(shape_of(*shape, dtype=jnp.float32))
+        specs.append(pl.BlockSpec(block, (lambda j, m: (0, m[j])) if turned else (lambda j, m: (m[j], 0))))
+    return kernel_call(body, name, meta, (mine, other), [side, side], out, specs, grid=(CHIPS,))
+
+
+def local_paired(
+    tokens,
+    slide_tiles,
+    norm1_gain,
+    norm1_bias,
+    w_query,
+    b_query,
+    w_key,
+    w_value,
+    b_value,
+    w_out,
+    b_out,
+    scale_attn,
+    norm2_gain,
+    norm2_bias,
+    w_up,
+    b_up,
+    w_down,
+    b_down,
+    scale_mlp,
+    cotangent,
+):
+    row_count, width = tokens.shape
+    half_u = w_up.shape[1] // 2
+    here = lax.axis_index("dp")
+    level = lax.axis_index("mp")
+    crops_here = row_count // L
+    per_slide = CROPS_DEV // SLIDES_DEV
+    crop = level * crops_here + jnp.arange(crops_here, dtype=jnp.int32)
+    owner = (crop // per_slide)[:, None] == jnp.arange(SLIDES_DEV, dtype=jnp.int32)[None, :]
+    limit = jnp.sum(jnp.where(owner, slide_tiles[None, :], 0), axis=1)
+    valid = (crop % per_slide < limit).astype(jnp.int32)
+    core = here & 1
+    sides = jnp.stack([(here >> 1) ^ side for side in range(CHIPS)] + [core]).astype(jnp.int32)
+    meta = jnp.concatenate([sides, valid])
+    biases = jnp.concatenate([b_query, b_value, b_up]).reshape(-1, BLOCK)
+    vectors = jnp.stack([norm1_gain, norm1_bias, norm2_gain, norm2_bias, scale_attn, scale_mlp, b_out, b_down])
+    first, second = (X_SIDE, Y_SIDE), (Y_SIDE, X_SIDE)
+
+    order = Order()
+
+    tokens_other = swap_plane(tokens, CORE_SIDE)
+    slice_attn, slice_rest = order(slice_weights, meta, w_query, w_key, w_value, w_out, w_up, w_down, biases)
+    level_attn = [swap_depth(slice_attn, mask) for mask in (1, 2, 3)]
+    one, one_other, grad, grad_b_down, one_turned, one_other_turned, grad_turned = order(
+        prepare, meta, tokens, tokens_other, cotangent, vectors
+    )
+    level_attn = order.land(*level_attn)
+
+    def stacked(low, high):
+        return lambda *parts: jnp.concatenate([part[low:high] for part in parts], axis=0)
+
+    far_attn = order(stacked(0, 3 * QUARTER), *level_attn)
+    plane_attn = plane_swaps(far_attn)
+    level_rest = swap_depth(order.hold(slice_rest), 2)
+    grad_far = swap_depth(order.hold(grad), 1)
+    far_out = order(stacked(3 * QUARTER, 4 * QUARTER), *level_attn)
+    level_rest, grad_far, *plane_attn = order.land(level_rest, grad_far, *plane_attn)
+    chips_attn = [far_attn] + plane_attn
+    far_out, grad, grad_far = order.hold((far_out, grad, grad_far))
+    plane_out = plane_swaps(far_out)
+    grad_other = swap_plane(grad, CORE_SIDE)
+    grad_far_other = swap_plane(grad_far, CORE_SIDE)
+    qkv, attended, probs = order(
+        attention_forward, meta, one, one_other, w_query, w_key, w_value, biases, level_attn, chips_attn
+    )
+    grad_other, grad_far_other, *plane_out = order.land(grad_other, grad_far_other, *plane_out)
+    chips_out = [far_out] + plane_out
+    plane_rest = plane_swaps(order.hold(level_rest))
+    out_near, *out_across = order(attention_out, meta, attended, w_out, chips_out)
+    out_got = [swap_plane(part, CORE_SIDE) for part in out_across]
+    grads_turned = [grad_turned] + list(order(turn, meta, grad_other, grad_far, grad_far_other))
+    hidden, branch, normed = order(attention_norm, meta, out_near, *out_got, tokens, vectors)
+    normed_far = swap_depth(normed, 1)
+
+    plane_rest = order.land(*plane_rest)
+    chips_rest = [level_rest] + plane_rest
+    normed_other = swap_plane(order.hold(normed), CORE_SIDE)
+    pair_rows = level_attn[1][4 * QUARTER :].astype(jnp.float32)
+    n_u = half_u // BLOCK
+    pair_bias = (pair_rows[2 : 2 + n_u] + pair_rows[4 + n_u : 4 + 2 * n_u]).reshape(-1)
+    bias_up = jnp.concatenate([lax.dynamic_slice_in_dim(b_up, core * half_u, half_u), pair_bias])[None, :]
+    near = order(
+        feed_forward, meta, (normed, normed_other), (grad, grad_other), w_up, w_down, bias_up, chips_rest, 10**12
+    )
+    (normed_far,) = order.land(normed_far)
+    normed_far_other = swap_plane(order.hold(normed_far), CORE_SIDE)
+    far = order(feed_forward, meta, (normed_far,), (grad_far,), w_up, w_down, bias_up, chips_rest)
+    far_other = order(
+        feed_forward, meta, (normed_far_other,), (grad_far_other,), w_up, w_down, bias_up, chips_rest
+    )
+    acts, gups, backs = [list(a) + list(b) + list(c) for a, b, c in zip(near[:3], far[:3], far_other[:3])]
+    grad_b_up = near[3] + far[3] + far_other[3]
+    (back_got,) = order.land(swap_plane(backs[3], CORE_SIDE))
+    back_far = order(add_low, backs[2], back_got)
+    back_far, back_near = order.hold((back_far, backs[1]))
+    back_far = swap_depth(back_far, 1)
+    back_near = swap_plane(back_near, CORE_SIDE)
+    kept_own, sent_own, kept_pair, sent_pair = order(
+        feed_gradients, meta, (normed, normed_other, normed_far, normed_far_other), grads_turned, gups, acts
+    )
+    downs = order(feed_down, meta, acts, w_down, chips_rest)
+    back_far, back_near = order.land(back_far, back_near)
+    sent_own, sent_pair, down_near, down_far = order.hold((sent_own, sent_pair, downs[1], downs[3]))
+    rest_got = [swap_plane(sent, side) for sent, side in zip((sent_own, sent_pair), first)]
+    down_near = swap_plane(down_near, CORE_SIDE)
+    down_far = swap_plane(down_far, CORE_SIDE)
+    dh, e1, sums_two = order(
+        hidden_gradient, meta, (backs[0], back_near, back_far), hidden, branch, cotangent, vectors
+    )
+    e1_other = swap_plane(e1, CORE_SIDE)
+    down_near, down_far = order.land(down_near, down_far)
+    down_far = swap_depth(order(add_low, downs[2], down_far), 1)
+    low_qkv, low_kept, low_sent = order(
+        attention_backward, meta, qkv, probs, attended, (e1, e1_other), (one_turned, one_other_turned), w_out, chips_out, 0
+    )
+    rest_got = order.land(*rest_got)
+
+    def add_sent(kept, got):
+        return add_low(kept[QUARTER:], got[QUARTER:])
+
+    def add_kept(kept, got, last):
+        return add_low(kept[:QUARTER], got[:QUARTER], last)
+
+    rest_kept = (kept_own, kept_pair)
+    rest_sent = [order(add_sent, kept, got) for kept, got in zip(rest_kept, rest_got)]
+    rest_last = [swap_plane(sent, side) for sent, side in zip(order.hold(rest_sent), second)]
+    high_qkv, high_kept, high_sent = order(
+        attention_backward, meta, qkv, probs, attended, (e1, e1_other), (one_turned, one_other_turned), w_out, chips_out, 1
+    )
+    *rest_last, down_far = order.land(*rest_last, down_far)
+    rest_own, rest_pair = [order(add_kept, *parts) for parts in zip(rest_kept, rest_got, rest_last)]
+    low_sent, high_sent, rest_pair = order.hold((low_sent, high_sent, rest_pair))
+    attn_got = [swap_plane(sent, side) for sent, side in zip((low_sent, high_sent), first)]
+    rest_pair = swap_depth(rest_pair, 2)
+    one_near, one_across, sums_qkv = order(
+        token_shares, meta, (low_qkv, high_qkv), w_query, w_key, w_value, chips_attn
+    )
+    one_got = swap_plane(one_across, CORE_SIDE)
+    layer_out, grad_scale_mlp = order(
+        layer_result, meta, (downs[0], down_near, down_far), hidden, cotangent, vectors
+    )
+    grad_tokens, sums_one = order(token_gradient, meta, one_near, one_got, tokens, dh, vectors)
+    *attn_got, rest_pair = order.land(*attn_got, rest_pair)
+    attn_kept = (low_kept, high_kept)
+    attn_sent = [order(add_sent, kept, got) for kept, got in zip(attn_kept, attn_got)]
+    attn_last = [swap_plane(sent, side) for sent, side in zip(order.hold(attn_sent), second)]
+    grad_rest = order(add_low, rest_own, rest_pair)
+
+    def gather_small(sums_qkv, grad_b_up, *small):
+        sums_qkv = sums_qkv.reshape(DEPTH, 3, BLOCK)
+        nothing = jnp.zeros((1, half_u), jnp.float32)
+        sums_up = jnp.concatenate([grad_b_up[:, :half_u], nothing, grad_b_up[:, half_u:], nothing], axis=0)
+        shared = jnp.concatenate([sums_qkv[:, 0], sums_qkv[:, 2], sums_up], axis=1)
+        shared = jnp.concatenate(
+            [lax.dynamic_slice_in_dim(shared, level ^ index, 1, 0) for index in range(DEPTH)]
+        ).reshape(1, -1, BLOCK)
+        shared = jnp.concatenate([jnp.where(core == half, shared, 0.0) for half in range(2)])
+        return jnp.concatenate([value.reshape(-1, BLOCK) for value in small] + [shared.reshape(-1, BLOCK)])
+
+    totals = order(gather_small, sums_qkv, grad_b_up, sums_one, sums_two, grad_scale_mlp, grad_b_down)
+    totals_got = swap_plane(totals, X_SIDE)
+    *attn_last, totals_got = order.land(*attn_last, totals_got)
+    totals = order(jnp.add, totals, totals_got)
+    low, high = [order(add_kept, *parts) for parts in zip(attn_kept, attn_got, attn_last)]
+    wide = 4 * BLOCK
+    level_sent = order(lambda low, high: jnp.stack([low[:, wide:], high[:, wide:]]), low, high)
+    totals, grad_rest, level_sent = order.hold((totals, grad_rest, level_sent))
+    level_got = swap_depth(level_sent, 1)
+    rest_x, rest_y = swap_plane(grad_rest, X_SIDE), swap_plane(grad_rest, Y_SIDE)
+    totals_got = swap_plane(totals, Y_SIDE)
+    level_got, rest_x, rest_y, totals_got = order.land(level_got, rest_x, rest_y, totals_got)
+    totals = order(jnp.add, totals, totals_got)
+    level_kept, level_sent = order(
+        lambda low, high, got: (add_low(low[:, :wide], got[0]), add_low(high[:, :wide], got[1])), low, high, level_got
+    )
+    totals, grad_rest, level_sent = order.hold((totals, grad_rest, level_sent))
+    level_got = swap_depth(level_sent, 2)
+    rest_corner = swap_plane(grad_rest, X_SIDE | Y_SIDE)
+    totals_got = swap_depth(totals, 1)
+    level_got, rest_corner, totals_got = order.land(level_got, rest_corner, totals_got)
+    grad_attn = order(add_low, level_kept, level_got)
+    totals = order(jnp.add, totals, totals_got)
+    rest_mine = order(lambda *parts: jnp.stack(parts), grad_rest, rest_x, rest_y, rest_corner)
+    totals, grad_attn, rest_mine = order.hold((totals, grad_attn, rest_mine))
+    plane_attn = plane_swaps(grad_attn)
+    rest_other = swap_plane(rest_mine, CORE_SIDE)
+    totals_got = swap_depth(totals, 2)
+    full_grad_up, full_grad_down = order(
+        finish, meta, rest_mine, rest_other, ((half_u, False), (half_u, True)), "finish_rest"
+    )
+    *plane_attn, totals_got = order.land(*plane_attn, totals_got)
+    attn_mine = order(lambda *parts: jnp.stack(parts), grad_attn, *plane_attn)
+    totals = order(jnp.add, totals, totals_got)
+    totals, attn_mine = order.hold((totals, attn_mine))
+    attn_other = swap_plane(attn_mine, CORE_SIDE)
+    totals_got = swap_plane(totals, CORE_SIDE)
+    full_grad_q, full_grad_k, full_grad_v, full_grad_o = order(
+        finish, meta, attn_mine, attn_other, ((BLOCK, False),) * 3 + ((BLOCK, True),), "finish_attn"
+    )
+    totals = order(jnp.add, totals, totals_got)
+    lines = width // BLOCK
+    small_total = totals[: 8 * lines].reshape(8, width)
+    shared_total = totals[8 * lines :].reshape(2, DEPTH, -1)
+    shared_total = lax.dynamic_index_in_dim(shared_total, level, 1, keepdims=False)
+    return (
+        layer_out,
+        grad_tokens,
+        small_total[0],
+        small_total[1],
+        full_grad_q,
+        shared_total[:, :BLOCK].reshape(-1),
+        full_grad_k,
+        full_grad_v,
+        shared_total[:, BLOCK : 2 * BLOCK].reshape(-1),
+        full_grad_o,
+        small_total[5],
+        small_total[4],
+        small_total[2],
+        small_total[3],
+        full_grad_up,
+        shared_total[:, 2 * BLOCK :].reshape(-1),
+        full_grad_down,
+        small_total[7],
+        small_total[6],
+    )
+
+
+def local_general(
     tokens,
     slide_tiles,
     norm1_gain,
@@ -346,4 +1328,6 @@
         P(),
         P(),
     )
+    paired = mesh.shape["dp"] == 8 and mesh.shape["mp"] == 4
+    local = local_paired if paired else local_general
     return jax.shard_map(local, mesh=mesh, in_specs=in_specs, out_specs=out_specs, check_vma=False)

time: 938 us -> 337 us (0.36)
  blocking collectives: 336 us -> 0 us
  waiting for transfers between devices: 294 us -> 115 us
  matrix products: 111 us -> 0 us
  Pallas kernels: 0 us -> 110 us
  local copies, waits for them, and re-layouts: 106 us -> 37.4 us
  starting transfers between devices: 9.17 us -> 51.3 us
  other arithmetic: 57.8 us -> 15.9 us
  between operations: 17.4 us -> 2.22 us
    unnamed x5 -> x0, blocking collectives: 270 us -> none
    all_gather x6 -> x0, waiting for transfers between devices: 214 us -> none  [the longest x1 67.1 us: local(): rows_one = lax.all_gather(normed_one, 'mp', axis=0, tiled=True)]
    ppermute x0 -> x54, waiting for transfers between devices: none -> 115 us  [the longest x13 68.5 us: swap_depth(): return lax.ppermute(values, 'mp', [(i, i ^ mask) for i in range(DEPTH)])]
    dot_general x24 -> x0, matrix products: 111 us -> none  [the longest x6 35 us: contract_cols(): lax.dot_general(left, right, (((1,), (1,)), ((), ())), preferred_element_...]
    pallas_call x0 -> x19, Pallas kernels: none -> 110 us  [kernel_call(): pl.pallas_call(body, grid_spec=pltpu.PrefetchScalarGridSpec(num_scalar_pr...]
    reduce_scatter x6 -> x0, waiting for transfers between devices: 77.4 us -> none  [the longest x1 27.2 us: local(): lax.psum_scatter(grad_w_query.astype(jnp.bfloat16), 'dp', scatter_dimensi...]
    all_gather x6 -> x0, blocking collectives: 55.4 us -> none  [the longest x1 9.79 us: local(): lax.all_gather(share_wv.astype(jnp.bfloat16), 'dp', axis=0, tiled=True)]
    ppermute x0 -> x54, starting transfers between devices: none -> 51.3 us  [the longest x41 31.5 us: swap_plane(): return lax.ppermute(values, 'dp', [(i, i ^ mask) for i in range(PLANE)])]
  transfers between devices with their start and end apart: 17 -> 54, of which waited for: 10 -> 21; matrix products, arithmetic and copies ran while one was open for 42% -> 1% of each run, Pallas kernels for 0% -> 32%
where the time goes in v2:
time: 337 us; the launch traced here: 332 us
  waiting for transfers between devices  115 us (34%)
  Pallas kernels  110 us (33%)
  starting transfers between devices  51.3 us (15%)
  local copies, waits for them, and re-layouts  37.4 us (11%)
  other arithmetic  15.9 us (5%)
    pallas_call x19, Pallas kernels, kernel_call(): pl.pallas_call(body, grid_spec=pltpu.PrefetchScalarGridSpec(num_scalar_pr...  110 us
    ppermute x13, waiting for transfers between devices, swap_depth(): return lax.ppermute(values, 'mp', [(i, i ^ mask) for i in range(DEPTH)])  68.5 us
    ppermute x41, waiting for transfers between devices, swap_plane(): return lax.ppermute(values, 'dp', [(i, i ^ mask) for i in range(PLANE)])  46.2 us
    unnamed x227, local copies, waits for them, and re-layouts  35.8 us
    ppermute x41, starting transfers between devices, swap_plane(): return lax.ppermute(values, 'dp', [(i, i ^ mask) for i in range(PLANE)])  31.5 us
    ppermute x13, starting transfers between devices, swap_depth(): return lax.ppermute(values, 'mp', [(i, i ^ mask) for i in range(DEPTH)])  19.8 us
    convert_element_type x13, other arithmetic, add_low(): sum((value.astype(jnp.float32) for value in values)).astype(jnp.bfloat16)  11.7 us
  transfers between devices with their start and end apart: 54, of which 21 were waited for; matrix products, arithmetic and copies ran while one was open for 1% of the time, Pallas kernels for 32%

profile of v2, /device:TPU:0, one launch (start us, length us, event | category | flops | bytes accessed | tf_op | source)
XLA Modules:
  0.0 331.6 jit_solution(10419780323127836102)
XLA Ops:
  2.9 1.6 copy-done
  4.4 1.6 copy-done.2
  10.3 1.4 slice_weights.1
  12.5 4.6 %collective-permute-start.3 = (bf16[1040,128]{1,0:T(8,128)(2,1)}, bf16[1040,128]{1,0:T(8,128)(2,1)S(1)}, u32[]{:S(2)}, u32[]{:S(2)}) collective-permute-start(bf16[1040,128]{1,0:T(8,128)(2,1)} %get-tuple-element.389), channel_id=1, source_target_pairs={{0,3},{1,2},{2,1},{3,0},{4,7},{5,6},{6,5},{7,4},{8,11},{9,10},{10,... | collective-permute-start | bytes 798728 | tf_op jit(solution)/shard_map/ppermute | solution.py:67
  17.9 3.3 prepare.1
  22.2 2.6 collective-permute-done.3.three_ref
  24.7 15.9 %collective-permute-done.2.two_ref = bf16[1040,128]{1,0:T(8,128)(2,1)S(1)} collective-permute-done((bf16[1040,128]{1,0:T(8,128)(2,1)}, bf16[1040,128]{1,0:T(8,128)(2,1)S(1)}, u32[]{:S(2)}, u32[]{:S(2)}) %collective-permute-start.2) | collective-permute-done | bytes 266272 | tf_op jit(solution)/shard_map/ppermute | solution.py:67
  40.9 2.5 collective-permute-start.8
  44.4 3.0 collective-permute-start.4
  47.5 22.3 %collective-permute-done.4.refs_7_.refs_5_ = bf16[2048,128]{1,0:T(8,128)(2,1)S(1)} collective-permute-done((bf16[2048,128]{1,0:T(8,128)(2,1)S(1)}, bf16[2048,128]{1,0:T(8,128)(2,1)S(1)}, u32[]{:S(2)}, u32[]{:S(2)}) %collective-permute-start.4) | collective-permute-done | bytes 524320 | tf_op jit(solution)/shard_map/ppermute | solution.py:67
  69.8 2.2 collective-permute-done.5.refs_1_
  72.5 2.5 collective-permute-start.13
  76.0 10.6 %attention_forward.1 = (bf16[2,394,1536]{2,1,0:T(8,128)(2,1)S(1)}, bf16[2,394,512]{2,1,0:T(8,128)(2,1)S(1)}, bf16[4,2,2,2,208,208]{5,4,3,2,1,0:T(8,128)(2,1)S(1)}) custom-call(s32[7]{0:T(128)S(1)} %concatenate.30.meta_ref, bf16[394,1024]{1,0:T(8,128)(2,1)S(1)} %get-tuple-element.415.normed_ref, bf16[394,1024]{1,0:T(8,128)(2,1)S(1)} %get-tuple-element.416.other_ref, ...), custom_call_target="tpu_custom_call" | custom-call | flops 1000 | bytes 1000 | tf_op jit(solution)/shard_map/attention_forward/pallas_call | solution.py:129
  86.6 1.4 copy-done.6
  88.1 2.5 collective-permute-start.18
  91.7 1.8 attention_out.1
  96.0 1.4 turn.1
  100.3 2.3 attention_norm.1
  105.8 7.6 %collective-permute-done.17.refs_9_.refs_7_ = bf16[2048,128]{1,0:T(8,128)(2,1)S(1)} collective-permute-done((bf16[2048,128]{1,0:T(8,128)(2,1)S(1)}, bf16[2048,128]{1,0:T(8,128)(2,1)S(1)}, u32[]{:S(2)}, u32[]{:S(2)}) %collective-permute-start.17) | collective-permute-done | bytes 524320 | tf_op jit(solution)/shard_map/ppermute | solution.py:63
  115.7 1.6 collective-permute-start.20
  117.6 1.6 copy-done.3
  124.6 9.6 %feed_forward.3 = (bf16[394,1024]{1,0:T(8,128)(2,1)S(1)}, bf16[394,1024]{1,0:T(8,128)(2,1)S(1)}, bf16[394,1024]{1,0:T(8,128)(2,1)S(1)}, bf16[394,1024]{1,0:T(8,1...) custom-call(s32[7]{0:T(128)S(1)} %concatenate.30.meta_ref, ...), custom_call_target="tpu_custom_call" | custom-call | flops 999999995904 | bytes 1000 | tf_op jit(solution)/shard_map/feed_forward/pallas_call | solution.py:129
  134.3 2.5 collective-permute-done.20.refs_0_.refs_2_
  136.8 5.8 %feed_forward.4 = (bf16[394,1024]{1,0:T(8,128)(2,1)S(1)}, bf16[394,1024]{1,0:T(8,128)(2,1)S(1)}, bf16[394,1024]{1,0:T(8,128)(2,1)S(1)}, f32[1,1024]{1,0:T(1,128)S(1)}) custom-call(s32[7]{0:T(128)S(1)} %concatenate.30.meta_ref, bf16[394,1024]{1,0:T(8,128)(2,1)} %collective-permute-done.20.refs_0_.refs_2_, bf16[394,1024]{1,0:T(8,128)(2,1)S(1)} %copy-done.45, ...), custom_call_target="tpu_custom_call" | custom-call | flops 1000 | bytes 1000 | tf_op jit(solution)/shard_map/feed_forward/pallas_call | solution.py:129
  142.7 5.0 %feed_forward.5 = (bf16[394,1024]{1,0:T(8,128)(2,1)S(1)}, bf16[394,1024]{1,0:T(8,128)(2,1)S(1)}, bf16[394,1024]{1,0:T(8,128)(2,1)S(1)}, f32[1,1024]{1,0:T(1,128)S(1)}) custom-call(s32[7]{0:T(128)S(1)} %concatenate.30.meta_ref, bf16[394,1024]{1,0:T(8,128)(2,1)S(1)} %collective-permute-done.21.refs_0_.refs_3_, bf16[394,1024]{1,0:T(8,128)(2,1)S(1)} %copy-done.47, ...), custom_call_target="tpu_custom_call" | custom-call | flops 1000 | bytes 1000 | tf_op jit(solution)/shard_map/feed_forward/pallas_call | solution.py:129
  148.3 2.0 collective-permute-done.22
  150.5 1.6 collective-permute-start.23
  152.2 13.1 %feed_gradients.1 = (bf16[512,1024]{1,0:T(8,128)(2,1)S(1)}, bf16[512,1024]{1,0:T(8,128)(2,1)S(1)}, bf16[512,1024]{1,0:T(8,128)(2,1)S(1)}, bf16[512,1024]{1,0:T(8,128)(2,1)S(1)}) custom-call(s32[7]{0:T(128)S(1)} %concatenate.30.meta_ref, bf16[394,1024]{1,0:T(8,128)(2,1)} %get-tuple-element.520.refs_0_, bf16[394,1024]{1,0:T(8,128)(2,1)} %collective-permute-done.19.refs_1_, ...), custom_call_target="tpu_custom_call" | custom-call | flops 1000 | bytes 1000 | tf_op jit(solution)/shard_map/feed_gradients/pallas_call | solution.py:129
  165.4 4.5 %feed_down.1 = (bf16[394,1024]{1,0:T(8,128)(2,1)S(1)}, bf16[394,1024]{1,0:T(8,128)(2,1)S(1)}, bf16[394,1024]{1,0:T(8,128)(2,1)S(1)}, bf16[394,1024]{1,0:T(8,128)(2,1)S(1)}) custom-call(s32[7]{0:T(128)S(1)} %concatenate.30.meta_ref, bf16[394,1024]{1,0:T(8,128)(2,1)S(1)} %get-tuple-element.538.refs_12_.refs_0_, ...), custom_call_target="tpu_custom_call" | custom-call | flops 1000 | bytes 1000 | tf_op jit(solution)/shard_map/feed_down/pallas_call | solution.py:129
  171.6 1.5 collective-permute-start.27
  174.0 2.3 hidden_gradient.1
  177.9 1.6 collective-permute-start.32
  180.0 12.9 %attention_backward.2 = (bf16[2,394,768]{2,1,0:T(8,128)(2,1)S(1)}, bf16[512,1024]{1,0:T(8,128)(2,1)S(1)}, bf16[512,1024]{1,0:T(8,128)(2,1)}) custom-call(s32[7]{0:T(128)S(1)} %concatenate.30.meta_ref, bf16[2,394,1536]{2,1,0:T(8,128)(2,1)S(1)} %copy-done.7, bf16[4,2,2,2,208,208]{5,4,3,2,1,0:T(8,128)(2,1)S(1)} %copy-done.5, ...), custom_call_target="tpu_custom_call" | custom-call | flops 1000 | bytes 1000 | tf_op jit(solution)/shard_map/attention_backward/pallas_call | solution.py:129
  192.8 4.0 %collective-permute-done.27 = bf16[512,1024]{1,0:T(8,128)(2,1)S(1)} collective-permute-done((bf16[512,1024]{1,0:T(8,128)(2,1)S(1)}, bf16[512,1024]{1,0:T(8,128)(2,1)S(1)}, u32[]{:S(2)}, u32[]{:S(2)}) %collective-permute-start.27) | collective-permute-done | bytes 1048608 | tf_op jit(solution)/shard_map/ppermute | solution.py:63
  199.3 1.2 collective-permute-start.31
  200.5 13.1 %attention_backward.3 = (bf16[2,394,768]{2,1,0:T(8,128)(2,1)S(1)}, bf16[512,1024]{1,0:T(8,128)(2,1)S(1)}, bf16[512,1024]{1,0:T(8,128)(2,1)}) custom-call(s32[7]{0:T(128)S(1)} %concatenate.30.meta_ref, bf16[2,394,1536]{2,1,0:T(8,128)(2,1)S(1)} %copy-done.7, bf16[4,2,2,2,208,208]{5,4,3,2,1,0:T(8,128)(2,1)S(1)} %copy-done.5, ...), custom_call_target="tpu_custom_call" | custom-call | flops 1000 | bytes 1000 | tf_op jit(solution)/shard_map/attention_backward/pallas_call | solution.py:129
  218.1 9.1 %token_shares.1 = (f32[394,1024]{1,0:T(8,128)S(1)}, bf16[394,1024]{1,0:T(8,128)(2,1)}, f32[4,1,384]{2,1,0:T(1,128)S(1)}) custom-call(s32[7]{0:T(128)S(1)} %concatenate.30.meta_ref, bf16[2,394,768]{2,1,0:T(8,128)(2,1)S(1)} %get-tuple-element.629.low_ref, bf16[2,394,768]{2,1,0:T(8,128)(2,1)S(1)} %get-tuple-element.630.high_ref, ...), custom_call_target="tpu_custom_call" | custom-call | flops 1000 | bytes 1000 | tf_op jit(solution)/shard_map/token_shares/pallas_call | solution.py:129
  228.3 1.6 collective-permute-start.36
  229.9 1.3 add_add_fusion
  231.2 1.4 copy-done.19
  234.9 2.4 layer_result.1
  237.3 4.2 %token_gradient.1 = (f32[394,1024]{1,0:T(8,128)}, f32[2,1024]{1,0:T(2,128)S(1)}) custom-call(s32[7]{0:T(128)S(1)} %concatenate.30.meta_ref, f32[394,1024]{1,0:T(8,128)S(1)} %copy-done.65, bf16[394,1024]{1,0:T(8,128)(2,1)} %collective-permute-done.33.got_ref, bf16[394,1024]{1,0:T(8,128)(2,1)S(1)} %copy-done.13, f32[394,1024]{1,0:T(8,128)S(1)} %copy-done.63, ...), custom_call_target="tpu_custom_call" | custom-call | flops 1000 | bytes 1000 | tf_op jit(solution)/shard_map/token_gradient/pallas_call | solution.py:129
  241.6 13.5 %collective-permute-done.36 = bf16[256,1024]{1,0:T(8,128)(2,1)} collective-permute-done((bf16[256,1024]{1,0:T(8,128)(2,1)}, bf16[256,1024]{1,0:T(8,128)(2,1)}, u32[]{:S(2)}, u32[]{:S(2)}) %collective-permute-start.36) | collective-permute-done | bytes 524320 | tf_op jit(solution)/shard_map/ppermute | solution.py:67
  255.1 2.0 add_convert_fusion.6
  257.2 2.1 add_convert_fusion.5
  259.2 1.2 add_convert_fusion.4
  261.5 1.2 collective-permute-start.38
  263.7 12.4 %collective-permute-done.39 = f32[112,128]{1,0:T(8,128)S(1)} collective-permute-done((f32[112,128]{1,0:T(8,128)S(1)}, f32[112,128]{1,0:T(8,128)S(1)}, u32[]{:S(2)}, u32[]{:S(2)}) %collective-permute-start.39) | collective-permute-done | bytes 57376 | tf_op jit(solution)/shard_map/ppermute | solution.py:63
  277.0 1.5 add_convert_fusion.3
  278.5 1.5 add_convert_fusion.2
  280.1 1.3 collective-permute-start.42
  281.9 1.5 collective-permute-start.43
  283.4 10.4 %collective-permute-done.43 = f32[112,128]{1,0:T(8,128)S(1)} collective-permute-done((f32[112,128]{1,0:T(8,128)S(1)}, f32[112,128]{1,0:T(8,128)S(1)}, u32[]{:S(2)}, u32[]{:S(2)}) %collective-permute-start.43) | collective-permute-done | bytes 57376 | tf_op jit(solution)/shard_map/ppermute | solution.py:63
  294.1 1.2 collective-permute-start.45
  295.3 3.1 collective-permute-start.44
  298.8 4.2 %collective-permute-done.46 = f32[112,128]{1,0:T(8,128)S(1)} collective-permute-done((f32[112,128]{1,0:T(8,128)S(1)}, f32[112,128]{1,0:T(8,128)S(1)}, u32[]{:S(2)}, u32[]{:S(2)}) %collective-permute-start.46) | collective-permute-done | bytes 57376 | tf_op jit(solution)/shard_map/ppermute | solution.py:67
  303.0 4.9 %collective-permute-done.44 = bf16[256,512]{1,0:T(8,128)(2,1)S(1)} collective-permute-done((bf16[256,512]{1,0:T(8,128)(2,1)S(1)}, bf16[256,512]{1,0:T(8,128)(2,1)S(1)}, u32[]{:S(2)}, u32[]{:S(2)}) %collective-permute-start.44) | collective-permute-done | bytes 262176 | tf_op jit(solution)/shard_map/ppermute | solution.py:67
  308.3 1.8 collective-permute-start.49
  310.2 1.2 collective-permute-start.48
  311.9 1.8 collective-permute-start.50
  313.7 4.3 %finish_rest.1 = (f32[1024,1024]{1,0:T(8,128)}, f32[1024,1024]{1,0:T(8,128)}) custom-call(s32[7]{0:T(128)S(1)} %concatenate.30.meta_ref, bf16[4,256,1024]{2,1,0:T(8,128)(2,1)S(1)} %pad_maximum_fusion.mine_ref, bf16[4,256,1024]{2,1,0:T(8,128)(2,1)S(1)} %collective-permute-done.51.other_ref), custom_call_target="tpu_custom_call" | custom-call | flops 1000 | bytes 1000 | tf_op jit(solution)/shard_map/finish_rest/pallas_call | solution.py:129
  318.4 5.1 %collective-permute-done.48 = bf16[256,512]{1,0:T(8,128)(2,1)S(1)} collective-permute-done((bf16[256,512]{1,0:T(8,128)(2,1)S(1)}, bf16[256,512]{1,0:T(8,128)(2,1)S(1)}, u32[]{:S(2)}, u32[]{:S(2)}) %collective-permute-start.48) | collective-permute-done | bytes 262176 | tf_op jit(solution)/shard_map/ppermute | solution.py:63
  324.4 2.1 collective-permute-done.53.other_ref
  326.6 3.0 finish_attn.1
  (349 shorter events, 53.1 us)
Async XLA Ops:
  0.7 17.2 %collective-permute-start = (bf16[394,1024]{1,0:T(8,128)(2,1)}, bf16[394,1024]{1,0:T(8,128)(2,1)S(1)}, u32[]{:S(2)}, u32[]{:S(2)}) collective-permute-start(bf16[394,1024]{1,0:T(8,128)(2,1)} %tokens_ref.2), channel_id=1, source_target_pairs={{0,4},{4,0},{8,12},{12,8},{16,20},{20,16},{24,28},{28,24},{1,5},{5... | collective-permute-start | bytes 2420744 | tf_op jit(solution)/shard_map/ppermute | solution.py:63
  12.5 12.2 %collective-permute-start.3 = (bf16[1040,128]{1,0:T(8,128)(2,1)}, bf16[1040,128]{1,0:T(8,128)(2,1)S(1)}, u32[]{:S(2)}, u32[]{:S(2)}) collective-permute-start(bf16[1040,128]{1,0:T(8,128)(2,1)} %get-tuple-element.389), channel_id=1, source_target_pairs={{0,3},{1,2},{2,1},{3,0},{4,7},{5,6},{6,5},{7,4},{8,11},{9,10},{10,... | collective-permute-start | bytes 798728 | tf_op jit(solution)/shard_map/ppermute | solution.py:67
  17.1 23.5 %collective-permute-start.2 = (bf16[1040,128]{1,0:T(8,128)(2,1)}, bf16[1040,128]{1,0:T(8,128)(2,1)S(1)}, u32[]{:S(2)}, u32[]{:S(2)}) collective-permute-start(bf16[1040,128]{1,0:T(8,128)(2,1)} %get-tuple-element.389), channel_id=1, source_target_pairs={{0,2},{1,3},{2,0},{3,1},{4,6},{5,7},{6,4},{7,5},{8,10},{9,11},{10,... | collective-permute-start | bytes 798728 | tf_op jit(solution)/shard_map/ppermute | solution.py:67
  17.2 23.5 %collective-permute-start.1 = (bf16[1040,128]{1,0:T(8,128)(2,1)}, bf16[1040,128]{1,0:T(8,128)(2,1)S(1)}, u32[]{:S(2)}, u32[]{:S(2)}) collective-permute-start(bf16[1040,128]{1,0:T(8,128)(2,1)} %get-tuple-element.389), channel_id=1, source_target_pairs={{0,1},{1,0},{2,3},{3,2},{4,5},{5,4},{6,7},{7,6},{8,9},{9,8},{10,11... | collective-permute-start | bytes 798728 | tf_op jit(solution)/shard_map/ppermute | solution.py:67
  22.1 53.8 %copy-start.40 = (bf16[1024,394]{1,0:T(8,128)(2,1)}, bf16[1024,394]{1,0:T(8,128)(2,1)S(1)}, u32[]{:S(2)}) copy-start(bf16[1024,394]{1,0:T(8,128)(2,1)S(1)} %get-tuple-element.611.n_ref) | copy-start | bytes 2420740
  22.1 53.8 %copy-start.42 = (bf16[1024,394]{1,0:T(8,128)(2,1)}, bf16[1024,394]{1,0:T(8,128)(2,1)S(1)}, u32[]{:S(2)}) copy-start(bf16[1024,394]{1,0:T(8,128)(2,1)S(1)} %get-tuple-element.612.n_other_ref) | copy-start | bytes 2420740
  22.1 64.4 %copy-start.94 = (bf16[394,1024]{1,0:T(8,128)(2,1)}, bf16[394,1024]{1,0:T(8,128)(2,1)S(1)}, u32[]{:S(2)}) copy-start(bf16[394,1024]{1,0:T(8,128)(2,1)S(1)} %get-tuple-element.473.refs_2_) | copy-start | bytes 2420740
  22.1 53.8 %copy-start.23 = (bf16[1024,256]{1,0:T(8,128)(2,1)S(1)}, bf16[1024,256]{1,0:T(8,128)(2,1)}, u32[]{:S(2)}) copy-start(bf16[1024,256]{1,0:T(8,128)(2,1)} %q_ref.3) | copy-start | bytes 1572868
  22.2 53.8 %copy-start.26 = (bf16[1024,256]{1,0:T(8,128)(2,1)S(1)}, bf16[1024,256]{1,0:T(8,128)(2,1)}, u32[]{:S(2)}) copy-start(bf16[1024,256]{1,0:T(8,128)(2,1)} %k_ref.3) | copy-start | bytes 1572868
  22.2 53.8 %copy-start.29 = (bf16[1024,256]{1,0:T(8,128)(2,1)S(1)}, bf16[1024,256]{1,0:T(8,128)(2,1)}, u32[]{:S(2)}) copy-start(bf16[1024,256]{1,0:T(8,128)(2,1)} %v_ref.3) | copy-start | bytes 1572868
  40.7 45.9 %copy-start.68 = (bf16[1040,128]{1,0:T(8,128)(2,1)}, bf16[1040,128]{1,0:T(8,128)(2,1)S(1)}, u32[]{:S(2)}) copy-start(bf16[1040,128]{1,0:T(8,128)(2,1)S(1)} %collective-permute-done.2.two_ref) | copy-start | bytes 798724
  40.8 45.8 %copy-start.20 = (bf16[2304,128]{1,0:T(8,128)(2,1)}, bf16[2304,128]{1,0:T(8,128)(2,1)S(1)}, u32[]{:S(2)}) copy-start(bf16[2304,128]{1,0:T(8,128)(2,1)S(1)} %pad_maximum_fusion.2.refs_0_) | copy-start | bytes 1769476
  40.8 31.1 %collective-permute-start.5 = (bf16[394,1024]{1,0:T(8,128)(2,1)S(1)}, bf16[394,1024]{1,0:T(8,128)(2,1)S(1)}, u32[]{:S(2)}, u32[]{:S(2)}) collective-permute-start(bf16[394,1024]{1,0:T(8,128)(2,1)S(1)} %get-tuple-element.473.refs_2_), channel_id=1, source_target_pairs={{0,1},{1,0},{2,3},{3,2},{4,5},{5,4},{6,7},{7,6},{8,9},{9,8},{10,11... | collective-permute-start | bytes 2420744 | tf_op jit(solution)/shard_map/ppermute | solution.py:67
  40.9 28.9 %collective-permute-start.8 = (bf16[2304,128]{1,0:T(8,128)(2,1)S(1)}, bf16[2304,128]{1,0:T(8,128)(2,1)S(1)}, u32[]{:S(2)}, u32[]{:S(2)}) collective-permute-start(bf16[2304,128]{1,0:T(8,128)(2,1)S(1)} %pad_maximum_fusion.2.refs_0_), channel_id=1, source_target_pairs={{0,24},{4,28},{8,16},{12,20},{16,8},{20,12},{24,0},{28,4},{1,25},{... | collective-permute-start | bytes 1769480 | tf_op jit(solution)/shard_map/ppermute | solution.py:63
  43.4 26.4 %collective-permute-start.7 = (bf16[2304,128]{1,0:T(8,128)(2,1)S(1)}, bf16[2304,128]{1,0:T(8,128)(2,1)S(1)}, u32[]{:S(2)}, u32[]{:S(2)}) collective-permute-start(bf16[2304,128]{1,0:T(8,128)(2,1)S(1)} %pad_maximum_fusion.2.refs_0_), channel_id=1, source_target_pairs={{0,16},{4,20},{8,24},{12,28},{16,0},{20,4},{24,8},{28,12},{1,17},{... | collective-permute-start | bytes 1769480 | tf_op jit(solution)/shard_map/ppermute | solution.py:63
  43.9 25.9 %collective-permute-start.6 = (bf16[2304,128]{1,0:T(8,128)(2,1)S(1)}, bf16[2304,128]{1,0:T(8,128)(2,1)S(1)}, u32[]{:S(2)}, u32[]{:S(2)}) collective-permute-start(bf16[2304,128]{1,0:T(8,128)(2,1)S(1)} %pad_maximum_fusion.2.refs_0_), channel_id=1, source_target_pairs={{0,8},{4,12},{8,0},{12,4},{16,24},{20,28},{24,16},{28,20},{1,9},{5... | collective-permute-start | bytes 1769480 | tf_op jit(solution)/shard_map/ppermute | solution.py:63
  44.4 25.3 %collective-permute-start.4 = (bf16[2048,128]{1,0:T(8,128)(2,1)S(1)}, bf16[2048,128]{1,0:T(8,128)(2,1)S(1)}, u32[]{:S(2)}, u32[]{:S(2)}) collective-permute-start(bf16[2048,128]{1,0:T(8,128)(2,1)S(1)} %copy-done.97), channel_id=1, source_target_pairs={{0,2},{1,3},{2,0},{3,1},{4,6},{5,7},{6,4},{7,5},{8,10},{9,11},{10,... | collective-permute-start | bytes 1572872 | tf_op jit(solution)/shard_map/ppermute | solution.py:67
  47.4 44.2 %copy-start.48 = (bf16[768,128]{1,0:T(8,128)(2,1)}, bf16[768,128]{1,0:T(8,128)(2,1)S(1)}, u32[]{:S(2)}) copy-start(bf16[768,128]{1,0:T(8,128)(2,1)S(1)} %pad_maximum_fusion.4) | copy-start | bytes 589828
  71.9 24.1 %copy-start.44 = (bf16[394,1024]{1,0:T(8,128)(2,1)}, bf16[394,1024]{1,0:T(8,128)(2,1)S(1)}, u32[]{:S(2)}) copy-start(bf16[394,1024]{1,0:T(8,128)(2,1)S(1)} %collective-permute-done.5.refs_1_) | copy-start | bytes 2420740
  71.9 16.2 %collective-permute-start.9 = (bf16[394,1024]{1,0:T(8,128)(2,1)S(1)}, bf16[394,1024]{1,0:T(8,128)(2,1)S(1)}, u32[]{:S(2)}, u32[]{:S(2)}) collective-permute-start(bf16[394,1024]{1,0:T(8,128)(2,1)S(1)} %get-tuple-element.473.refs_2_), channel_id=1, source_target_pairs={{0,4},{4,0},{8,12},{12,8},{16,20},{20,16},{24,28},{28,24},{1,5},{5... | collective-permute-start | bytes 2420744 | tf_op jit(solution)/shard_map/ppermute | solution.py:63
  71.9 16.2 %collective-permute-start.10 = (bf16[394,1024]{1,0:T(8,128)(2,1)S(1)}, bf16[394,1024]{1,0:T(8,128)(2,1)S(1)}, u32[]{:S(2)}, u32[]{:S(2)}) collective-permute-start(bf16[394,1024]{1,0:T(8,128)(2,1)S(1)} %collective-permute-done.5.refs_1_), channel_id=1, source_target_pairs={{0,4},{4,0},{8,12},{12,8},{16,20},{20,16},{24,28},{28,24},{1,5},{5... | collective-permute-start | bytes 2420744 | tf_op jit(solution)/shard_map/ppermute | solution.py:63
  72.5 15.6 %collective-permute-start.13 = (bf16[768,128]{1,0:T(8,128)(2,1)S(1)}, bf16[768,128]{1,0:T(8,128)(2,1)S(1)}, u32[]{:S(2)}, u32[]{:S(2)}) collective-permute-start(bf16[768,128]{1,0:T(8,128)(2,1)S(1)} %pad_maximum_fusion.4), channel_id=1, source_target_pairs={{0,24},{4,28},{8,16},{12,20},{16,8},{20,12},{24,0},{28,4},{1,25},{... | collective-permute-start | bytes 589832 | tf_op jit(solution)/shard_map/ppermute | solution.py:63
  74.9 13.2 %collective-permute-start.12 = (bf16[768,128]{1,0:T(8,128)(2,1)S(1)}, bf16[768,128]{1,0:T(8,128)(2,1)S(1)}, u32[]{:S(2)}, u32[]{:S(2)}) collective-permute-start(bf16[768,128]{1,0:T(8,128)(2,1)S(1)} %pad_maximum_fusion.4), channel_id=1, source_target_pairs={{0,16},{4,20},{8,24},{12,28},{16,0},{20,4},{24,8},{28,12},{1,17},{... | collective-permute-start | bytes 589832 | tf_op jit(solution)/shard_map/ppermute | solution.py:63
  75.4 12.7 %collective-permute-start.11 = (bf16[768,128]{1,0:T(8,128)(2,1)S(1)}, bf16[768,128]{1,0:T(8,128)(2,1)S(1)}, u32[]{:S(2)}, u32[]{:S(2)}) collective-permute-start(bf16[768,128]{1,0:T(8,128)(2,1)S(1)} %pad_maximum_fusion.4), channel_id=1, source_target_pairs={{0,8},{4,12},{8,0},{12,4},{16,24},{20,28},{24,16},{28,20},{1,9},{5... | collective-permute-start | bytes 589832 | tf_op jit(solution)/shard_map/ppermute | solution.py:63
  88.1 16.8 %collective-permute-start.18 = (bf16[2048,128]{1,0:T(8,128)(2,1)S(1)}, bf16[2048,128]{1,0:T(8,128)(2,1)S(1)}, u32[]{:S(2)}, u32[]{:S(2)}) collective-permute-start(bf16[2048,128]{1,0:T(8,128)(2,1)S(1)} %collective-permute-done.4.refs_7_.refs_5_), channel_id=1, source_target_pairs={{0,24},{4,28},{8,16},{12,20},{16,8},{20,12},{24,0},{28,4},{1,25},{... | collective-permute-start | bytes 1572872 | tf_op jit(solution)/shard_map/ppermute | solution.py:63
  90.7 22.7 %collective-permute-start.17 = (bf16[2048,128]{1,0:T(8,128)(2,1)S(1)}, bf16[2048,128]{1,0:T(8,128)(2,1)S(1)}, u32[]{:S(2)}, u32[]{:S(2)}) collective-permute-start(bf16[2048,128]{1,0:T(8,128)(2,1)S(1)} %collective-permute-done.4.refs_7_.refs_5_), channel_id=1, source_target_pairs={{0,16},{4,20},{8,24},{12,28},{16,0},{20,4},{24,8},{28,12},{1,17},{... | collective-permute-start | bytes 1572872 | tf_op jit(solution)/shard_map/ppermute | solution.py:63
  91.1 23.0 %collective-permute-start.16 = (bf16[2048,128]{1,0:T(8,128)(2,1)S(1)}, bf16[2048,128]{1,0:T(8,128)(2,1)S(1)}, u32[]{:S(2)}, u32[]{:S(2)}) collective-permute-start(bf16[2048,128]{1,0:T(8,128)(2,1)S(1)} %collective-permute-done.4.refs_7_.refs_5_), channel_id=1, source_target_pairs={{0,8},{4,12},{8,0},{12,4},{16,24},{20,28},{24,16},{28,20},{1,9},{5... | collective-permute-start | bytes 1572872 | tf_op jit(solution)/shard_map/ppermute | solution.py:63
  95.5 4.8 %collective-permute-start.14 = (bf16[394,512]{1,0:T(8,128)(2,1)S(1)}, bf16[394,512]{1,0:T(8,128)(2,1)S(1)}, u32[]{:S(2)}, u32[]{:S(2)}) collective-permute-start(bf16[394,512]{1,0:T(8,128)(2,1)S(1)} %get-tuple-element.446), channel_id=1, source_target_pairs={{0,4},{4,0},{8,12},{12,8},{16,20},{20,16},{24,28},{28,24},{1,5},{5... | collective-permute-start | bytes 1210376 | tf_op jit(solution)/shard_map/ppermute | solution.py:63
  95.5 4.8 %collective-permute-start.15 = (bf16[394,512]{1,0:T(8,128)(2,1)S(1)}, bf16[394,512]{1,0:T(8,128)(2,1)S(1)}, u32[]{:S(2)}, u32[]{:S(2)}) collective-permute-start(bf16[394,512]{1,0:T(8,128)(2,1)S(1)} %get-tuple-element.447), channel_id=1, source_target_pairs={{0,4},{4,0},{8,12},{12,8},{16,20},{20,16},{24,28},{28,24},{1,5},{5... | collective-permute-start | bytes 1210376 | tf_op jit(solution)/shard_map/ppermute | solution.py:63
  114.9 2.7 collective-permute-start.19
  115.7 21.0 %collective-permute-start.20 = (bf16[394,1024]{1,0:T(8,128)(2,1)}, bf16[394,1024]{1,0:T(8,128)(2,1)}, u32[]{:S(2)}, u32[]{:S(2)}) collective-permute-start(bf16[394,1024]{1,0:T(8,128)(2,1)} %get-tuple-element.520.refs_0_), channel_id=1, source_target_pairs={{0,1},{1,0},{2,3},{3,2},{4,5},{5,4},{6,7},{7,6},{8,9},{9,8},{10,11... | collective-permute-start | bytes 2420744 | tf_op jit(solution)/shard_map/ppermute | solution.py:67
  136.7 5.9 %collective-permute-start.21 = (bf16[394,1024]{1,0:T(8,128)(2,1)}, bf16[394,1024]{1,0:T(8,128)(2,1)S(1)}, u32[]{:S(2)}, u32[]{:S(2)}) collective-permute-start(bf16[394,1024]{1,0:T(8,128)(2,1)} %collective-permute-done.20.refs_0_.refs_2_), channel_id=1, source_target_pairs={{0,4},{4,0},{8,12},{12,8},{16,20},{20,16},{24,28},{28,24},{1,5},{5... | collective-permute-start | bytes 2420744 | tf_op jit(solution)/shard_map/ppermute | solution.py:63
  147.7 2.5 collective-permute-start.22
  150.5 20.6 %collective-permute-start.23 = (bf16[394,1024]{1,0:T(8,128)(2,1)S(1)}, bf16[394,1024]{1,0:T(8,128)(2,1)S(1)}, u32[]{:S(2)}, u32[]{:S(2)}) collective-permute-start(bf16[394,1024]{1,0:T(8,128)(2,1)S(1)} %add_convert_fusion.1), channel_id=1, source_target_pairs={{0,1},{1,0},{2,3},{3,2},{4,5},{5,4},{6,7},{7,6},{8,9},{9,8},{10,11... | collective-permute-start | bytes 2420744 | tf_op jit(solution)/shard_map/ppermute | solution.py:67
  152.1 19.0 %collective-permute-start.24 = (bf16[394,1024]{1,0:T(8,128)(2,1)S(1)}, bf16[394,1024]{1,0:T(8,128)(2,1)S(1)}, u32[]{:S(2)}, u32[]{:S(2)}) collective-permute-start(bf16[394,1024]{1,0:T(8,128)(2,1)S(1)} %get-tuple-element.554), channel_id=1, source_target_pairs={{0,4},{4,0},{8,12},{12,8},{16,20},{20,16},{24,28},{28,24},{1,5},{5... | collective-permute-start | bytes 2420744 | tf_op jit(solution)/shard_map/ppermute | solution.py:63
  171.1 6.4 %collective-permute-start.25 = (bf16[394,1024]{1,0:T(8,128)(2,1)S(1)}, bf16[394,1024]{1,0:T(8,128)(2,1)S(1)}, u32[]{:S(2)}, u32[]{:S(2)}) collective-permute-start(bf16[394,1024]{1,0:T(8,128)(2,1)S(1)} %get-tuple-element.556), channel_id=1, source_target_pairs={{0,4},{4,0},{8,12},{12,8},{16,20},{20,16},{24,28},{28,24},{1,5},{5... | collective-permute-start | bytes 2420744 | tf_op jit(solution)/shard_map/ppermute | solution.py:63
  171.2 6.4 %collective-permute-start.26 = (bf16[394,1024]{1,0:T(8,128)(2,1)S(1)}, bf16[394,1024]{1,0:T(8,128)(2,1)S(1)}, u32[]{:S(2)}, u32[]{:S(2)}) collective-permute-start(bf16[394,1024]{1,0:T(8,128)(2,1)S(1)} %get-tuple-element.557), channel_id=1, source_target_pairs={{0,4},{4,0},{8,12},{12,8},{16,20},{20,16},{24,28},{28,24},{1,5},{5... | collective-permute-start | bytes 2420744 | tf_op jit(solution)/shard_map/ppermute | solution.py:63
  171.6 25.1 %collective-permute-start.27 = (bf16[512,1024]{1,0:T(8,128)(2,1)S(1)}, bf16[512,1024]{1,0:T(8,128)(2,1)S(1)}, u32[]{:S(2)}, u32[]{:S(2)}) collective-permute-start(bf16[512,1024]{1,0:T(8,128)(2,1)S(1)} %get-tuple-element.572), channel_id=1, source_target_pairs={{0,8},{4,12},{8,0},{12,4},{16,24},{20,28},{24,16},{28,20},{1,9},{5... | collective-permute-start | bytes 3145736 | tf_op jit(solution)/shard_map/ppermute | solution.py:63
  173.2 24.8 %collective-permute-start.28 = (bf16[512,1024]{1,0:T(8,128)(2,1)S(1)}, bf16[512,1024]{1,0:T(8,128)(2,1)S(1)}, u32[]{:S(2)}, u32[]{:S(2)}) collective-permute-start(bf16[512,1024]{1,0:T(8,128)(2,1)S(1)} %get-tuple-element.573), channel_id=1, source_target_pairs={{0,16},{4,20},{8,24},{12,28},{16,0},{20,4},{24,8},{28,12},{1,17},{... | collective-permute-start | bytes 3145736 | tf_op jit(solution)/shard_map/ppermute | solution.py:63
  177.6 2.3 collective-permute-start.29
  177.9 35.7 %collective-permute-start.32 = (bf16[394,1024]{1,0:T(8,128)(2,1)S(1)}, bf16[394,1024]{1,0:T(8,128)(2,1)S(1)}, u32[]{:S(2)}, u32[]{:S(2)}) collective-permute-start(bf16[394,1024]{1,0:T(8,128)(2,1)S(1)} %add_convert_fusion), channel_id=1, source_target_pairs={{0,1},{1,0},{2,3},{3,2},{4,5},{5,4},{6,7},{7,6},{8,9},{9,8},{10,11... | collective-permute-start | bytes 2420744 | tf_op jit(solution)/shard_map/ppermute | solution.py:67
  198.4 15.2 %collective-permute-start.30 = (bf16[256,1024]{1,0:T(8,128)(2,1)S(1)}, bf16[256,1024]{1,0:T(8,128)(2,1)S(1)}, u32[]{:S(2)}, u32[]{:S(2)}) collective-permute-start(bf16[256,1024]{1,0:T(8,128)(2,1)S(1)} %add_convert_fusion.10), channel_id=1, source_target_pairs={{0,16},{4,20},{8,24},{12,28},{16,0},{20,4},{24,8},{28,12},{1,17},{... | collective-permute-start | bytes 1572872 | tf_op jit(solution)/shard_map/ppermute | solution.py:63
  199.3 14.3 %collective-permute-start.31 = (bf16[256,1024]{1,0:T(8,128)(2,1)S(1)}, bf16[256,1024]{1,0:T(8,128)(2,1)S(1)}, u32[]{:S(2)}, u32[]{:S(2)}) collective-permute-start(bf16[256,1024]{1,0:T(8,128)(2,1)S(1)} %add_convert_fusion.9), channel_id=1, source_target_pairs={{0,8},{4,12},{8,0},{12,4},{16,24},{20,28},{24,16},{28,20},{1,9},{5... | collective-permute-start | bytes 1572872 | tf_op jit(solution)/shard_map/ppermute | solution.py:63
  216.0 39.1 %collective-permute-start.34 = (bf16[512,1024]{1,0:T(8,128)(2,1)}, bf16[512,1024]{1,0:T(8,128)(2,1)}, u32[]{:S(2)}, u32[]{:S(2)}) collective-permute-start(bf16[512,1024]{1,0:T(8,128)(2,1)} %get-tuple-element.665), channel_id=1, source_target_pairs={{0,8},{4,12},{8,0},{12,4},{16,24},{20,28},{24,16},{28,20},{1,9},{5... | collective-permute-start | bytes 3145736 | tf_op jit(solution)/shard_map/ppermute | solution.py:63
  216.8 38.3 %collective-permute-start.35 = (bf16[512,1024]{1,0:T(8,128)(2,1)}, bf16[512,1024]{1,0:T(8,128)(2,1)}, u32[]{:S(2)}, u32[]{:S(2)}) collective-permute-start(bf16[512,1024]{1,0:T(8,128)(2,1)} %get-tuple-element.666), channel_id=1, source_target_pairs={{0,16},{4,20},{8,24},{12,28},{16,0},{20,4},{24,8},{28,12},{1,17},{... | collective-permute-start | bytes 3145736 | tf_op jit(solution)/shard_map/ppermute | solution.py:63
  228.3 9.0 %collective-permute-start.33 = (bf16[394,1024]{1,0:T(8,128)(2,1)}, bf16[394,1024]{1,0:T(8,128)(2,1)}, u32[]{:S(2)}, u32[]{:S(2)}) collective-permute-start(bf16[394,1024]{1,0:T(8,128)(2,1)} %get-tuple-element.647), channel_id=1, source_target_pairs={{0,4},{4,0},{8,12},{12,8},{16,20},{20,16},{24,28},{28,24},{1,5},{5... | collective-permute-start | bytes 2420744 | tf_op jit(solution)/shard_map/ppermute | solution.py:63
  228.3 26.8 %collective-permute-start.36 = (bf16[256,1024]{1,0:T(8,128)(2,1)}, bf16[256,1024]{1,0:T(8,128)(2,1)}, u32[]{:S(2)}, u32[]{:S(2)}) collective-permute-start(bf16[256,1024]{1,0:T(8,128)(2,1)} %add_convert_fusion.7), channel_id=1, source_target_pairs={{0,2},{1,3},{2,0},{3,1},{4,6},{5,7},{6,4},{7,5},{8,10},{9,11},{10,... | collective-permute-start | bytes 1572872 | tf_op jit(solution)/shard_map/ppermute | solution.py:67
  260.6 15.6 %collective-permute-start.37 = (bf16[256,1024]{1,0:T(8,128)(2,1)}, bf16[256,1024]{1,0:T(8,128)(2,1)S(1)}, u32[]{:S(2)}, u32[]{:S(2)}) collective-permute-start(bf16[256,1024]{1,0:T(8,128)(2,1)} %add_convert_fusion.6), channel_id=1, source_target_pairs={{0,16},{4,20},{8,24},{12,28},{16,0},{20,4},{24,8},{28,12},{1,17},{... | collective-permute-start | bytes 1572872 | tf_op jit(solution)/shard_map/ppermute | solution.py:63
  261.5 14.7 %collective-permute-start.38 = (bf16[256,1024]{1,0:T(8,128)(2,1)}, bf16[256,1024]{1,0:T(8,128)(2,1)}, u32[]{:S(2)}, u32[]{:S(2)}) collective-permute-start(bf16[256,1024]{1,0:T(8,128)(2,1)} %add_convert_fusion.5), channel_id=1, source_target_pairs={{0,8},{4,12},{8,0},{12,4},{16,24},{20,28},{24,16},{28,20},{1,9},{5... | collective-permute-start | bytes 1572872 | tf_op jit(solution)/shard_map/ppermute | solution.py:63
  262.9 13.3 %collective-permute-start.39 = (f32[112,128]{1,0:T(8,128)S(1)}, f32[112,128]{1,0:T(8,128)S(1)}, u32[]{:S(2)}, u32[]{:S(2)}) collective-permute-start(f32[112,128]{1,0:T(8,128)S(1)} %constant_dynamic-update-slice_fusion), channel_id=1, source_target_pairs={{0,8},{4,12},{8,0},{12,4},{16,24},{20,28},{24,16},{28,20},{1,9},{5... | collective-permute-start | bytes 172040 | tf_op jit(solution)/shard_map/ppermute | solution.py:63
  280.0 13.8 %collective-permute-start.40 = (bf16[2,256,512]{2,1,0:T(8,128)(2,1)S(1)}, bf16[2,256,512]{2,1,0:T(8,128)(2,1)S(1)}, u32[]{:S(2)}, u32[]{:S(2)}) collective-permute-start(bf16[2,256,512]{2,1,0:T(8,128)(2,1)S(1)} %pad_maximum_fusion.3), channel_id=1, source_target_pairs={{0,1},{1,0},{2,3},{3,2},{4,5},{5,4},{6,7},{7,6},{8,9},{9,8},{10,11... | collective-permute-start | bytes 1572872 | tf_op jit(solution)/shard_map/ppermute | solution.py:67
  280.1 13.8 %collective-permute-start.42 = (bf16[256,1024]{1,0:T(8,128)(2,1)S(1)}, bf16[256,1024]{1,0:T(8,128)(2,1)S(1)}, u32[]{:S(2)}, u32[]{:S(2)}) collective-permute-start(bf16[256,1024]{1,0:T(8,128)(2,1)S(1)} %add_convert_fusion.4), channel_id=1, source_target_pairs={{0,16},{4,20},{8,24},{12,28},{16,0},{20,4},{24,8},{28,12},{1,17},{... | collective-permute-start | bytes 1572872 | tf_op jit(solution)/shard_map/ppermute | solution.py:63
  281.4 12.5 %collective-permute-start.41 = (bf16[256,1024]{1,0:T(8,128)(2,1)S(1)}, bf16[256,1024]{1,0:T(8,128)(2,1)S(1)}, u32[]{:S(2)}, u32[]{:S(2)}) collective-permute-start(bf16[256,1024]{1,0:T(8,128)(2,1)S(1)} %add_convert_fusion.4), channel_id=1, source_target_pairs={{0,8},{4,12},{8,0},{12,4},{16,24},{20,28},{24,16},{28,20},{1,9},{5... | collective-permute-start | bytes 1572872 | tf_op jit(solution)/shard_map/ppermute | solution.py:63
  281.9 11.9 %collective-permute-start.43 = (f32[112,128]{1,0:T(8,128)S(1)}, f32[112,128]{1,0:T(8,128)S(1)}, u32[]{:S(2)}, u32[]{:S(2)}) collective-permute-start(f32[112,128]{1,0:T(8,128)S(1)} %add.138), channel_id=1, source_target_pairs={{0,16},{4,20},{8,24},{12,28},{16,0},{20,4},{24,8},{28,12},{1,17},{... | collective-permute-start | bytes 172040 | tf_op jit(solution)/shard_map/ppermute | solution.py:63
  294.1 13.8 %collective-permute-start.45 = (bf16[256,1024]{1,0:T(8,128)(2,1)S(1)}, bf16[256,1024]{1,0:T(8,128)(2,1)S(1)}, u32[]{:S(2)}, u32[]{:S(2)}) collective-permute-start(bf16[256,1024]{1,0:T(8,128)(2,1)S(1)} %add_convert_fusion.4), channel_id=1, source_target_pairs={{0,24},{4,28},{8,16},{12,20},{16,8},{20,12},{24,0},{28,4},{1,25},{... | collective-permute-start | bytes 1572872 | tf_op jit(solution)/shard_map/ppermute | solution.py:63
  295.3 12.6 %collective-permute-start.44 = (bf16[256,512]{1,0:T(8,128)(2,1)S(1)}, bf16[256,512]{1,0:T(8,128)(2,1)S(1)}, u32[]{:S(2)}, u32[]{:S(2)}) collective-permute-start(bf16[256,512]{1,0:T(8,128)(2,1)S(1)} %get-tuple-element.711), channel_id=1, source_target_pairs={{0,2},{1,3},{2,0},{3,1},{4,6},{5,7},{6,4},{7,5},{8,10},{9,11},{10,... | collective-permute-start | bytes 786440 | tf_op jit(solution)/shard_map/ppermute | solution.py:67
  298.4 4.6 %collective-permute-start.46 = (f32[112,128]{1,0:T(8,128)S(1)}, f32[112,128]{1,0:T(8,128)S(1)}, u32[]{:S(2)}, u32[]{:S(2)}) collective-permute-start(f32[112,128]{1,0:T(8,128)S(1)} %add.143), channel_id=1, source_target_pairs={{0,1},{1,0},{2,3},{3,2},{4,5},{5,4},{6,7},{7,6},{8,9},{9,8},{10,11... | collective-permute-start | bytes 172040 | tf_op jit(solution)/shard_map/ppermute | solution.py:67
  308.3 5.4 %collective-permute-start.51 = (bf16[4,256,1024]{2,1,0:T(8,128)(2,1)S(1)}, bf16[4,256,1024]{2,1,0:T(8,128)(2,1)S(1)}, u32[]{:S(2)}, u32[]{:S(2)}) collective-permute-start(bf16[4,256,1024]{2,1,0:T(8,128)(2,1)S(1)} %pad_maximum_fusion.mine_ref), channel_id=1, source_target_pairs={{0,4},{4,0},{8,12},{12,8},{16,20},{20,16},{24,28},{28,24},{1,5},{5... | collective-permute-start | bytes 6291464 | tf_op jit(solution)/shard_map/ppermute | solution.py:63
  308.3 10.1 %collective-permute-start.49 = (bf16[256,512]{1,0:T(8,128)(2,1)S(1)}, bf16[256,512]{1,0:T(8,128)(2,1)S(1)}, u32[]{:S(2)}, u32[]{:S(2)}) collective-permute-start(bf16[256,512]{1,0:T(8,128)(2,1)S(1)} %add_convert_fusion.11), channel_id=1, source_target_pairs={{0,24},{4,28},{8,16},{12,20},{16,8},{20,12},{24,0},{28,4},{1,25},{... | collective-permute-start | bytes 786440 | tf_op jit(solution)/shard_map/ppermute | solution.py:63
  310.2 13.4 %collective-permute-start.48 = (bf16[256,512]{1,0:T(8,128)(2,1)S(1)}, bf16[256,512]{1,0:T(8,128)(2,1)S(1)}, u32[]{:S(2)}, u32[]{:S(2)}) collective-permute-start(bf16[256,512]{1,0:T(8,128)(2,1)S(1)} %add_convert_fusion.11), channel_id=1, source_target_pairs={{0,16},{4,20},{8,24},{12,28},{16,0},{20,4},{24,8},{28,12},{1,17},{... | collective-permute-start | bytes 786440 | tf_op jit(solution)/shard_map/ppermute | solution.py:63
  311.4 12.3 %collective-permute-start.47 = (bf16[256,512]{1,0:T(8,128)(2,1)S(1)}, bf16[256,512]{1,0:T(8,128)(2,1)S(1)}, u32[]{:S(2)}, u32[]{:S(2)}) collective-permute-start(bf16[256,512]{1,0:T(8,128)(2,1)S(1)} %add_convert_fusion.11), channel_id=1, source_target_pairs={{0,8},{4,12},{8,0},{12,4},{16,24},{20,28},{24,16},{28,20},{1,9},{5... | collective-permute-start | bytes 786440 | tf_op jit(solution)/shard_map/ppermute | solution.py:63
  311.9 6.1 %collective-permute-start.50 = (f32[112,128]{1,0:T(8,128)S(1)}, f32[112,128]{1,0:T(8,128)S(1)}, u32[]{:S(2)}, u32[]{:S(2)}) collective-permute-start(f32[112,128]{1,0:T(8,128)S(1)} %add.147), channel_id=1, source_target_pairs={{0,2},{1,3},{2,0},{3,1},{4,6},{5,7},{6,4},{7,5},{8,10},{9,11},{10,... | collective-permute-start | bytes 172040 | tf_op jit(solution)/shard_map/ppermute | solution.py:67
  323.8 2.7 collective-permute-start.53
  323.9 5.6 %collective-permute-start.52 = (f32[112,128]{1,0:T(8,128)S(1)}, f32[112,128]{1,0:T(8,128)S(1)}, u32[]{:S(2)}, u32[]{:S(2)}) collective-permute-start(f32[112,128]{1,0:T(8,128)S(1)} %add.148), channel_id=1, source_target_pairs={{0,4},{4,0},{8,12},{12,8},{16,20},{20,16},{24,28},{28,24},{1,5},{5... | collective-permute-start | bytes 172040 | tf_op jit(solution)/shard_map/ppermute | solution.py:63
  (100 other events, 616.7 us)
